TPU v7x, 32 devices: a whole 2x2x4 slice. The times are simulated.
32 devices in a mesh: dp: 2 (over x), wide: 4 (over z), narrow: 4 (over y, core).
Axes of the slice: x: 2, y: 2, z: 4, core: 2. Of those that a mesh axis runs over, the one named last changes fastest.
Arguments:
- hidden_in: bfloat16 [2, 8, 1024, 768], P(None, ('dp', 'wide'), 'narrow'), may hold values from -6 to 6
- encoder_out: bfloat16 [2, 8, 512, 768], P(None, ('dp', 'wide'), 'narrow'), may hold values from -6 to 6
- cotangent: bfloat16 [2, 8, 1024, 768], P(None, ('dp', 'wide'), 'narrow'), may hold values from -6 to 6
- piece_starts: int32 [2, 8], P(None, ('dp', 'wide')), may hold values from 0 to 768
- valid_lengths: int32 [2, 8], P(None, ('dp', 'wide')), may hold values from 512 to 1024
- bucket_table: int32 [2047], replicated, may hold values from 0 to 31
- gain_self: float32 [768], replicated, may hold values from 0.5 to 1.5
- gain_cross: float32 [768], replicated, may hold values from 0.5 to 1.5
- gain_feed: float32 [768], replicated, may hold values from 0.5 to 1.5
- relative_bias: float32 [32, 12], P(None, 'narrow'), may hold values from -4 to 4
- self_query: bfloat16 [768, 768], P('wide', 'narrow'), may hold values from -0.0546875 to 0.0546875
- self_key: bfloat16 [768, 768], P('wide', 'narrow'), may hold values from -0.21875 to 0.21875
- self_value: bfloat16 [768, 768], P('wide', 'narrow'), may hold values from -0.21875 to 0.21875
- self_output: bfloat16 [768, 768], P('wide', 'narrow'), may hold values from -0.875 to 0.875
- cross_query: bfloat16 [768, 768], P('wide', 'narrow'), may hold values from -0.0546875 to 0.0546875
- cross_key: bfloat16 [768, 768], P('wide', 'narrow'), may hold values from -0.21875 to 0.21875
- cross_value: bfloat16 [768, 768], P('wide', 'narrow'), may hold values from -0.21875 to 0.21875
- cross_output: bfloat16 [768, 768], P('wide', 'narrow'), may hold values from -0.875 to 0.875
- gate_weight: bfloat16 [768, 2048], P('wide', 'narrow'), may hold values from -0.21875 to 0.21875
- up_weight: bfloat16 [768, 2048], P('wide', 'narrow'), may hold values from -0.21875 to 0.21875
- down_weight: bfloat16 [768, 2048], P('wide', 'narrow'), may hold values from -0.125 to 0.125
Outputs:
- output: bfloat16 [2, 8, 1024, 768], P(None, ('dp', 'wide'), 'narrow')
- grad_input: float32 [2, 8, 1024, 768], P(None, ('dp', 'wide'), 'narrow')
- grad_encoder: float32 [2, 8, 512, 768], P(None, ('dp', 'wide'), 'narrow')
- grad_gain_self: float32 [768], replicated
- grad_gain_cross: float32 [768], replicated
- grad_gain_feed: float32 [768], replicated
- grad_relative_bias: float32 [32, 12], P(None, 'narrow')
- grad_self_query: float32 [768, 768], P('wide', 'narrow')
- grad_self_key: float32 [768, 768], P('wide', 'narrow')
- grad_self_value: float32 [768, 768], P('wide', 'narrow')
- grad_self_output: float32 [768, 768], P('wide', 'narrow')
- grad_cross_query: float32 [768, 768], P('wide', 'narrow')
- grad_cross_key: float32 [768, 768], P('wide', 'narrow')
- grad_cross_value: float32 [768, 768], P('wide', 'narrow')
- grad_cross_output: float32 [768, 768], P('wide', 'narrow')
- grad_gate_weight: float32 [768, 2048], P('wide', 'narrow')
- grad_up_weight: float32 [768, 2048], P('wide', 'narrow')
- grad_down_weight: float32 [768, 2048], P('wide', 'narrow')
Inputs may be any that keep to these rules, and one draw needn't show every extreme that they name: `piece_starts`: each sequence's picture piece of 256 tokens lies inside the sequence. `valid_lengths`: keys at or past a sequence's valid length are padding. `bucket_table`: entry j - i + 1023 is the bucket of offset j - i.
All inputs are finite; a program needn't handle non-finite values.
Results may differ from a plain program's by a relative error of at most 0.025.
Values may be sent and summed in bfloat16 or wider, within the bound.
A program may use at most 256 MiB of HBM per device.

v0:
```python
from functools import partial

import jax
import jax.numpy as jnp
from jax import lax
from jax.sharding import PartitionSpec as P

D = 768
DHEAD = 64
BUCKETS = 32
LEN = 1024
ENC = 512
PIC = 256


precise = lax.Precision.HIGHEST
epsilon = 1e-06
masked_value = -1e30


def shortened(array):

    def short(part):
        return part.astype(jnp.bfloat16) if part.dtype == jnp.float32 else part

    return jax.tree.map(short, array)


def matmul(left_arg, right_arg):
    return jnp.dot(left_arg, right_arg, preferred_element_type=jnp.float32)


def against(left_arg, right_arg):
    return lax.dot_general(
        left_arg, right_arg, (((1,), (1,)), ((), ())), preferred_element_type=jnp.float32
    )


def over_rows(left_arg, right_arg):
    return lax.dot_general(
        left_arg, right_arg, (((0,), (0,)), ((), ())), preferred_element_type=jnp.float32
    )


def gather_weights(matrices):
    return jax.tree.map(
        lambda part, own: part.astype(own.dtype),
        lax.all_gather(shortened(matrices), "wide", axis=0, tiled=True),
        matrices,
    )


def reduce_grads(local_grads):
    shards = jax.tree.map(
        lambda part: part.astype(jnp.float32),
        lax.psum_scatter(shortened(local_grads), "wide", scatter_dimension=0, tiled=True),
    )
    return jax.tree.map(lambda part: part.astype(jnp.float32), lax.psum(shortened(shards), "dp"))


def norm_forward(hidden, gain):
    factor = lax.rsqrt(jnp.mean(hidden * hidden, axis=1) + epsilon)
    normed = (hidden * factor[:, None] * gain).astype(jnp.bfloat16)
    return (normed, factor)


def norm_backward(hidden, factor, gain, upstream):
    weighted = upstream * gain
    inner = jnp.sum(weighted * hidden, axis=1)
    cubed = factor * factor * factor
    grad_hidden = weighted * factor[:, None] - hidden * (cubed * inner / D)[:, None]
    grad_gain = jnp.sum(upstream * hidden * factor[:, None], axis=0)
    return (grad_hidden, grad_gain)


def features_in(normed):
    return lax.all_gather(normed, "narrow", axis=1, tiled=True)


def partial_out(terms):
    return lax.psum_scatter(terms, "narrow", scatter_dimension=1, tiled=True)


def grad_in(grad_rows):
    return lax.all_gather(grad_rows, "narrow", axis=1, tiled=True)


def grad_partial(terms):
    return lax.psum_scatter(terms, "narrow", scatter_dimension=1, tiled=True)


def visible(seq_start, length, row_start, row_count, key_count):
    query_pos = row_start + jnp.arange(row_count)[:, None]
    key_pos = jnp.arange(key_count)[None, :]
    query_piece = (query_pos >= seq_start) & (query_pos < seq_start + PIC)
    key_piece = (key_pos >= seq_start) & (key_pos < seq_start + PIC)
    return ((key_pos <= query_pos) | query_piece & key_piece) & (key_pos < length)


def bias_block(offsets, row_count, key_count):
    span_width = key_count + row_count - 1
    head_count = offsets.shape[0]
    tiled_rows = jnp.broadcast_to(offsets[:, None, :], (head_count, row_count, span_width))
    tiled_rows = tiled_rows.reshape(head_count, row_count * span_width)
    tiled_rows = jnp.pad(tiled_rows, ((0, 0), (0, row_count)))
    bias_rows = tiled_rows.reshape(head_count, row_count, key_count + row_count)[:, :, :key_count]
    return bias_rows[:, ::-1, :]


def bias_grad_block(grad_scores, row_count, key_count):
    head_count = grad_scores.shape[0]
    span_width = key_count + row_count - 1
    flipped = grad_scores[:, ::-1, :]
    padded = jnp.pad(flipped, ((0, 0), (0, 0), (0, row_count))).reshape(
        head_count, row_count * (key_count + row_count)
    )
    skewed = padded[:, : row_count * span_width].reshape(head_count, row_count, span_width)
    return jnp.sum(skewed, axis=1)


def block_scores(query_rows, keys_in, bias_full, seq_start, length, row_start, causal):
    scores = jnp.einsum("qhd,khd->hqk", query_rows, keys_in, preferred_element_type=jnp.float32)
    if causal:
        key_count = keys_in.shape[0]
        row_count = query_rows.shape[0]
        scores = scores + bias_full[:, row_start : row_start + row_count, :]
        allowed = visible(seq_start, length, row_start, row_count, key_count)
        scores = jnp.where(allowed[None], scores, masked_value)
    return scores


def attend_forward(queries, keys_in, values_in, bias_full, seq_start, length, causal):
    row_total = queries.shape[0]
    step_rows = min(512, row_total)
    outputs = []
    sums_log = []
    for row_start in range(0, row_total, step_rows):
        query_rows = queries[row_start : row_start + step_rows]
        scores = block_scores(query_rows, keys_in, bias_full, seq_start, length, row_start, causal)
        largest = jnp.max(scores, axis=-1, keepdims=True)
        shifted = jnp.exp(scores - largest)
        summed = jnp.sum(shifted, axis=-1, keepdims=True)
        probability = shifted / summed
        attended = jnp.einsum(
            "hqk,khd->qhd",
            probability.astype(jnp.bfloat16),
            values_in,
            preferred_element_type=jnp.float32,
        )
        outputs.append(attended.astype(jnp.bfloat16))
        sums_log.append((largest + jnp.log(summed))[..., 0])
    return (jnp.concatenate(outputs, axis=0), jnp.concatenate(sums_log, axis=1))


def attend_backward(
    queries, keys_in, values_in, log_sums, grad_out, bias_full, seq_start, length, causal
):
    row_total = queries.shape[0]
    step_rows = min(512, row_total)
    grad_keys = jnp.zeros(keys_in.shape, jnp.float32)
    grad_values = jnp.zeros(values_in.shape, jnp.float32)
    grad_queries = []
    pair_blocks = []
    for row_start in range(0, row_total, step_rows):
        query_rows = queries[row_start : row_start + step_rows]
        upstream = grad_out[row_start : row_start + step_rows]
        scores = block_scores(query_rows, keys_in, bias_full, seq_start, length, row_start, causal)
        probability = jnp.exp(scores - log_sums[:, row_start : row_start + step_rows, None])
        grad_probs = jnp.einsum(
            "qhd,khd->hqk", upstream, values_in, preferred_element_type=jnp.float32
        )
        grad_values = grad_values + jnp.einsum(
            "hqk,qhd->khd",
            probability.astype(jnp.bfloat16),
            upstream,
            preferred_element_type=jnp.float32,
        )
        grad_scores = probability * (
            grad_probs - jnp.sum(probability * grad_probs, axis=-1, keepdims=True)
        )
        if causal:
            pair_blocks.append(grad_scores)
        scores_low = grad_scores.astype(jnp.bfloat16)
        grad_queries.append(
            jnp.einsum("hqk,khd->qhd", scores_low, keys_in, preferred_element_type=jnp.float32)
        )
        grad_keys = grad_keys + jnp.einsum(
            "hqk,qhd->khd", scores_low, query_rows, preferred_element_type=jnp.float32
        )
    pair_grads = jnp.concatenate(pair_blocks, axis=1) if causal else None
    return (
        jnp.concatenate(grad_queries, axis=0).astype(jnp.bfloat16),
        grad_keys.astype(jnp.bfloat16),
        grad_values.astype(jnp.bfloat16),
        pair_grads,
    )


def gated(gate_in, up_in):
    return jax.nn.gelu(gate_in, approximate=True) * up_in


def on_device(
    hidden_in,
    encoder_out,
    cotangent,
    piece_starts,
    valid_lengths,
    bucket_table,
    gain_self,
    gain_cross,
    gain_feed,
    relative_bias,
    self_query,
    self_key,
    self_value,
    self_output,
    cross_query,
    cross_key,
    cross_value,
    cross_output,
    gate_weight,
    up_weight,
    down_weight,
):
    local_mats = (
        self_query,
        self_key,
        self_value,
        self_output,
        cross_query,
        cross_key,
        cross_value,
        cross_output,
        gate_weight,
        up_weight,
        down_weight,
    )
    one_hot = (bucket_table[:, None] == jnp.arange(BUCKETS)[None, :]).astype(jnp.float32)
    self_fwd = jax.vmap(partial(attend_forward, causal=True), in_axes=(0, 0, 0, None, 0, 0))
    cross_fwd = jax.vmap(partial(attend_forward, causal=False), in_axes=(0, 0, 0, None, 0, 0))
    self_back = jax.vmap(partial(attend_backward, causal=True), in_axes=(0, 0, 0, 0, 0, None, 0, 0))
    cross_back = jax.vmap(
        partial(attend_backward, causal=False), in_axes=(0, 0, 0, 0, 0, None, 0, 0)
    )
    gain_self_acc = jnp.zeros((D,), jnp.float32)
    gain_cross_acc = jnp.zeros((D,), jnp.float32)
    gain_feed_acc = jnp.zeros((D,), jnp.float32)
    outputs = []
    grads_input = []
    grads_encoder = []
    micro_count = hidden_in.shape[0]
    head_local = self_query.shape[1] // DHEAD
    offsets = jnp.dot(one_hot, relative_bias, precision=precise).T
    bias_full = bias_block(offsets, LEN, LEN)
    pairs_acc = jnp.zeros((head_local, LEN, LEN), jnp.float32)
    grad_total = tuple((jnp.zeros(matrix.shape, jnp.float32) for matrix in local_mats))
    for micro_step in range(micro_count):
        full_mats = gather_weights(local_mats)
        back_mats = gather_weights(local_mats)
        tokens_in = hidden_in[micro_step]
        memory_in = encoder_out[micro_step]
        seq_starts = piece_starts[micro_step]
        seq_lengths = valid_lengths[micro_step]
        seq_count = tokens_in.shape[0]
        tok_local = tokens_in.shape[1]
        run_head_local = full_mats[0].shape[1] // DHEAD
        row_count = seq_count * LEN
        row_local = seq_count * tok_local
        enc_rows = seq_count * ENC

        def to_heads(matrix, length_of):
            return matrix.astype(jnp.bfloat16).reshape(seq_count, length_of, run_head_local, DHEAD)

        def gather_rows(local_rows):
            return features_in(local_rows.reshape(seq_count, tok_local, D)).reshape(row_count, D)

        def gather_grad(local_rows):
            return grad_in(local_rows.reshape(seq_count, tok_local, D)).reshape(row_count, D)

        def back_to_tokens(terms):
            return partial_out(terms.reshape(seq_count, LEN, D)).reshape(row_local, D)

        def grad_to_tokens(terms):
            return grad_partial(terms.reshape(seq_count, LEN, D)).reshape(row_local, D)

        gathered_enc = features_in(memory_in).reshape(enc_rows, D)
        (
            self_query_full,
            self_key_full,
            self_value_full,
            self_out_full,
            cross_query_full,
            cross_key_full,
            cross_value_full,
            cross_out_full,
            gate_full,
            up_full,
            down_full,
        ) = full_mats
        resid_in = tokens_in.astype(jnp.float32).reshape(row_local, D)
        normed_self, factor_self = norm_forward(resid_in, gain_self)
        gathered_self = gather_rows(normed_self)
        sq_heads = to_heads(matmul(gathered_self, self_query_full), LEN)
        sk_heads = to_heads(matmul(gathered_self, self_key_full), LEN)
        sv_heads = to_heads(matmul(gathered_self, self_value_full), LEN)
        self_attn, self_lse = self_fwd(
            sq_heads, sk_heads, sv_heads, bias_full, seq_starts, seq_lengths
        )
        self_flat = self_attn.reshape(row_count, run_head_local * DHEAD)
        hidden_one = resid_in + back_to_tokens(against(self_flat, self_out_full))
        normed_cross, factor_cross = norm_forward(hidden_one, gain_cross)
        gathered_cross = gather_rows(normed_cross)
        cq_heads = to_heads(matmul(gathered_cross, cross_query_full), LEN)
        ck_heads = to_heads(matmul(gathered_enc, cross_key_full), ENC)
        cv_heads = to_heads(matmul(gathered_enc, cross_value_full), ENC)
        cross_attn, cross_lse = cross_fwd(
            cq_heads, ck_heads, cv_heads, bias_full, seq_starts, seq_lengths
        )
        cross_flat = cross_attn.reshape(row_count, run_head_local * DHEAD)
        hidden_two = hidden_one + back_to_tokens(against(cross_flat, cross_out_full))
        (
            self_query_back,
            self_key_back,
            self_value_back,
            self_out_back,
            cross_query_back,
            cross_key_back,
            cross_value_back,
            cross_out_back,
            gate_back,
            up_back,
            down_back,
        ) = back_mats
        cot_rows = cotangent[micro_step].reshape(row_local, D)
        normed_feed, factor_feed = norm_forward(hidden_two, gain_feed)
        feed_rows = gather_rows(normed_feed)
        gate_pre = matmul(feed_rows, gate_full)
        up_pre = matmul(feed_rows, up_full)
        activated = gated(gate_pre, up_pre).astype(jnp.bfloat16)
        feed_terms = against(activated, down_full)
        result = hidden_two + back_to_tokens(feed_terms)
        grad_out_feed = gather_grad(cot_rows)
        result_rows = result.astype(jnp.bfloat16).reshape(seq_count, tok_local, D)
        grad_activated = matmul(grad_out_feed, down_back)
        _, pull_back = jax.vjp(gated, gate_pre, up_pre)
        grad_gate, grad_up = pull_back(grad_activated)
        grad_gate = grad_gate.astype(jnp.bfloat16)
        grad_up = grad_up.astype(jnp.bfloat16)
        new_down = over_rows(grad_out_feed, activated)
        new_gate = over_rows(feed_rows, grad_gate)
        new_up = over_rows(feed_rows, grad_up)
        feed_back = against(grad_gate, gate_back) + against(grad_up, up_back)
        grad_normed_feed = grad_to_tokens(feed_back)
        back_feed, gain_feed_part = norm_backward(
            hidden_two, factor_feed, gain_feed, grad_normed_feed
        )
        grad_two = cot_rows.astype(jnp.float32) + back_feed
        grad_out_cross = gather_grad(grad_two.astype(jnp.bfloat16))
        new_cross_out = over_rows(grad_out_cross, cross_flat)
        grad_cross = to_heads(matmul(grad_out_cross, cross_out_back), LEN)
        cq_grad, ck_grad, cv_grad, _ = cross_back(
            cq_heads, ck_heads, cv_heads, cross_lse, grad_cross, bias_full, seq_starts, seq_lengths
        )
        cq_flat = cq_grad.reshape(row_count, run_head_local * DHEAD)
        ck_flat = ck_grad.reshape(enc_rows, run_head_local * DHEAD)
        cv_flat = cv_grad.reshape(enc_rows, run_head_local * DHEAD)
        new_cross_query = over_rows(gathered_cross, cq_flat)
        new_cross_key = over_rows(gathered_enc, ck_flat)
        new_cross_value = over_rows(gathered_enc, cv_flat)
        grad_normed_cross = grad_to_tokens(against(cq_flat, cross_query_back))
        memory_terms = against(ck_flat, cross_key_back) + against(cv_flat, cross_value_back)
        grad_memory = grad_partial(memory_terms.reshape(seq_count, ENC, D))
        back_cross, gain_cross_part = norm_backward(
            hidden_one, factor_cross, gain_cross, grad_normed_cross
        )
        grad_one = grad_two + back_cross
        grad_out_self = gather_grad(grad_one.astype(jnp.bfloat16))
        new_self_out = over_rows(grad_out_self, self_flat)
        grad_self = to_heads(matmul(grad_out_self, self_out_back), LEN)
        sq_grad, sk_grad, sv_grad, pair_grads = self_back(
            sq_heads, sk_heads, sv_heads, self_lse, grad_self, bias_full, seq_starts, seq_lengths
        )
        sq_flat = sq_grad.reshape(row_count, run_head_local * DHEAD)
        sk_flat = sk_grad.reshape(row_count, run_head_local * DHEAD)
        sv_flat = sv_grad.reshape(row_count, run_head_local * DHEAD)
        new_self_query = over_rows(gathered_self, sq_flat)
        new_self_key = over_rows(gathered_self, sk_flat)
        new_self_value = over_rows(gathered_self, sv_flat)
        grad_normed_self = grad_to_tokens(
            against(sq_flat, self_query_back)
            + against(sk_flat, self_key_back)
            + against(sv_flat, self_value_back)
        )
        back_self, gain_self_part = norm_backward(
            resid_in, factor_self, gain_self, grad_normed_self
        )
        grad_tokens = (grad_one + back_self).reshape(seq_count, tok_local, D)
        local_grads = (
            new_self_query,
            new_self_key,
            new_self_value,
            new_self_out,
            new_cross_query,
            new_cross_key,
            new_cross_value,
            new_cross_out,
            new_gate,
            new_up,
            new_down,
        )
        result_rows, grad_tokens, grad_memory, gain_parts, pairs_part, local_grads = (
            result_rows,
            grad_tokens,
            grad_memory,
            (gain_self_part, gain_cross_part, gain_feed_part),
            jnp.sum(pair_grads, axis=0),
            local_grads,
        )
        outputs.append(result_rows)
        grads_input.append(grad_tokens)
        grads_encoder.append(grad_memory)
        gain_self_acc = gain_self_acc + gain_parts[0]
        gain_cross_acc = gain_cross_acc + gain_parts[1]
        gain_feed_acc = gain_feed_acc + gain_parts[2]
        pairs_acc = pairs_acc + pairs_part
        grad_total = tuple(
            (running + fresh for running, fresh in zip(grad_total, reduce_grads(local_grads)))
        )
    offsets_acc = bias_grad_block(pairs_acc, LEN, LEN)
    table_grad = jnp.dot(one_hot.T, offsets_acc.T, precision=precise)
    output_all = jnp.stack(outputs)
    grad_input_all = jnp.stack(grads_input)
    grad_encoder_all = jnp.stack(grads_encoder)
    table_sum = lax.psum(table_grad, ("dp", "wide"))
    gain_sums = lax.psum((gain_self_acc, gain_cross_acc, gain_feed_acc), ("dp", "wide", "narrow"))
    return (
        output_all,
        grad_input_all,
        grad_encoder_all,
        gain_sums[0],
        gain_sums[1],
        gain_sums[2],
        table_sum,
        grad_total[0],
        grad_total[1],
        grad_total[2],
        grad_total[3],
        grad_total[4],
        grad_total[5],
        grad_total[6],
        grad_total[7],
        grad_total[8],
        grad_total[9],
        grad_total[10],
    )


def solution(mesh):
    return jax.shard_map(
        on_device,
        mesh=mesh,
        in_specs=(
            P(None, ("dp", "wide"), "narrow", None),
            P(None, ("dp", "wide"), "narrow", None),
            P(None, ("dp", "wide"), "narrow", None),
            P(None, ("dp", "wide")),
            P(None, ("dp", "wide")),
            P(),
            P(),
            P(),
            P(),
            P(None, "narrow"),
            P("wide", "narrow"),
            P("wide", "narrow"),
            P("wide", "narrow"),
            P("wide", "narrow"),
            P("wide", "narrow"),
            P("wide", "narrow"),
            P("wide", "narrow"),
            P("wide", "narrow"),
            P("wide", "narrow"),
            P("wide", "narrow"),
            P("wide", "narrow"),
        ),
        out_specs=(
            P(None, ("dp", "wide"), "narrow", None),
            P(None, ("dp", "wide"), "narrow", None),
            P(None, ("dp", "wide"), "narrow", None),
            P(),
            P(),
            P(),
            P(None, "narrow"),
            P("wide", "narrow"),
            P("wide", "narrow"),
            P("wide", "narrow"),
            P("wide", "narrow"),
            P("wide", "narrow"),
            P("wide", "narrow"),
            P("wide", "narrow"),
            P("wide", "narrow"),
            P("wide", "narrow"),
            P("wide", "narrow"),
            P("wide", "narrow"),
        ),
        check_vma=False,
    )
```

profile of v0, /device:TPU:0, one launch (start us, length us, event | category | flops | bytes accessed | tf_op | source)
XLA Modules:
  0.0 2793.7 jit_solution(8759003723626149916)
XLA Ops:
  27.7 34.9 %reshape.2303 = f32[6288384]{0:T(1024)} reshape(f32[3,1024,2047]{2,1,0:T(8,128)} %broadcast_in_dim.49) | data formatting | bytes 50307072
  62.7 491.0 %while.2 = (u32[]{:T(128)}, f32[6288384]{0:T(1024)}, f32[1,3,2096128]{2,1,0:T(4,128)}, u32[]{}, u32[]{}, /*index=5*/u32[]{}, u32[]{}, u32[]{}) while((u32[]{:T(128)}, f32[6288384]{0:T(1024)}, f32[1,3,2096128]{2,1,0:T(4,128)}, u32[]{}, u32[]{}, /*index=5*/u32[]{}, u32[]{}, u32[]{}) %tuple.93), condition=%wide.cond, body=%wide.body.sunk | while | flops 9 | bytes 50307248
  75.4 150.7 %dynamic-update-slice.4 = f32[1,3,2096128]{2,1,0:T(4,128)} dynamic-update-slice(f32[1,3,2096128]{2,1,0:T(4,128)} %get-tuple-element.259, f32[1,1,2096128]{2,1,0:T(1,128)} %reshape.2308, u32[]{:T(128)S(6)} %multiply.98, u32[]{:T(128)S(6)} %multiply.100, u32[]{} %constant.418..sunk) | dynamic-update-slice | bytes 16769028
  238.8 151.1 %dynamic-update-slice.4 = f32[1,3,2096128]{2,1,0:T(4,128)} dynamic-update-slice(f32[1,3,2096128]{2,1,0:T(4,128)} %get-tuple-element.259, f32[1,1,2096128]{2,1,0:T(1,128)} %reshape.2308, u32[]{:T(128)S(6)} %multiply.98, u32[]{:T(128)S(6)} %multiply.100, u32[]{} %constant.418..sunk) | dynamic-update-slice | bytes 16769028
  402.6 151.1 %dynamic-update-slice.4 = f32[1,3,2096128]{2,1,0:T(4,128)} dynamic-update-slice(f32[1,3,2096128]{2,1,0:T(4,128)} %get-tuple-element.259, f32[1,1,2096128]{2,1,0:T(1,128)} %reshape.2308, u32[]{:T(128)S(6)} %multiply.98, u32[]{:T(128)S(6)} %multiply.100, u32[]{} %constant.418..sunk) | dynamic-update-slice | bytes 16769028
  553.7 22.7 pad.8
  576.3 26.3 copy.108
  614.5 48.4 %slice.115 = f32[3,512,1024]{2,1,0:T(8,128)} reverse(f32[3,512,1024]{2,1,0:T(8,128)} %get-tuple-element.127), dimensions={1} | reverse | bytes 12582912 | tf_op jit(solution)/shard_map/vmap()/slice | solution.py:126
  662.9 48.6 %slice.118 = f32[3,512,1024]{2,1,0:T(8,128)} reverse(f32[3,512,1024]{2,1,0:T(8,128)} %get-tuple-element.128), dimensions={1} | reverse | bytes 12582912 | tf_op jit(solution)/shard_map/vmap()/slice | solution.py:126
  803.6 39.6 %reduce-scatter.49.cloned.1.call-done = f32[1,256,768]{2,1,0:T(8,128)} async-done(((f32[1,1024,768]{2,1,0:T(8,128)}), f32[1,256,768]{2,1,0:T(8,128)}) %reduce-scatter.49.cloned.1.call-update) | async-done | bytes 786448 | tf_op jit(solution)/shard_map/reduce_scatter | solution.py:81
  887.6 38.0 %reduce-scatter.55.cloned.1.call-done = f32[1,256,768]{2,1,0:T(8,128)} async-done(((f32[1,1024,768]{2,1,0:T(8,128)}), f32[1,256,768]{2,1,0:T(8,128)}) %reduce-scatter.55.cloned.1.call-update) | async-done | bytes 786448 | tf_op jit(solution)/shard_map/reduce_scatter | solution.py:81
  1035.7 31.5 %reduce-scatter.57.cloned.1.call-done = f32[1,256,768]{2,1,0:T(8,128)} async-done(((f32[1,1024,768]{2,1,0:T(8,128)}), f32[1,256,768]{2,1,0:T(8,128)}) %reduce-scatter.57.cloned.1.call-update) | async-done | bytes 786448 | tf_op jit(solution)/shard_map/reduce_scatter | solution.py:81
  1067.2 40.6 %reduce-scatter.51.cloned.1.call-done = f32[1,256,768]{2,1,0:T(8,128)} async-done(((f32[1,1024,768]{2,1,0:T(8,128)}), f32[1,256,768]{2,1,0:T(8,128)}) %reduce-scatter.51.cloned.1.call-update) | async-done | bytes 786448 | tf_op jit(solution)/shard_map/reduce_scatter | solution.py:81
  1116.2 20.1 all_gather.120
  1207.7 29.3 %reduce-scatter.67.cloned.1.call-done = f32[1,256,768]{2,1,0:T(8,128)} async-done(((f32[1,1024,768]{2,1,0:T(8,128)}), f32[1,256,768]{2,1,0:T(8,128)}) %reduce-scatter.67.cloned.1.call-update) | async-done | bytes 786448 | tf_op jit(solution)/shard_map/reduce_scatter | solution.py:89
  1237.0 40.5 %reduce-scatter.61.cloned.1.call-done = f32[1,256,768]{2,1,0:T(8,128)} async-done(((f32[1,1024,768]{2,1,0:T(8,128)}), f32[1,256,768]{2,1,0:T(8,128)}) %reduce-scatter.61.cloned.1.call-update) | async-done | bytes 786448 | tf_op jit(solution)/shard_map/reduce_scatter | solution.py:89
  1338.0 27.2 reduce-scatter.69.cloned.1.call-done
  1365.2 40.5 %reduce-scatter.63.cloned.1.call-done = f32[1,256,768]{2,1,0:T(8,128)} async-done(((f32[1,1024,768]{2,1,0:T(8,128)}), f32[1,256,768]{2,1,0:T(8,128)}) %reduce-scatter.63.cloned.1.call-update) | async-done | bytes 786448 | tf_op jit(solution)/shard_map/reduce_scatter | solution.py:89
  1590.6 22.7 reduce-scatter.103.cloned.1.call-done
  1613.3 24.9 reduce-scatter.107.cloned.1.call-done
  1638.1 24.9 reduce-scatter.101.cloned.1.call-done
  1663.0 24.7 reduce-scatter.105.cloned.1.call-done
  1687.7 22.2 reduce-scatter.93.cloned.1.call-done
  1709.9 21.3 reduce-scatter.95.cloned.1.call-done
  1731.2 21.0 reduce-scatter.99.cloned.1.call-done
  1752.2 21.3 reduce-scatter.97.cloned.1.call-done
  1773.5 21.2 reduce-scatter.77.cloned.1.call-done
  1794.7 21.1 reduce-scatter.79.cloned.1.call-done
  1815.8 21.1 reduce-scatter.87.cloned.1.call-done
  1836.8 21.3 reduce-scatter.83.cloned.1.call-done
  1858.1 21.0 reduce-scatter.91.cloned.1.call-done
  1879.1 21.3 reduce-scatter.89.cloned.1.call-done
  1900.4 21.2 reduce-scatter.85.cloned.1.call-done
  1921.6 21.9 reduce-scatter.81.cloned.1.call-done
  1972.3 31.5 %reduce-scatter.75.cloned.1.call-done = f32[1,128,768]{2,1,0:T(8,128)} async-done(((f32[1,512,768]{2,1,0:T(8,128)}), f32[1,128,768]{2,1,0:T(8,128)}) %reduce-scatter.75.cloned.1.call-update) | async-done | bytes 393232 | tf_op jit(solution)/shard_map/reduce_scatter | solution.py:89
  2021.5 96.1 %rev.4 = f32[3,1024,1024]{2,1,0:T(8,128)} reverse(f32[3,1024,1024]{2,1,0:T(8,128)} %fusion), dimensions={1} | reverse | bytes 25165824 | tf_op jit(solution)/shard_map/rev | solution.py:113
  2132.1 33.5 %copy.106 = f32[1,3,1024,2048]{3,1,2,0:T(4,128)} copy(f32[1,3,1024,2048]{3,2,1,0:T(8,128)} %pad_bitcast_fusion) | data formatting | bytes 50331648
  2165.6 23.7 slice_bitcast_fusion.48
  2189.3 467.0 %while.3 = (u32[]{:T(128)}, f32[1,3,2096128]{2,1,0:T(4,128)}, f32[6288384]{0:T(1024)}, u32[]{}, f32[]{:T(128)}, /*index=5*/u32[]{}, u32[]{}, u32[]{}) while((u32[]{:T(128)}, f32[1,3,2096128]{2,1,0:T(4,128)}, f32[6288384]{0:T(1024)}, u32[]{}, f32[]{:T(128)}, /*index=5*/u32[]{}, u32[]{}, u32[]{}) %tuple.96), condition=%wide.cond.1, body=%wide.body.1.sunk | while | flops 9 | bytes 33538240
  2189.8 83.9 %dynamic-slice_reduce_fusion.2 = f32[2096128]{0:T(1024)} fusion(f32[]{:T(128)} %broadcast.1080, f32[1,3,2096128]{2,1,0:T(4,128)} %get-tuple-element.290, u32[]{:T(128)S(6)} %multiply.102, u32[]{:T(128)S(6)} %multiply.103), kind=kLoop, calls=%fused_computation.551.clone.1 | loop fusion | bytes 16769036
  2273.7 71.3 %dynamic-update-slice.5 = f32[6288384]{0:T(1024)} dynamic-update-slice(f32[6288384]{0:T(1024)} %get-tuple-element.283, f32[2096128]{0:T(1024)} %dynamic-slice_reduce_fusion.2, u32[]{:T(128)S(6)} %add.896) | dynamic-update-slice | bytes 16769028
  2345.5 83.9 %dynamic-slice_reduce_fusion.2 = f32[2096128]{0:T(1024)} fusion(f32[]{:T(128)} %broadcast.1080, f32[1,3,2096128]{2,1,0:T(4,128)} %get-tuple-element.290, u32[]{:T(128)S(6)} %multiply.102, u32[]{:T(128)S(6)} %multiply.103), kind=kLoop, calls=%fused_computation.551.clone.1 | loop fusion | bytes 16769036
  2429.4 71.3 %dynamic-update-slice.5 = f32[6288384]{0:T(1024)} dynamic-update-slice(f32[6288384]{0:T(1024)} %get-tuple-element.283, f32[2096128]{0:T(1024)} %dynamic-slice_reduce_fusion.2, u32[]{:T(128)S(6)} %add.896) | dynamic-update-slice | bytes 16769028
  2501.2 83.9 %dynamic-slice_reduce_fusion.2 = f32[2096128]{0:T(1024)} fusion(f32[]{:T(128)} %broadcast.1080, f32[1,3,2096128]{2,1,0:T(4,128)} %get-tuple-element.290, u32[]{:T(128)S(6)} %multiply.102, u32[]{:T(128)S(6)} %multiply.103), kind=kLoop, calls=%fused_computation.551.clone.1 | loop fusion | bytes 16769036
  2585.1 71.3 %dynamic-update-slice.5 = f32[6288384]{0:T(1024)} dynamic-update-slice(f32[6288384]{0:T(1024)} %get-tuple-element.283, f32[2096128]{0:T(1024)} %dynamic-slice_reduce_fusion.2, u32[]{:T(128)S(6)} %add.896) | dynamic-update-slice | bytes 16769028
  2656.3 37.5 %reshape.2276 = f32[3,1024,2047]{2,1,0:T(8,128)} reshape(f32[6288384]{0:T(1024)} %get-tuple-element.63) | data formatting | bytes 50307072 | tf_op jit(solution)/shard_map/reshape | solution.py:117
  2703.6 21.3 psum.185
  2749.4 37.1 %all-reduce.2 = (f32[768]{0:T(1024)}, f32[768]{0:T(1024)}, f32[768]{0:T(1024)}) all-reduce(f32[768]{0:T(1024)S(1)} %copy-done.210, f32[768]{0:T(1024)S(1)} %copy-done.209, f32[768]{0:T(1024)S(1)} %copy-done.208), channel_id=1, replica_groups=mesh['dp'=2,'wide'=4,'narrow'=4] {'dp','wide','narrow'}, use_global_device_ids=true, to_apply=%region_52.53 | all-reduce | flops 2304 | bytes 18432 | tf_op jit(solution)/shard_map/psum | solution.py:436
  (851 shorter events, 734.6 us)
Async XLA Ops:
  7.2 773.5 %all-gather.17.cloned.1.call-start = ((), (), s32[]{:S(2)}) async-start(), calls=%async_computation.36 | async-start | bytes 1966080 | tf_op jit(solution)/shard_map/all_gather | solution.py:77
  11.5 831.7 %reduce-scatter.49.cloned.1.call-start = ((), (), s32[]{:S(2)}) async-start(), calls=%async_computation.37 | async-start | bytes 3932160 | tf_op jit(solution)/shard_map/reduce_scatter | solution.py:81
  803.6 61.9 %all-gather.23.cloned.1.call-start = ((), (), s32[]{:S(2)}) async-start(), calls=%async_computation.42 | async-start | bytes 1966080 | tf_op jit(solution)/shard_map/all_gather | solution.py:77
  845.6 80.0 %reduce-scatter.55.cloned.1.call-start = ((), (), s32[]{:S(2)}) async-start(), calls=%async_computation.43 | async-start | bytes 3932160 | tf_op jit(solution)/shard_map/reduce_scatter | solution.py:81
  887.6 113.8 %all-gather.25.cloned.1.call-start = ((), (), s32[]{:S(2)}) async-start(), calls=%async_computation.44 | async-start | bytes 1966080 | tf_op jit(solution)/shard_map/all_gather | solution.py:77
  929.3 97.6 %all-gather.19.cloned.1.call-start = ((), (), s32[]{:S(2)}) async-start(), calls=%async_computation.38 | async-start | bytes 1966080 | tf_op jit(solution)/shard_map/all_gather | solution.py:77
  1001.0 66.2 %reduce-scatter.57.cloned.1.call-start = ((), (), s32[]{:S(2)}) async-start(), calls=%async_computation.45 | async-start | bytes 3932160 | tf_op jit(solution)/shard_map/reduce_scatter | solution.py:81
  1011.7 96.1 %reduce-scatter.51.cloned.1.call-start = ((), (), s32[]{:S(2)}) async-start(), calls=%async_computation.39 | async-start | bytes 3932160 | tf_op jit(solution)/shard_map/reduce_scatter | solution.py:81
  1035.6 137.3 %all-gather.27.cloned.1.call-start = ((), (), s32[]{:S(2)}) async-start(), calls=%async_computation.46 | async-start | bytes 1966080 | tf_op jit(solution)/shard_map/all_gather | solution.py:77
  1112.6 66.8 %all-gather.39.cloned.1.call-start = ((), (), s32[]{:S(2)}) async-start(), calls=%async_computation.77 | async-start | bytes 1966080 | tf_op jit(solution)/shard_map/all_gather | solution.py:85
  1114.8 75.5 %all-gather.21.cloned.1.call-start = ((), (), s32[]{:S(2)}) async-start(), calls=%async_computation.40 | async-start | bytes 1966080 | tf_op jit(solution)/shard_map/all_gather | solution.py:77
  1115.5 81.2 %all-gather.37.cloned.1.call-start = ((), (), s32[]{:S(2)}) async-start(), calls=%async_computation.76 | async-start | bytes 1966080 | tf_op jit(solution)/shard_map/all_gather | solution.py:85
  1116.1 120.9 %reduce-scatter.67.cloned.1.call-start = ((), (), s32[]{:S(2)}) async-start(), calls=%async_computation.53 | async-start | bytes 3932160 | tf_op jit(solution)/shard_map/reduce_scatter | solution.py:89
  1190.2 87.3 %reduce-scatter.61.cloned.1.call-start = ((), (), s32[]{:S(2)}) async-start(), calls=%async_computation.48 | async-start | bytes 3932160 | tf_op jit(solution)/shard_map/reduce_scatter | solution.py:89
  1207.7 96.1 %all-gather.33.cloned.1.call-start = ((), (), s32[]{:S(2)}) async-start(), calls=%async_computation.54 | async-start | bytes 1966080 | tf_op jit(solution)/shard_map/all_gather | solution.py:85
  1286.1 79.1 %reduce-scatter.69.cloned.1.call-start = ((), (), s32[]{:S(2)}) async-start(), calls=%async_computation.55 | async-start | bytes 3932160 | tf_op jit(solution)/shard_map/reduce_scatter | solution.py:89
  1317.3 88.4 %reduce-scatter.63.cloned.1.call-start = ((), (), s32[]{:S(2)}) async-start(), calls=%async_computation.50 | async-start | bytes 3932160 | tf_op jit(solution)/shard_map/reduce_scatter | solution.py:89
  1338.0 138.5 %all-gather.31.cloned.1.call-start = ((), (), s32[]{:S(2)}) async-start(), calls=%async_computation.51 | async-start | bytes 1966080 | tf_op jit(solution)/shard_map/all_gather | solution.py:85
  1411.8 85.5 %all-gather.35.cloned.1.call-start = ((), (), s32[]{:S(2)}) async-start(), calls=%async_computation.56 | async-start | bytes 1966080 | tf_op jit(solution)/shard_map/all_gather | solution.py:85
  1412.4 160.4 %reduce-scatter.119.cloned.1.call-start = ((), (), s32[]{:S(2)}) async-start(), calls=%async_computation.83 | async-start | bytes 983040
  1416.4 158.2 %reduce-scatter.117.cloned.1.call-start = ((), (), s32[]{:S(2)}) async-start(), calls=%async_computation.82 | async-start | bytes 983040
  1422.9 153.5 %reduce-scatter.113.cloned.1.call-start = ((), (), s32[]{:S(2)}) async-start(), calls=%async_computation.80 | async-start | bytes 491520
  1428.5 149.5 %reduce-scatter.109.cloned.1.call-start = ((), (), s32[]{:S(2)}) async-start(), calls=%async_computation.78 | async-start | bytes 491520
  1436.6 143.1 %reduce-scatter.115.cloned.1.call-start = ((), (), s32[]{:S(2)}) async-start(), calls=%async_computation.81 | async-start | bytes 491520
  1443.3 145.6 %reduce-scatter.111.cloned.1.call-start = ((), (), s32[]{:S(2)}) async-start(), calls=%async_computation.79 | async-start | bytes 491520
  1447.3 166.0 %reduce-scatter.103.cloned.1.call-start = ((), (), s32[]{:S(2)}) async-start(), calls=%async_computation.73 | async-start | bytes 983040 | tf_op jit(solution)/shard_map/reduce_scatter | solution.py:56
  1451.1 187.1 %reduce-scatter.107.cloned.1.call-start = ((), (), s32[]{:S(2)}) async-start(), calls=%async_computation.75 | async-start | bytes 983040 | tf_op jit(solution)/shard_map/reduce_scatter | solution.py:56
  1454.5 208.5 %reduce-scatter.101.cloned.1.call-start = ((), (), s32[]{:S(2)}) async-start(), calls=%async_computation.72 | async-start | bytes 983040 | tf_op jit(solution)/shard_map/reduce_scatter | solution.py:56
  1458.0 229.8 %reduce-scatter.105.cloned.1.call-start = ((), (), s32[]{:S(2)}) async-start(), calls=%async_computation.74 | async-start | bytes 983040 | tf_op jit(solution)/shard_map/reduce_scatter | solution.py:56
  1461.7 248.1 %reduce-scatter.93.cloned.1.call-start = ((), (), s32[]{:S(2)}) async-start(), calls=%async_computation.68 | async-start | bytes 491520 | tf_op jit(solution)/shard_map/reduce_scatter | solution.py:56
  1464.3 266.8 %reduce-scatter.95.cloned.1.call-start = ((), (), s32[]{:S(2)}) async-start(), calls=%async_computation.69 | async-start | bytes 491520 | tf_op jit(solution)/shard_map/reduce_scatter | solution.py:56
  1466.9 285.3 %reduce-scatter.99.cloned.1.call-start = ((), (), s32[]{:S(2)}) async-start(), calls=%async_computation.71 | async-start | bytes 491520 | tf_op jit(solution)/shard_map/reduce_scatter | solution.py:56
  1471.9 301.5 %reduce-scatter.97.cloned.1.call-start = ((), (), s32[]{:S(2)}) async-start(), calls=%async_computation.70 | async-start | bytes 491520 | tf_op jit(solution)/shard_map/reduce_scatter | solution.py:56
  1476.0 318.6 %reduce-scatter.77.cloned.1.call-start = ((), (), s32[]{:S(2)}) async-start(), calls=%async_computation.60 | async-start | bytes 491520 | tf_op jit(solution)/shard_map/reduce_scatter | solution.py:56
  1524.5 291.3 %reduce-scatter.79.cloned.1.call-start = ((), (), s32[]{:S(2)}) async-start(), calls=%async_computation.61 | async-start | bytes 491520 | tf_op jit(solution)/shard_map/reduce_scatter | solution.py:56
  1532.5 304.3 %reduce-scatter.87.cloned.1.call-start = ((), (), s32[]{:S(2)}) async-start(), calls=%async_computation.65 | async-start | bytes 491520 | tf_op jit(solution)/shard_map/reduce_scatter | solution.py:56
  1538.9 319.2 %reduce-scatter.83.cloned.1.call-start = ((), (), s32[]{:S(2)}) async-start(), calls=%async_computation.63 | async-start | bytes 491520 | tf_op jit(solution)/shard_map/reduce_scatter | solution.py:56
  1544.0 335.1 %reduce-scatter.91.cloned.1.call-start = ((), (), s32[]{:S(2)}) async-start(), calls=%async_computation.67 | async-start | bytes 491520 | tf_op jit(solution)/shard_map/reduce_scatter | solution.py:56
  1551.7 348.7 %reduce-scatter.89.cloned.1.call-start = ((), (), s32[]{:S(2)}) async-start(), calls=%async_computation.66 | async-start | bytes 491520 | tf_op jit(solution)/shard_map/reduce_scatter | solution.py:56
  1559.6 362.0 %reduce-scatter.85.cloned.1.call-start = ((), (), s32[]{:S(2)}) async-start(), calls=%async_computation.64 | async-start | bytes 491520 | tf_op jit(solution)/shard_map/reduce_scatter | solution.py:56
  1564.1 379.3 %reduce-scatter.81.cloned.1.call-start = ((), (), s32[]{:S(2)}) async-start(), calls=%async_computation.62 | async-start | bytes 491520 | tf_op jit(solution)/shard_map/reduce_scatter | solution.py:56
  1568.5 403.8 %reduce-scatter.73.cloned.1.call-start = ((), (), s32[]{:S(2)}) async-start(), calls=%async_computation.58 | async-start | bytes 1966080 | tf_op jit(solution)/shard_map/reduce_scatter | solution.py:89
  1570.6 433.1 %reduce-scatter.75.cloned.1.call-start = ((), (), s32[]{:S(2)}) async-start(), calls=%async_computation.59 | async-start | bytes 1966080 | tf_op jit(solution)/shard_map/reduce_scatter | solution.py:89
  1572.7 1152.2 %all-reduce.6.cloned.1.call-start = ((), (), s32[]{:S(2)}) async-start(), calls=%async_computation.84 | async-start | bytes 5767168 | tf_op jit(solution)/shard_map/psum | solution.py:58
  1943.5 793.2 %reduce-scatter.65.cloned.1.call-start = ((), (), s32[]{:S(2)}) async-start(), calls=%async_computation.52 | async-start | bytes 3932160 | tf_op jit(solution)/shard_map/reduce_scatter | solution.py:89
  1947.4 789.2 %reduce-scatter.71.cloned.1.call-start = ((), (), s32[]{:S(2)}) async-start(), calls=%async_computation.57 | async-start | bytes 3932160 | tf_op jit(solution)/shard_map/reduce_scatter | solution.py:89
  1952.0 788.4 %reduce-scatter.53.cloned.1.call-start = ((), (), s32[]{:S(2)}) async-start(), calls=%async_computation.41 | async-start | bytes 3932160 | tf_op jit(solution)/shard_map/reduce_scatter | solution.py:81
  1956.1 788.2 %reduce-scatter.59.cloned.1.call-start = ((), (), s32[]{:S(2)}) async-start(), calls=%async_computation.47 | async-start | bytes 3932160 | tf_op jit(solution)/shard_map/reduce_scatter | solution.py:81
  (242 other events, 4473.1 us)
Sparse Core Ops, SparseCore 0:
  11.7 22.3 all-gather.16
  803.7 39.4 reduce-scatter.48
  845.7 19.6 all-gather.22
  887.6 37.9 reduce-scatter.54
  929.4 19.6 all-gather.24
  1001.1 25.5 all-gather.18
  1029.2 37.9 reduce-scatter.56
  1069.9 37.9 reduce-scatter.50
  1112.7 19.6 all-gather.26
  1133.8 19.6 all-gather.38
  1155.7 19.6 all-gather.20
  1176.8 19.6 all-gather.36
  1199.0 37.9 reduce-scatter.66
  1239.6 37.9 reduce-scatter.60
  1284.1 19.6 all-gather.32
  1305.2 19.6 all-gather.28
  1327.2 37.9 reduce-scatter.68
  1367.8 37.9 reduce-scatter.62
  1412.0 19.6 all-gather.30
  1433.1 19.6 all-gather.34
  1455.1 23.2 reduce-scatter.118
  1480.7 22.5 reduce-scatter.116
  1505.6 19.8 reduce-scatter.112
  1527.7 18.9 reduce-scatter.108
  1570.0 18.8 reduce-scatter.110
  1591.7 21.5 reduce-scatter.102
  1615.6 22.5 reduce-scatter.106
  1640.4 22.5 reduce-scatter.100
  1665.2 22.5 reduce-scatter.104
  1690.0 19.8 reduce-scatter.92
  1712.3 18.8 reduce-scatter.94
  1733.3 18.8 reduce-scatter.98
  1754.6 18.8 reduce-scatter.96
  1775.8 18.8 reduce-scatter.76
  1796.9 18.8 reduce-scatter.78
  1817.9 18.8 reduce-scatter.86
  1839.2 18.8 reduce-scatter.82
  1860.2 18.8 reduce-scatter.90
  1881.5 18.8 reduce-scatter.88
  1902.7 18.8 reduce-scatter.84
  1924.5 18.8 reduce-scatter.80
  1945.8 26.4 reduce-scatter.72
  1975.5 28.1 reduce-scatter.74
  2008.4 83.7 all-reduce.5
  2094.8 38.0 reduce-scatter.64
  2135.2 37.9 reduce-scatter.70
  2175.8 37.9 reduce-scatter.52
  2216.1 37.9 reduce-scatter.58
  (1 shorter events, 18.7 us)
where the time goes:
time: 2840 us; the launch traced here: 2790 us
  local copies, waits for them, and re-layouts  1420 us (50%)
  waiting for transfers between devices  736 us (26%)
  blocking collectives  258 us (9%)
  matrix products  239 us (8%)
  other arithmetic  115 us (4%)
    unnamed x520, local copies, waits for them, and re-layouts  1140 us
    reduce_scatter x16, waiting for transfers between devices, reduce_grads(): lax.psum_scatter(shortened(local_grads), 'wide', scatter_dimension=0, til...  353 us
    reduce_scatter x8, waiting for transfers between devices, grad_partial(): return lax.psum_scatter(terms, 'narrow', scatter_dimension=1, tiled=True)  182 us
    all_gather x11, blocking collectives, gather_weights(): lax.all_gather(shortened(matrices), 'wide', axis=0, tiled=True)  179 us
    reduce_scatter x6, waiting for transfers between devices, partial_out(): return lax.psum_scatter(terms, 'narrow', scatter_dimension=1, tiled=True)  150 us
    slice x3, local copies, waits for them, and re-layouts, block_scores(): scores = scores + bias_full[:, row_start:row_start + row_count, :]  109 us
    rev x1, local copies, waits for them, and re-layouts, bias_grad_block(): flipped = grad_scores[:, ::-1, :]  96.1 us
  transfers between devices with their start and end apart: 49, of which 30 were waited for; matrix products, arithmetic and copies ran while one was open for 60% of the time, Pallas kernels for 0%

commit v1 on v0

v1 whole, which is shorter than its diff:
```python
from functools import partial

import jax
import jax.numpy as jnp
from jax import lax
from jax.experimental import pallas as pl
from jax.experimental.pallas import tpu as pltpu
from jax.sharding import PartitionSpec as P

D = 768
HD = 192
HEADS = 12
DHEAD = 64
FFB = 512
BUCKETS = 32
LEN = 1024
ENC = 512
PIC = 256
TILES = 11
ROWS = 32

precise = lax.Precision.HIGHEST
epsilon = 1e-06
masked_value = -1e30
f32 = jnp.float32
bf16 = jnp.bfloat16
MESH = pl.DeviceIdType.MESH
ANY = pl.BlockSpec(memory_space=pl.ANY)
VMEM_LIMIT = 60 << 20


def nn(a, b):
    return lax.dot_general(a, b, (((1,), (0,)), ((), ())), preferred_element_type=f32)


def nt(a, b):
    return lax.dot_general(a, b, (((1,), (1,)), ((), ())), preferred_element_type=f32)


def tn(a, b):
    return lax.dot_general(a, b, (((0,), (0,)), ((), ())), preferred_element_type=f32)


def rows_loop(total, step, body, unroll=1):
    def run(i, carry):
        body(pl.ds(pl.multiple_of(i * step, step), step))
        return carry

    lax.fori_loop(0, total // step, run, 0, unroll=unroll)


def normed(x, gain):
    factor = lax.rsqrt(jnp.mean(x * x, axis=1, keepdims=True) + epsilon)
    return x * factor * gain


def norm_back(x, gain, upstream):
    factor = lax.rsqrt(jnp.mean(x * x, axis=1, keepdims=True) + epsilon)
    weighted = upstream * gain
    inner = jnp.sum(weighted * x, axis=1, keepdims=True)
    dx = weighted * factor - x * (factor * factor * factor * inner * (1.0 / D))
    return dx, jnp.sum(upstream * x * factor, axis=0, keepdims=True)


def own_blocks():
    me = lax.axis_index("narrow")
    return (me, 3 - me)


def block_rows(blk):
    return pl.ds(pl.multiple_of(blk * 256, 256), 256)


def softmax_rows(v):
    e = jnp.exp(v - jnp.max(v, axis=1, keepdims=True))
    return e * (1.0 / jnp.sum(e, axis=1, keepdims=True))


def self_forward_kernel(
    info, xf, w, off, gain, q_o, kv_o, at_o, p_o, h1_o, nf, mask, tb, s
):
    n = pl.program_id(0)
    blks = own_blocks()

    @pl.when(n == 0)
    def _():
        def norm_rows(r):
            nf[r, :] = normed(xf[r, :].astype(f32), gain[...]).astype(bf16)

        rows_loop(LEN, 64, norm_rows)
        start, length = info[0], info[1]
        for i in range(2):
            h1_o[i * 256 : (i + 1) * 256, :] = xf[block_rows(blks[i]), :].astype(f32)

            def mask_rows(r, i=i):
                shape = (ROWS, LEN)
                qi = blks[i] * 256 + r.start + lax.broadcasted_iota(jnp.int32, shape, 0)
                kj = lax.broadcasted_iota(jnp.int32, shape, 1)
                inside = (qi >= start) & (qi < start + PIC) & (kj >= start) & (kj < start + PIC)
                allowed = ((kj <= qi) | inside) & (kj < length)
                mask[pl.ds(i * 256 + r.start, ROWS), :] = jnp.where(allowed, 0.0, masked_value)

            rows_loop(256, ROWS, mask_rows)

    kv_o[0] = nn(nf[...], w[0, :, 384:768]).astype(bf16).T
    for i in range(2):
        q_o[0, i * 256 : (i + 1) * 256, :] = nn(nf[block_rows(blks[i]), :], w[0, :, 0:192]).astype(bf16)
    for h in range(3):
        for t in range(TILES):
            line = jnp.broadcast_to(off[0, h : h + 1, 128 * t : 128 * t + 256], (128, 256))
            tb[t] = pltpu.roll(line, 129, 1, stride=1, stride_axis=0)[:, :128]
        hs = slice(h * DHEAD, (h + 1) * DHEAD)
        vs = slice(HD + h * DHEAD, HD + (h + 1) * DHEAD)
        for i in range(2):
            s[...] = nn(q_o[0, i * 256 : (i + 1) * 256, hs], kv_o[0, hs, :])
            for r in range(2):
                idx = [jnp.minimum(kb - 2 * blks[i] - r, 3) + 7 for kb in range(8)]

                def soft_rows(rr, i=i, r=r, h=h, idx=idx):
                    bias = jnp.concatenate([tb[idx[kb], rr, :] for kb in range(8)], axis=1)
                    v = s[pl.ds(r * 128 + rr.start, ROWS), :] + bias
                    v = v + mask[pl.ds(i * 256 + r * 128 + rr.start, ROWS), :]
                    p_o[0, h, pl.ds(i * 256 + r * 128 + rr.start, ROWS), :] = softmax_rows(v).astype(bf16)

                rows_loop(128, ROWS, soft_rows)
            at_o[0, i * 256 : (i + 1) * 256, hs] = nt(
                p_o[0, h, i * 256 : (i + 1) * 256, :], kv_o[0, vs, :]
            ).astype(bf16)
    h1_o[...] += nt(at_o[0], w[0, :, 192:384])


def whole(shape):
    zero = (0,) * len(shape)
    return pl.BlockSpec(shape, lambda n: zero)


def slab(shape):
    zero = (0,) * len(shape)
    return pl.BlockSpec((1,) + shape, lambda n: (n,) + zero)


def params():
    return pltpu.CompilerParams(
        dimension_semantics=("arbitrary",), vmem_limit_bytes=VMEM_LIMIT
    )


def out(shape, dtype):
    return jax.ShapeDtypeStruct(shape, dtype)


SMEM = pl.BlockSpec(memory_space=pltpu.SMEM)


def cost(gflop):
    return pl.CostEstimate(flops=int(gflop * 1e9), bytes_accessed=20 << 20, transcendentals=0)


def self_forward(info, xf, w, off, gain):
    return pl.pallas_call(
        self_forward_kernel,
        grid=(4,),
        in_specs=[SMEM, whole((LEN, D)), slab((D, D)), slab((3, 2048)), whole((1, D))],
        out_specs=[slab((512, HD)), slab((2 * HD, LEN)), slab((512, HD)), slab((3, 512, LEN)), whole((512, D))],
        out_shape=[
            out((4, 512, HD), bf16),
            out((4, 2 * HD, LEN), bf16),
            out((4, 512, HD), bf16),
            out((4, 3, 512, LEN), bf16),
            out((512, D), f32),
        ],
        scratch_shapes=[
            pltpu.VMEM((LEN, D), bf16),
            pltpu.VMEM((512, LEN), f32),
            pltpu.VMEM((TILES, 128, 128), f32),
            pltpu.VMEM((256, LEN), f32),
        ],
        compiler_params=params(),
        cost_estimate=cost(20),
        name="self_forward",
    )(info, xf, w, off, gain)


def cross_forward_kernel(h1, ef, w, gain, q_o, kv_o, at_o, p_o, h2_o, nc, s):
    n = pl.program_id(0)

    @pl.when(n == 0)
    def _():
        def norm_rows(r):
            x = h1[r, :]
            nc[r, :] = normed(x, gain[...]).astype(bf16)
            h2_o[r, :] = x

        rows_loop(512, 64, norm_rows)

    kv_o[0] = nn(ef[...], w[0, :, 384:768]).astype(bf16).T
    q_o[0] = nn(nc[...], w[0, :, 0:192]).astype(bf16)
    for h in range(3):
        hs = slice(h * DHEAD, (h + 1) * DHEAD)
        vs = slice(HD + h * DHEAD, HD + (h + 1) * DHEAD)
        s[...] = nn(q_o[0, :, hs], kv_o[0, hs, :])

        def soft_rows(r, h=h):
            p_o[0, h, r, :] = softmax_rows(s[r, :]).astype(bf16)

        rows_loop(512, 64, soft_rows)
        at_o[0, :, hs] = nt(p_o[0, h], kv_o[0, vs, :]).astype(bf16)
    h2_o[...] += nt(at_o[0], w[0, :, 192:384])


def cross_forward(h1, ef, w, gain):
    return pl.pallas_call(
        cross_forward_kernel,
        grid=(4,),
        in_specs=[whole((512, D)), whole((ENC, D)), slab((D, D)), whole((1, D))],
        out_specs=[slab((512, HD)), slab((2 * HD, ENC)), slab((512, HD)), slab((3, 512, ENC)), whole((512, D))],
        out_shape=[
            out((4, 512, HD), bf16),
            out((4, 2 * HD, ENC), bf16),
            out((4, 512, HD), bf16),
            out((4, 3, 512, ENC), bf16),
            out((512, D), f32),
        ],
        scratch_shapes=[pltpu.VMEM((512, D), bf16), pltpu.VMEM((512, ENC), f32)],
        compiler_params=params(),
        cost_estimate=cost(10),
        name="cross_forward",
    )(h1, ef, w, gain)


GELU_A = 0.7978845608028654
GELU_B = 0.044715


def feed_kernel(h2, cf, w, gain, gw_o, out_o, d2_o, gg_o, nf, nft, ct, gu, da, act, dgu, acc):
    n = pl.program_id(0)

    @pl.when(n == 0)
    def _():
        def norm_rows(r):
            x = h2[r, :]
            nf[r, :] = normed(x, gain[...]).astype(bf16)
            acc[r, :] = x
            d2_o[r, :] = jnp.zeros((64, D), f32)

        rows_loop(512, 64, norm_rows)
        nft[...] = nf[...].T
        ct[...] = cf[...].T

    gu[...] = nn(nf[...], w[0, :, : 2 * FFB])
    da[...] = nn(cf[...], w[0, :, 2 * FFB :])

    def gelu_rows(r):
        gate = gu[r, :FFB]
        up = gu[r, FFB:]
        d_act = da[r, :]
        sq = gate * gate
        th = jnp.tanh(GELU_A * gate * (1.0 + GELU_B * sq))
        half = 0.5 + 0.5 * th
        gelu = gate * half
        slope = half + 0.5 * GELU_A * gate * (1.0 - th * th) * (1.0 + 3.0 * GELU_B * sq)
        act[r, :] = (gelu * up).astype(bf16)
        dgu[r, :FFB] = (d_act * up * slope).astype(bf16)
        dgu[r, FFB:] = (d_act * gelu).astype(bf16)

    rows_loop(512, 16, gelu_rows)
    acc[...] += nt(act[...], w[0, :, 2 * FFB :])
    gw_o[0, :, : 2 * FFB] = nn(nft[...], dgu[...]).astype(bf16)
    gw_o[0, :, 2 * FFB :] = nn(ct[...], act[...]).astype(bf16)
    d2_o[...] += nt(dgu[...], w[0, :, : 2 * FFB])

    @pl.when(n == 3)
    def _():
        gg_o[...] = jnp.zeros((1, D), f32)

        def back_rows(r):
            dx, gg = norm_back(h2[r, :], gain[...], d2_o[r, :])
            d2_o[r, :] = cf[r, :].astype(f32) + dx
            gg_o[...] += gg
            out_o[r, :] = acc[r, :].astype(bf16)

        rows_loop(512, 64, back_rows)


def feed(h2, cf, w, gain):
    return pl.pallas_call(
        feed_kernel,
        grid=(4,),
        in_specs=[whole((512, D)), whole((512, D)), slab((D, 3 * FFB)), whole((1, D))],
        out_specs=[slab((D, 3 * FFB)), whole((512, D)), whole((512, D)), whole((1, D))],
        out_shape=[out((4, D, 3 * FFB), bf16), out((512, D), bf16), out((512, D), f32), out((1, D), f32)],
        scratch_shapes=[
            pltpu.VMEM((512, D), bf16),
            pltpu.VMEM((D, 512), bf16),
            pltpu.VMEM((D, 512), bf16),
            pltpu.VMEM((512, 2 * FFB), f32),
            pltpu.VMEM((512, FFB), f32),
            pltpu.VMEM((512, FFB), bf16),
            pltpu.VMEM((512, 2 * FFB), bf16),
            pltpu.VMEM((512, D), f32),
        ],
        compiler_params=params(),
        cost_estimate=cost(30),
        name="feed",
    )(h2, cf, w, gain)


def cross_backward_kernel(
    h1, ef, d2, w, gain, q, kv, at, p, gw_o, d1_o, gg_o, ge_o, gep_o, d2b, d2t, nct, eft, get, do, dp, ds, dq, dkv
):
    n = pl.program_id(0)

    @pl.when(n == 0)
    def _():
        def norm_rows(r):
            d2b[r, :] = d2[r, :].astype(bf16)
            d1_o[r, :] = jnp.zeros((64, D), f32)
            dp[r, :] = normed(h1[r, :], gain[...])

        rows_loop(512, 64, norm_rows)
        nct[...] = dp[...].astype(bf16).T
        d2t[...] = d2b[...].T
        eft[...] = ef[...].T
        get[...] = jnp.zeros((D, ENC), f32)

    do[...] = nn(d2b[...], w[0, :, 192:384]).astype(bf16)
    for h in range(3):
        hs = slice(h * DHEAD, (h + 1) * DHEAD)
        vs = slice(HD + h * DHEAD, HD + (h + 1) * DHEAD)
        dp[:, :ENC] = nn(do[:, hs], kv[0, vs, :])

        def grad_rows(r, h=h, hs=hs):
            delta = jnp.sum(do[r, hs].astype(f32) * at[0, r, hs].astype(f32), axis=1, keepdims=True)
            ds[r, :] = (p[0, h, r, :].astype(f32) * (dp[r, :ENC] - delta)).astype(bf16)

        rows_loop(512, 64, grad_rows)
        dq[:, hs] = nt(ds[...], kv[0, hs, :]).astype(bf16)
        dkv[hs, :] = tn(q[0, :, hs], ds[...]).astype(bf16)
        dkv[vs, :] = tn(do[:, hs], p[0, h]).astype(bf16)
    d1_o[...] += nt(dq[...], w[0, :, 0:192])
    get[...] += nn(w[0, :, 384:768], dkv[...])
    gw_o[0, :, 0:384] = jnp.concatenate([nn(nct[...], dq[...]), nn(d2t[...], at[0])], axis=1).astype(bf16)
    gw_o[0, :, 384:768] = nt(eft[...], dkv[...]).astype(bf16)

    @pl.when(n == 3)
    def _():
        gg_o[...] = jnp.zeros((1, D), f32)

        def back_rows(r):
            dx, gg = norm_back(h1[r, :], gain[...], d1_o[r, :])
            d1_o[r, :] = d2[r, :] + dx
            gg_o[...] += gg

        rows_loop(512, 64, back_rows)
        me = lax.axis_index("narrow")
        pn = me + 1 - 2 * lax.rem(me, 2)
        for i in range(2):
            half = slice(i * 128, (i + 1) * 128)
            cols = lambda blk: pl.ds(pl.multiple_of(blk * 128, 128), 128)
            ge_o[half, :] = get[:, cols((me, 3 - me)[i])].T
            gep_o[half, :] = get[:, cols((pn, 3 - pn)[i])].T.astype(bf16)


def cross_backward(h1, ef, d2, w, gain, q, kv, at, p):
    return pl.pallas_call(
        cross_backward_kernel,
        grid=(4,),
        in_specs=[
            whole((512, D)),
            whole((ENC, D)),
            whole((512, D)),
            slab((D, D)),
            whole((1, D)),
            slab((512, HD)),
            slab((2 * HD, ENC)),
            slab((512, HD)),
            slab((3, 512, ENC)),
        ],
        out_specs=[slab((D, D)), whole((512, D)), whole((1, D)), whole((256, D)), whole((256, D))],
        out_shape=[out((4, D, D), bf16), out((512, D), f32), out((1, D), f32), out((256, D), f32), out((256, D), bf16)],
        scratch_shapes=[
            pltpu.VMEM((512, D), bf16),
            pltpu.VMEM((D, 512), bf16),
            pltpu.VMEM((D, 512), bf16),
            pltpu.VMEM((D, ENC), bf16),
            pltpu.VMEM((D, ENC), f32),
            pltpu.VMEM((512, HD), bf16),
            pltpu.VMEM((512, D), f32),
            pltpu.VMEM((512, ENC), bf16),
            pltpu.VMEM((512, HD), bf16),
            pltpu.VMEM((2 * HD, ENC), bf16),
        ],
        compiler_params=params(),
        cost_estimate=cost(14),
        name="cross_backward",
    )(h1, ef, d2, w, gain, q, kv, at, p)


def self_backward_kernel(
    xf, d1, w, gain, q, kv, at, p, gw_o, g_o, gp_o, dl_o, d1b, d1t, nft, nqt, gt, gq, do, dp, ds, dq, dkv, dt
):
    n = pl.program_id(0)
    blks = own_blocks()

    @pl.when(n == 0)
    def _():
        def cast_rows(r):
            d1b[r, :] = d1[r, :].astype(bf16)
            gq[r, :] = jnp.zeros((64, D), f32)

        rows_loop(512, 64, cast_rows)
        d1t[...] = d1b[...].T
        for i in range(4):
            part = normed(xf[i * 256 : (i + 1) * 256, :].astype(f32), gain[...]).astype(bf16)
            nft[:, i * 256 : (i + 1) * 256] = part.T
        for i in range(2):
            part = normed(xf[block_rows(blks[i]), :].astype(f32), gain[...]).astype(bf16)
            nqt[:, i * 256 : (i + 1) * 256] = part.T
        gt[...] = jnp.zeros((D, LEN), f32)

    do[...] = nn(d1b[...], w[0, :, 192:384]).astype(bf16)
    for h in range(3):
        hs = slice(h * DHEAD, (h + 1) * DHEAD)
        vs = slice(HD + h * DHEAD, HD + (h + 1) * DHEAD)
        dt[...] = jnp.zeros((TILES, 128, 128), f32)
        dk = jnp.zeros((DHEAD, LEN), f32)
        dv = jnp.zeros((DHEAD, LEN), f32)
        for i in range(2):
            half = slice(i * 256, (i + 1) * 256)
            dp[...] = nn(do[half, hs], kv[0, vs, :])
            for r in range(2):
                idx = [jnp.minimum(kb - 2 * blks[i] - r, 3) + 7 for kb in range(8)]

                def grad_rows(rr, i=i, r=r, h=h, hs=hs, idx=idx):
                    rows = pl.ds(i * 256 + r * 128 + rr.start, ROWS)
                    local = pl.ds(r * 128 + rr.start, ROWS)
                    delta = jnp.sum(
                        do[rows, hs].astype(f32) * at[0, rows, hs].astype(f32), axis=1, keepdims=True
                    )
                    grad = p[0, h, rows, :].astype(f32) * (dp[local, :] - delta)
                    ds[local, :] = grad.astype(bf16)
                    for kb in range(8):
                        dt[idx[kb], rr, :] += grad[:, kb * 128 : (kb + 1) * 128]

                rows_loop(128, ROWS, grad_rows)
            dq[half, hs] = nt(ds[...], kv[0, hs, :]).astype(bf16)
            dk = dk + tn(q[0, half, hs], ds[...])
            dv = dv + tn(do[half, hs], p[0, h, half, :])
        dkv[hs, :] = dk.astype(bf16)
        dkv[vs, :] = dv.astype(bf16)
        for t in range(TILES):
            part = jnp.concatenate([dt[t], jnp.zeros((128, 128), f32)], axis=1)
            height = 128
            while height > 1:
                height //= 2
                part = part[:height] + pltpu.roll(part[height:], 256 - height, 1)
            dl_o[0, h * TILES + t : h * TILES + t + 1, :] = pltpu.roll(part, 127, 1)
    gq[...] += nt(dq[...], w[0, :, 0:192])
    gt[...] += nn(w[0, :, 384:768], dkv[...])
    gw_o[0, :, 0:384] = jnp.concatenate([nn(nqt[...], dq[...]), nn(d1t[...], at[0])], axis=1).astype(bf16)
    gw_o[0, :, 384:768] = nt(nft[...], dkv[...]).astype(bf16)

    @pl.when(n == 3)
    def _():
        pn = blks[0] + 1 - 2 * lax.rem(blks[0], 2)
        for i in range(2):
            half = slice(i * 256, (i + 1) * 256)
            g_o[half, :] = gq[half, :] + gt[:, block_rows(blks[i])].T
            gp_o[half, :] = gt[:, block_rows((pn, 3 - pn)[i])].T.astype(bf16)


def self_backward(xf, d1, w, gain, q, kv, at, p):
    return pl.pallas_call(
        self_backward_kernel,
        grid=(4,),
        in_specs=[
            whole((LEN, D)),
            whole((512, D)),
            slab((D, D)),
            whole((1, D)),
            slab((512, HD)),
            slab((2 * HD, LEN)),
            slab((512, HD)),
            slab((3, 512, LEN)),
        ],
        out_specs=[slab((D, D)), whole((512, D)), whole((512, D)), slab((3 * TILES, 256))],
        out_shape=[out((4, D, D), bf16), out((512, D), f32), out((512, D), bf16), out((4, 3 * TILES, 256), f32)],
        scratch_shapes=[
            pltpu.VMEM((512, D), bf16),
            pltpu.VMEM((D, 512), bf16),
            pltpu.VMEM((D, LEN), bf16),
            pltpu.VMEM((D, 512), bf16),
            pltpu.VMEM((D, LEN), f32),
            pltpu.VMEM((512, D), f32),
            pltpu.VMEM((512, HD), bf16),
            pltpu.VMEM((256, LEN), f32),
            pltpu.VMEM((256, LEN), bf16),
            pltpu.VMEM((512, HD), bf16),
            pltpu.VMEM((2 * HD, LEN), bf16),
            pltpu.VMEM((TILES, 128, 128), f32),
        ],
        compiler_params=params(),
        cost_estimate=cost(25),
        name="self_backward",
    )(xf, d1, w, gain, q, kv, at, p)


def place_here():
    d, w, n = lax.axis_index("dp"), lax.axis_index("wide"), lax.axis_index("narrow")
    return d, w, n, n + 1 - 2 * lax.rem(n, 2), lax.rem(n + 2, 4), 3 - n


def remote(src, dst, send, recv, dev):
    return pltpu.make_async_remote_copy(
        src_ref=src, dst_ref=dst, send_sem=send, recv_sem=recv, device_id=dev, device_id_type=MESH
    )


def greet(wide):
    d, w, n, pn, yn, dn = place_here()
    barrier = pltpu.get_barrier_semaphore()
    for dev in ((d, w, pn), (d, w, yn), (d, w, dn), (1 - d, w, n)):
        pl.semaphore_signal(barrier, inc=1, device_id=dev, device_id_type=MESH)

    def line(k, carry):
        dev = (d, lax.rem(w + k, wide), n)
        pl.semaphore_signal(barrier, inc=1, device_id=dev, device_id_type=MESH)
        return carry

    lax.fori_loop(1, wide, line, 0)
    pl.semaphore_wait(barrier, wide + 3)


def loop(lo, hi, body):
    def run(k, carry):
        body(k)
        return carry

    lax.fori_loop(lo, hi, run, 0)


def gather_kernel(
    wide, hid, enc, cot, tab, ps, pc, pf, xf, ef, cf, tabs, gs, gc, gf, ls, ins, inr, zs, zr, ys, yr, xs, xr, cs, cr
):
    d, w, n, pn, yn, dn = place_here()
    y = n // 2
    groups = ((ps, gs, 0, 768, True), (pc, gc, 0, 768, True), (pf, gf, 0, 512, True), (pf, gf, 512, 1024, False))

    def cols(s, which):
        start, width, split = groups[s][2:]
        if which == 2 or not split:
            return pl.ds(start, width)
        half = width // 2
        pos = d if which == 0 else 1 - d
        return pl.ds(pl.multiple_of(start + pos * half, 128), half)

    def own(s, which):
        return groups[s][0].at[:, cols(s, which)]

    def spot(s, slab, row, which):
        return groups[s][1].at[slab, row, :, cols(s, which)]

    def zcopy(s, k):
        return remote(own(s, 0), spot(s, n, w, 0), zs.at[s, k], zr.at[s, w], (d, lax.rem(w + k, wide), n))

    def zgot(s, row):
        return remote(spot(s, n, row, 0), spot(s, n, row, 0), zs.at[s, 0], zr.at[s, row], (1 - d, w, n))

    def ycopy(s, row, src):
        return remote(src, spot(s, n, row, 0), ys.at[s, row], yr.at[s, row], (d, w, yn))

    def ygot(s, row):
        return remote(spot(s, yn, row, 0), spot(s, yn, row, 0), ys.at[s, row], yr.at[s, row], (d, w, yn))

    def slab_of(side):
        return n if side == 0 else yn

    def xcopy(s, side, row):
        ref = spot(s, slab_of(side), row, 0)
        return remote(ref, ref, xs.at[s, side, row], xr.at[s, side, row], (1 - d, w, n))

    def xgot(s, side, row):
        ref = spot(s, slab_of(side), row, 1)
        return remote(ref, ref, xs.at[s, side, row], xr.at[s, side, row], (1 - d, w, n))

    def ccopy(s, side, row, src=None):
        ref = spot(s, slab_of(side), row, 2)
        return remote(ref if src is None else src, ref, cs.at[s, side, row], cr.at[s, side, row], (d, w, pn))

    def cgot(s, side, row):
        ref = spot(s, pn if side == 0 else 3 - n, row, 2)
        return remote(ref, ref, cs.at[s, side, row], cr.at[s, side, row], (d, w, pn))

    local = [
        pltpu.make_async_copy(src, dst, ls.at[i])
        for i, (src, dst) in enumerate(
            (
                (ps, gs.at[n, w]),
                (pc, gc.at[n, w]),
                (pf, gf.at[n, w]),
                (hid.at[y], xf.at[n]),
                (enc.at[y], ef.at[n]),
                (cot.at[y], cf.at[0]),
                (tab, tabs.at[n]),
            )
        )
    ]
    for copy in local:
        copy.start()
    greet(wide)
    diag, pair = (d, w, dn), (d, w, pn)
    first = [
        remote(hid.at[1 - y], xf.at[n], ins.at[0], inr.at[0], diag),
        remote(enc.at[1 - y], ef.at[n], ins.at[1], inr.at[1], diag),
        remote(cot.at[1 - y], cf.at[1], ins.at[2], inr.at[2], diag),
        remote(tab, tabs.at[n], ins.at[3], inr.at[3], pair),
        remote(tab, tabs.at[n], ins.at[4], inr.at[4], (d, w, yn)),
        remote(tab, tabs.at[n], ins.at[5], inr.at[5], diag),
        remote(hid.at[y], xf.at[n], ins.at[6], inr.at[6], pair),
        remote(enc.at[y], ef.at[n], ins.at[7], inr.at[7], pair),
    ]
    got = [
        remote(xf.at[dn], xf.at[dn], ins.at[0], inr.at[0], diag),
        remote(ef.at[dn], ef.at[dn], ins.at[1], inr.at[1], diag),
        remote(cf.at[1], cf.at[1], ins.at[2], inr.at[2], diag),
        remote(tabs.at[pn], tabs.at[pn], ins.at[3], inr.at[3], pair),
        remote(tabs.at[yn], tabs.at[yn], ins.at[4], inr.at[4], (d, w, yn)),
        remote(tabs.at[dn], tabs.at[dn], ins.at[5], inr.at[5], diag),
        remote(xf.at[pn], xf.at[pn], ins.at[6], inr.at[6], pair),
        remote(ef.at[pn], ef.at[pn], ins.at[7], inr.at[7], pair),
        remote(xf.at[yn], xf.at[yn], ins.at[8], inr.at[8], pair),
        remote(ef.at[yn], ef.at[yn], ins.at[9], inr.at[9], pair),
    ]
    later = [
        remote(xf.at[dn], xf.at[dn], ins.at[8], inr.at[8], pair),
        remote(ef.at[dn], ef.at[dn], ins.at[9], inr.at[9], pair),
    ]
    for copy in first:
        copy.start()
    for s in range(4):
        loop(1, wide, lambda k, s=s: zcopy(s, k).start())
        ycopy(s, w, own(s, 0)).start()
        ccopy(s, 0, w, own(s, 2)).start()
    got[0].wait_recv()
    later[0].start()
    got[1].wait_recv()
    later[1].start()

    def zstep(s):
        def one(k):
            row = lax.rem(w + k, wide)
            zgot(s, row).wait_recv()
            ycopy(s, row, spot(s, n, row, 0)).start()
            if groups[s][4]:
                xcopy(s, 0, row).start()
            else:
                ccopy(s, 0, row).start()

        loop(1, wide, one)

    def ystep(s):
        def one(k):
            row = lax.rem(w + k, wide)
            ygot(s, row).wait_recv()
            if groups[s][4]:
                xcopy(s, 1, row).start()
            else:
                ccopy(s, 1, row).start()

        loop(0, wide, one)

    def xstep(s):
        def one(side):
            def step(k):
                row = lax.rem(w + k, wide)
                xgot(s, side, row).wait_recv()
                ccopy(s, side, row).start()

            return step

        loop(1, wide, one(0))
        loop(0, wide, one(1))

    zstep(0)
    ystep(0)
    zstep(1)
    ystep(1)
    xstep(0)
    zstep(2)
    ystep(2)
    xstep(1)
    zstep(3)
    ystep(3)
    xstep(2)
    for copy in got[2:]:
        copy.wait_recv()
    for copy in local:
        copy.wait()
    for copy in first + later:
        copy.wait_send()

    def finish(k):
        row = lax.rem(w + k, wide)
        for s in range(4):
            for side in range(2):
                cgot(s, side, row).wait_recv()
                ccopy(s, side, row).wait_send()
            ycopy(s, row, spot(s, n, row, 0)).wait_send()
            if groups[s][4]:
                xcopy(s, 1, row).wait_send()

    loop(0, wide, finish)

    def finish_line(k):
        row = lax.rem(w + k, wide)
        for s in range(4):
            zcopy(s, k).wait_send()
            if groups[s][4]:
                xcopy(s, 0, row).wait_send()

    loop(1, wide, finish_line)


def gather(wide, hid, enc, cot, tab, ps, pc, pf):
    rl = ps.shape[0]
    sem = pltpu.SemaphoreType.DMA
    return pl.pallas_call(
        partial(gather_kernel, wide),
        in_specs=[ANY] * 7,
        out_specs=[ANY] * 7,
        out_shape=[
            out((4, 256, D), bf16),
            out((4, 128, D), bf16),
            out((2, 256, D), bf16),
            out((4, 32, 128), f32),
            out((4, wide, rl, D), bf16),
            out((4, wide, rl, D), bf16),
            out((4, wide, rl, 2 * D), bf16),
        ],
        scratch_shapes=[
            sem((7,)),
            sem((10,)),
            sem((10,)),
            sem((4, wide)),
            sem((4, wide)),
            sem((4, wide)),
            sem((4, wide)),
            sem((4, 2, wide)),
            sem((4, 2, wide)),
            sem((4, 2, wide)),
            sem((4, 2, wide)),
        ],
        compiler_params=pltpu.CompilerParams(collective_id=0, has_side_effects=True),
        name="gather",
    )(hid, enc, cot, tab, ps, pc, pf)


SHARE = (512, 256, 512, 256)


def reduce_kernel(
    wide, rl, ff, cr, se, outp, gxo, gxp, geo, gep, xf, d1, gain, gfeed, gcross, tg,
    out_o, gin_o, gen_o, sg_o, st_o, f0, f1, f2, f3, *scratch
):
    d, w, n, pn, yn, dn = place_here()
    y = n // 2
    pair, line_y, diag, line_x = (d, w, pn), (d, w, yn), (d, w, dn), (1 - d, w, n)
    it = iter(scratch)
    take = lambda count: [next(it) for _ in range(count)]
    acc, rc, rx, ry1, ry2, rz1, rz2, fin, rf = (take(4) for _ in range(9))
    rgx, rge, tmp_in, tmp_en, back_in, back_en, rows_f = take(7)
    sg, st, rsg, rst, rsgz, rstz = take(6)
    ls, lin, cs, crv, xs, xr, ys, yr, zs, zr, fs, fr, ms, mr, ss, sr, os = take(17)
    source = ((ff, 0), (ff, D), (cr, 0), (se, 0))
    final = (f0, f1, f2, f3)
    step_rows = 64 if rl % 64 == 0 else rl
    parts = rl // step_rows

    def rows(j):
        return pl.ds(pl.multiple_of(j * step_rows, 8), step_rows)

    def half(g, mine):
        a = SHARE[g] // 2
        pos = d if mine else 1 - d
        return pl.ds(pl.multiple_of(pos * a, 128), a)

    def rest(g):
        return pl.ds(SHARE[g], D - SHARE[g])

    def slab(g, k):
        ref, start = source[g]
        return ref.at[k, :, :, pl.ds(start, D)]

    loads = [
        [pltpu.make_async_copy(slab(g, k), acc[g].at[i], ls.at[g, i]) for i, k in enumerate((n, yn))]
        for g in range(4)
    ]
    core = [
        [remote(slab(g, k), rc[g].at[i], cs.at[g, i], crv.at[g, i], pair) for i, k in enumerate((pn, 3 - n))]
        for g in range(4)
    ]
    for g in range(4):
        for copy in loads[g]:
            copy.start()
    out_local = pltpu.make_async_copy(outp.at[0], out_o.at[y], os.at[0])
    out_local.start()
    greet(wide)
    cross = [
        remote(gxp, rgx, ms.at[0], mr.at[0], pair),
        remote(gep, rge, ms.at[1], mr.at[1], pair),
        remote(outp.at[1], out_o.at[y], ms.at[2], mr.at[2], diag),
    ]
    out_got = remote(out_o.at[1 - y], out_o.at[1 - y], ms.at[2], mr.at[2], diag)
    for copy in cross:
        copy.start()
    for g in range(4):
        for copy in core[g]:
            copy.start()

    xcopy = [
        remote(acc[g].at[:, :, :, half(g, False)], rx[g], xs.at[g], xr.at[g], line_x) for g in range(4)
    ]
    y1 = [
        remote(acc[g].at[1, :, :, half(g, True)], ry1[g], ys.at[g, 0], yr.at[g, 0], line_y) for g in range(4)
    ]
    y2 = [remote(acc[g].at[1, :, :, rest(g)], ry2[g], ys.at[g, 1], yr.at[g, 1], line_y) for g in range(4)]

    def zcopy(g, path, k):
        row = lax.rem(w + k, wide)
        if path == 0:
            src, dst = acc[g].at[0, row, :, half(g, True)], rz1[g].at[w]
        else:
            src, dst = acc[g].at[0, row, :, rest(g)], rz2[g].at[w]
        return remote(src, dst, zs.at[g, path, k], zr.at[g, path, w], (d, row, n))

    def zgot(g, path, row):
        ref = (rz1, rz2)[path][g].at[row]
        return remote(ref, ref, zs.at[g, path, 0], zr.at[g, path, row], line_x)

    x1 = [
        remote(fin[g].at[:, half(g, True)], fin[g].at[:, half(g, True)], fs.at[g, 0], fr.at[g, 0], line_x)
        for g in range(4)
    ]
    x1_got = [
        remote(fin[g].at[:, half(g, False)], fin[g].at[:, half(g, False)], fs.at[g, 0], fr.at[g, 0], line_x)
        for g in range(4)
    ]
    x2 = [remote(fin[g].at[:, rest(g)], rf[g], fs.at[g, 1], fr.at[g, 1], line_x) for g in range(4)]

    lins = [
        pltpu.make_async_copy(geo, tmp_en, lin.at[0]),
    ]
    for copy in lins:
        copy.start()
    sg[...] = jnp.zeros((8, D), f32)
    sg[1:2, :] = gcross[...]
    sg[2:3, :] = gfeed[...]
    st[...] = tg[...]

    def core_step(g):
        for i in range(2):
            loads[g][i].wait()
            core[g][i].wait_recv()

        def add(k):
            for i in range(2):
                for j in range(parts):
                    r = rows(j)
                    acc[g][i, k, r, :] = (acc[g][i, k, r, :].astype(f32) + rc[g][i, k, r, :].astype(f32)).astype(bf16)

        loop(0, wide, add)
        xcopy[g].start()
        y2[g].start()

    def x_step(g):
        xcopy[g].wait_recv()
        c = half(g, True)

        def add(k):
            for i in range(2):
                for j in range(parts):
                    r = rows(j)
                    acc[g][i, k, r, c] = (acc[g][i, k, r, c].astype(f32) + rx[g][i, k, r, :].astype(f32)).astype(bf16)

        loop(0, wide, add)
        y1[g].start()

    def y_step(g, path):
        (y1, y2)[path][g].wait_recv()
        c = half(g, True) if path == 0 else rest(g)
        ry = (ry1, ry2)[path][g]

        def add(k):
            for j in range(parts):
                r = rows(j)
                acc[g][0, k, r, c] = (acc[g][0, k, r, c].astype(f32) + ry[k, r, :].astype(f32)).astype(bf16)

        loop(0, wide, add)
        loop(1, wide, lambda k: zcopy(g, path, k).start())

    def z_step(g, path):
        loop(1, wide, lambda k: zgot(g, path, lax.rem(w + k, wide)).wait_recv())
        c = half(g, True) if path == 0 else rest(g)
        rz = (rz1, rz2)[path][g]
        for j in range(parts):
            r = rows(j)

            def add(k, total):
                return total + rz[lax.rem(w + k, wide), r, :].astype(f32)

            total = lax.fori_loop(1, wide, add, acc[g][0, w, r, c].astype(f32))
            fin[g][r, c] = total.astype(bf16)
        (x1, x2)[path][g].start()

    def last_step(g):
        x1_got[g].wait_recv()
        x2[g].wait_recv()
        for j in range(parts):
            r = rows(j)
            final[g][r, 0 : SHARE[g]] = fin[g][r, 0 : SHARE[g]].astype(f32)
            final[g][r, SHARE[g] :] = fin[g][r, SHARE[g] :].astype(f32) + rf[g][r, :].astype(f32)

    cross[0].wait_recv()
    own = (n, dn)
    for i in range(2):

        def back(r, i=i):
            x = xf[own[i], r, :].astype(f32)
            dx, gg = norm_back(x, gain[...], gxo[i, r, :] + rgx[i, r, :].astype(f32))
            total = d1[i, r, :] + dx
            sg[0:1, :] += gg
            if i == 0:
                rows_f[r, :] = total
            else:
                tmp_in[r, :] = total.astype(bf16)

        rows_loop(256, 64, back)
    in_local = pltpu.make_async_copy(rows_f, gin_o.at[y], os.at[1])
    in_local.start()
    in_send = remote(tmp_in, back_in, ms.at[3], mr.at[3], diag)
    in_send.start()
    cross[1].wait_recv()
    lins[0].wait()
    tmp_en[0] = tmp_en[0] + rge[0].astype(f32)
    en_bf = back_en.at[0]
    back_en[0] = (tmp_en[1] + rge[1].astype(f32)).astype(bf16)
    en_local = pltpu.make_async_copy(tmp_en.at[0], gen_o.at[y], os.at[2])
    en_local.start()
    en_send = remote(en_bf, back_en.at[1], ms.at[4], mr.at[4], diag)
    en_send.start()

    for g in range(4):
        core_step(g)

    for j, dev in enumerate((pair, line_y, line_x)):
        a = remote(sg, rsg.at[j], ss.at[0, j], sr.at[0, j], dev)
        b = remote(st, rst.at[j], ss.at[1, j], sr.at[1, j], dev)
        a.start()
        b.start()
        a.wait()
        b.wait()
        sg[...] += rsg[j]
        st[...] += rst[j]

    def small(k):
        dev = (d, lax.rem(w + k, wide), n)
        return (
            remote(sg, rsgz.at[w], ss.at[0, 3 + k], sr.at[0, 3 + w], dev),
            remote(st, rstz.at[w], ss.at[1, 3 + k], sr.at[1, 3 + w], dev),
        )

    def small_start(k):
        for copy in small(k):
            copy.start()

    loop(1, wide, small_start)
    rsgz[w] = sg[...]
    rstz[w] = st[...]

    for g in range(4):
        x_step(g)
        y_step(g, 1)
    for g in range(4):
        y_step(g, 0)
        z_step(g, 1)

    def small_wait(k):
        row = lax.rem(w + k, wide)
        for i, ref in enumerate((rsgz, rstz)):
            remote(ref.at[row], ref.at[row], ss.at[i, 3], sr.at[i, 3 + row], line_x).wait_recv()

    loop(1, wide, small_wait)
    sg_o[...] = lax.fori_loop(1, wide, lambda k, t: t + rsgz[k], rsgz[0])
    st_o[...] = lax.fori_loop(1, wide, lambda k, t: t + rstz[k], rstz[0])

    in_send.wait_recv()
    in_local.wait()

    def widen(r):
        rows_f[r, :] = back_in[r, :].astype(f32)

    rows_loop(256, 64, widen)
    in_last = pltpu.make_async_copy(rows_f, gin_o.at[1 - y], os.at[3])
    in_last.start()
    en_send.wait_recv()
    tmp_en[1] = back_en[1].astype(f32)
    en_last = pltpu.make_async_copy(tmp_en.at[1], gen_o.at[1 - y], os.at[4])
    en_last.start()
    out_got.wait_recv()
    for g in range(4):
        z_step(g, 0)
    for g in range(4):
        last_step(g)

    for copy in (out_local, en_local, in_last, en_last):
        copy.wait()
    for copy in (*cross, in_send, en_send):
        copy.wait_send()
    for g in range(4):
        for copy in (*core[g], xcopy[g], y1[g], y2[g], x1[g], x2[g]):
            copy.wait_send()

    def finish(k):
        for g in range(4):
            for path in range(2):
                zcopy(g, path, k).wait_send()
        for copy in small(k):
            copy.wait_send()

    loop(1, wide, finish)


def reduce_all(wide, ff, cr, se, outp, gxo, gxp, geo, gep, xf, d1, gain, gfeed, gcross, tg):
    rl = D // wide
    ff, cr, se = (g.reshape(4, wide, rl, g.shape[-1]) for g in (ff, cr, se))
    sem = pltpu.SemaphoreType.DMA
    V = pl.BlockSpec(memory_space=pltpu.VMEM)
    each = lambda shape: [pltpu.VMEM(shape(SHARE[g] // 2, D - SHARE[g]), bf16) for g in range(4)]
    return pl.pallas_call(
        partial(reduce_kernel, wide, rl),
        in_specs=[ANY, ANY, ANY, ANY, V, ANY, ANY, ANY, V, V, V, V, V, V],
        out_specs=[ANY, ANY, ANY, V, V, V, V, V, V],
        out_shape=[
            out((2, 256, D), bf16),
            out((2, 256, D), f32),
            out((2, 128, D), f32),
            out((8, D), f32),
            out((32, 128), f32),
        ]
        + [out((rl, D), f32)] * 4,
        scratch_shapes=[
            *each(lambda a, b: (2, wide, rl, D)),
            *each(lambda a, b: (2, wide, rl, D)),
            *each(lambda a, b: (2, wide, rl, a)),
            *each(lambda a, b: (wide, rl, a)),
            *each(lambda a, b: (wide, rl, b)),
            *each(lambda a, b: (wide, rl, a)),
            *each(lambda a, b: (wide, rl, b)),
            *each(lambda a, b: (rl, D)),
            *each(lambda a, b: (rl, b)),
            pltpu.VMEM((2, 256, D), bf16),
            pltpu.VMEM((2, 128, D), bf16),
            pltpu.VMEM((256, D), bf16),
            pltpu.VMEM((2, 128, D), f32),
            pltpu.VMEM((256, D), bf16),
            pltpu.VMEM((2, 128, D), bf16),
            pltpu.VMEM((256, D), f32),
            pltpu.VMEM((8, D), f32),
            pltpu.VMEM((32, 128), f32),
            pltpu.VMEM((3, 8, D), f32),
            pltpu.VMEM((3, 32, 128), f32),
            pltpu.VMEM((wide, 8, D), f32),
            pltpu.VMEM((wide, 32, 128), f32),
            sem((4, 2)),
            sem((1,)),
            sem((4, 2)),
            sem((4, 2)),
            sem((4,)),
            sem((4,)),
            sem((4, 2)),
            sem((4, 2)),
            sem((4, 2, wide)),
            sem((4, 2, wide)),
            sem((4, 2)),
            sem((4, 2)),
            sem((5,)),
            sem((5,)),
            sem((2, 3 + wide)),
            sem((2, 3 + wide)),
            sem((5,)),
        ],
        compiler_params=pltpu.CompilerParams(
            collective_id=1, has_side_effects=True, vmem_limit_bytes=VMEM_LIMIT
        ),
        name="reduce_all",
    )(ff, cr, se, outp, gxo, gxp, geo, gep, xf, d1, gain, gfeed, gcross, tg)


def on_device(
    wide, hidden_in, encoder_out, cotangent, piece_starts, valid_lengths, bucket_table,
    gain_self, gain_cross, gain_feed, relative_bias, *mats
):
    me = lax.axis_index("narrow")
    micro = me // 2
    sq, sk, sv, so, cq, ck, cv, co, gate, up, down = mats
    ps = jnp.concatenate((sq, so, sk, sv), axis=1)
    pc = jnp.concatenate((cq, co, ck, cv), axis=1)
    pf = jnp.concatenate((gate, up, down), axis=1)
    tab = jnp.pad(relative_bias.T, ((0, 29), (0, 96)))
    xf, ef, cf, tabs, ws, wc, wf = gather(
        wide, hidden_in[:, 0], encoder_out[:, 0], cotangent[:, 0], tab, ps, pc, pf
    )
    ws, wc, wf = (g.reshape(4, D, g.shape[-1]) for g in (ws, wc, wf))
    xs, es, cs = xf.reshape(LEN, D), ef.reshape(ENC, D), cf.reshape(512, D)
    table = tabs[:, :3, :32].reshape(12, 32)
    one_hot = (bucket_table[:, None] == jnp.arange(BUCKETS)[None, :]).astype(f32)
    off = lax.dot_general(table, one_hot, (((1,), (1,)), ((), ())), precision=precise)
    off = jnp.pad(off, ((0, 0), (0, 1))).reshape(4, 3, 2048)
    info = jnp.stack([piece_starts[micro, 0], valid_lengths[micro, 0]])
    gains = [g.reshape(1, D) for g in (gain_self, gain_cross, gain_feed)]

    q, kv, at, p, h1 = self_forward(info, xs, ws, off, gains[0])
    cq, ckv, cat, cp, h2 = cross_forward(h1, es, wc, gains[1])
    gff, outp, d2, gg_feed = feed(h2, cs, wf, gains[2])
    gcr, d1, gg_cross, geo, gep = cross_backward(h1, es, d2, wc, gains[1], cq, ckv, cat, cp)
    gse, gxo, gxp, dl = self_backward(xs, d1, ws, gains[0], q, kv, at, p)

    doff = dl.reshape(12, TILES, 256)
    doff = jnp.pad(doff[:, :, :128], ((0, 0), (0, 1), (0, 0))) + jnp.pad(doff[:, :, 128:], ((0, 0), (1, 0), (0, 0)))
    doff = doff.reshape(12, (TILES + 1) * 128)
    tg = lax.dot_general(one_hot[: (TILES + 1) * 128], doff, (((0,), (1,)), ((), ())), precision=precise)
    tg = jnp.pad(tg, ((0, 0), (0, 116)))
    two = lambda a: a.reshape(2, -1, D)
    outs, gin, gen, sg, st, f0, f1, b, a = reduce_all(
        wide, gff, gcr, gse, two(outp), two(gxo), two(gxp), two(geo), two(gep), xf, two(d1), gains[0], gg_feed, gg_cross, tg
    )
    tg = lax.dynamic_slice_in_dim(st, me * 3, 3, axis=1)
    return (
        outs[:, None], gin[:, None], gen[:, None],
        sg[0], sg[1], sg[2], tg,
        a[:, :192], a[:, 384:576], a[:, 576:], a[:, 192:384],
        b[:, :192], b[:, 384:576], b[:, 576:], b[:, 192:384],
        f0[:, :512], jnp.concatenate([f0[:, 512:], f1[:, :256]], axis=1), f1[:, 256:],
    )


def solution(mesh):
    rows = P(None, ("dp", "wide"), "narrow", None)
    mat = P("wide", "narrow")
    return jax.shard_map(
        partial(on_device, mesh.shape["wide"]),
        mesh=mesh,
        in_specs=(rows, rows, rows, P(None, ("dp", "wide")), P(None, ("dp", "wide")), P(), P(), P(), P(), P(None, "narrow"))
        + (mat,) * 11,
        out_specs=(rows, rows, rows, P(), P(), P(), P(None, "narrow")) + (mat,) * 11,
        check_vma=False,
    )
```

time: 2840 us -> 543 us (0.19); the launches traced: 2790 us -> 542 us
  local copies, waits for them, and re-layouts: 1420 us -> 17.9 us
  waiting for transfers between devices: 736 us -> 0 us
  Pallas kernels: 0 us -> 515 us
  blocking collectives: 258 us -> 0 us
  matrix products: 239 us -> 1.4 us
  other arithmetic: 115 us -> 7.26 us
    unnamed x520 -> x32, local copies, waits for them, and re-layouts: 1140 us -> 4.18 us
    reduce_scatter x30 -> x0, waiting for transfers between devices: 684 us -> none  [the longest x16 353 us: reduce_grads(): lax.psum_scatter(shortened(local_grads), 'wide', scatter_dimension=0, til...]
    pallas_call x0 -> x7, Pallas kernels: none -> 515 us  [the longest x1 168 us: reduce_all(): pl.pallas_call(partial(reduce_kernel, wide, rl), in_specs=[ANY, ANY, ANY,...]
    dot_general x116 -> x2, matrix products: 239 us -> 1.4 us  [the longest x1 0.92 us: on_device(): lax.dot_general(table, one_hot, (((1,), (1,)), ((), ())), precision=precise)]
    all_gather x13 -> x0, blocking collectives: 200 us -> none  [the longest x11 179 us: gather_weights(): lax.all_gather(shortened(matrices), 'wide', axis=0, tiled=True)]
    slice x7 -> x9, local copies, waits for them, and re-layouts: 115 us -> 7.73 us  [the longest x1 1.48 us: on_device(): sg[2]]
    rev x1 -> x0, local copies, waits for them, and re-layouts: 96.1 us -> none  [bias_grad_block(): flipped = grad_scores[:, ::-1, :]]
    psum x2 -> x0, blocking collectives: 58.4 us -> none  [the longest x1 37.1 us: on_device(): lax.psum((gain_self_acc, gain_cross_acc, gain_feed_acc), ('dp', 'wide', '...]
  transfers between devices with their start and end apart: 49 -> 0, of which waited for: 30 -> 0; matrix products, arithmetic and copies ran while one was open for 60% -> 0% of each run, Pallas kernels for 0% -> 0%
where the time goes in v1:
time: 543 us; the launch traced here: 542 us
  Pallas kernels  515 us (95%)
  local copies, waits for them, and re-layouts  17.9 us (3%)
  other arithmetic  7.26 us (1%)
    pallas_call x1, Pallas kernels, reduce_all(): pl.pallas_call(partial(reduce_kernel, wide, rl), in_specs=[ANY, ANY, ANY,...  168 us
    pallas_call x1, Pallas kernels, gather(): pl.pallas_call(partial(gather_kernel, wide), in_specs=[ANY] * 7, out_spec...  115 us
    pallas_call x1, Pallas kernels, self_backward(): pl.pallas_call(self_backward_kernel, grid=(4,), in_specs=[whole((LEN, D))...  69 us
    pallas_call x1, Pallas kernels, self_forward(): pl.pallas_call(self_forward_kernel, grid=(4,), in_specs=[SMEM, whole((LEN...  63.1 us
    pallas_call x1, Pallas kernels, cross_backward(): pl.pallas_call(cross_backward_kernel, grid=(4,), in_specs=[whole((512, D)...  36.7 us
    pallas_call x1, Pallas kernels, cross_forward(): pl.pallas_call(cross_forward_kernel, grid=(4,), in_specs=[whole((512, D))...  34.2 us
    pallas_call x1, Pallas kernels, feed(): pl.pallas_call(feed_kernel, grid=(4,), in_specs=[whole((512, D)), whole((...  28.2 us

profile of v1, /device:TPU:0, one launch (start us, length us, event | category | flops | bytes accessed | tf_op | source)
XLA Modules:
  0.0 542.0 jit_solution(18309397046561873935)
XLA Ops:
  0.7 0.0 copy-start.12
  0.7 1.3 constant_dynamic-slice_fusion.1
  1.9 1.9 pad_add_fusion.1.info
  3.8 2.3 pad_maximum_fusion.2
  6.1 2.0 pad_maximum_fusion.pf
  8.1 0.0 copy-done.12
  8.1 0.6 pad.20.tab
  8.7 115.1 %gather.1 = (bf16[4,256,768]{2,1,0:T(8,128)(2,1)}, bf16[4,128,768]{2,1,0:T(8,128)(2,1)}, bf16[2,256,768]{2,1,0:T(8,128)(2,1)}, f32[4,32,128]{2,1,0:T(8,128)}, bf...) custom-call(bf16[2,256,768]{2,1,0:T(8,128)(2,1)} %bitcast.48, ...), custom_call_target="tpu_custom_call" | custom-call | tf_op jit(solution)/shard_map/gather/pallas_call | solution.py:727
  123.8 0.7 slice.57
  124.5 0.0 copy-done.8
  124.5 0.9 fusion.1
  125.4 0.7 reshape.106.off
  126.1 0.0 copy-done.9
  126.1 0.6 reshape.107.gain
  126.7 63.1 %self_forward.1 = (bf16[4,512,192]{2,1,0:T(8,128)(2,1)}, bf16[4,384,1024]{2,1,0:T(8,128)(2,1)}, bf16[4,512,192]{2,1,0:T(8,128)(2,1)}, bf16[4,3,512,1024]{3,2,1,0:T(8,128)(2,1)}, f32[512,768]{1,0:T(8,128)}) custom-call(s32[2]{0:T(128)} %pad_add_fusion.1.info, bf16[1024,768]{1,0:T(8,128)(2,1)} %bitcast.39, bf16[4,768,768]{2,1,0:T(8,128)(2,1)} %bitcast.56, ...), custom_call_target="tpu_custom_call" | custom-call | flops 20000000000 | bytes 20971520 | tf_op jit(solution)/shard_map/self_forward/pallas_call | solution.py:160
  189.8 0.0 copy-done.10
  189.8 0.6 reshape.110.gain
  190.4 34.2 %cross_forward.1 = (bf16[4,512,192]{2,1,0:T(8,128)(2,1)}, bf16[4,384,512]{2,1,0:T(8,128)(2,1)}, bf16[4,512,192]{2,1,0:T(8,128)(2,1)}, bf16[4,3,512,512]{3,2,1,0:T(8,128)(2,1)}, f32[512,768]{1,0:T(8,128)}) custom-call(f32[512,768]{1,0:T(8,128)} %get-tuple-element.60.h1, bf16[512,768]{1,0:T(8,128)(2,1)} %bitcast.60, bf16[4,768,768]{2,1,0:T(8,128)(2,1)} %bitcast.58, ...), custom_call_target="tpu_custom_call" | custom-call | flops 10000000000 | bytes 20971520 | tf_op jit(solution)/shard_map/cross_forward/pallas_call | solution.py:212
  224.6 0.0 copy-done.11
  224.6 0.6 reshape.113.gain
  225.2 28.2 %feed.1 = (bf16[4,768,1536]{2,1,0:T(8,128)(2,1)}, bf16[512,768]{1,0:T(8,128)(2,1)}, f32[512,768]{1,0:T(8,128)}, f32[1,768]{1,0:T(1,128)}) custom-call(f32[512,768]{1,0:T(8,128)} %get-tuple-element.63.h2, bf16[512,768]{1,0:T(8,128)(2,1)} %bitcast.62, bf16[4,768,1536]{2,1,0:T(8,128)(2,1)} %bitcast.55, f32[1,768]{1,0:T(1,128)} %reshape.113.gain), custom_call_target="tpu_custom_call" | custom-call | flops 30000001024 | bytes 20971520 | tf_op jit(solution)/shard_map/feed/pallas_call | solution.py:286
  253.4 36.7 %cross_backward.1 = (bf16[4,768,768]{2,1,0:T(8,128)(2,1)}, f32[512,768]{1,0:T(8,128)}, f32[1,768]{1,0:T(1,128)}, f32[256,768]{1,0:T(8,128)}, bf16[256,768]{1,0:T(8,128)(2,1)}) custom-call(f32[512,768]{1,0:T(8,128)} %get-tuple-element.60.h1, bf16[512,768]{1,0:T(8,128)(2,1)} %bitcast.61, f32[512,768]{1,0:T(8,128)} %get-tuple-element.67.d2, ...), custom_call_target="tpu_custom_call" | custom-call | flops 14000000000 | bytes 20971520 | tf_op jit(solution)/shard_map/cross_backward/pallas_call | solution.py:365
  290.1 69.0 %self_backward.1 = (bf16[4,768,768]{2,1,0:T(8,128)(2,1)}, f32[512,768]{1,0:T(8,128)}, bf16[512,768]{1,0:T(8,128)(2,1)}, f32[4,33,256]{2,1,0:T(8,128)}) custom-call(bf16[1024,768]{1,0:T(8,128)(2,1)} %bitcast.40, f32[512,768]{1,0:T(8,128)} %get-tuple-element.73.d1, bf16[4,768,768]{2,1,0:T(8,128)(2,1)} %bitcast.57, f32[1,768]{1,0:T(1,128)} %reshape.107.gain, ...), custom_call_target="tpu_custom_call" | custom-call | flops 24999999488 | bytes 20971520 | tf_op jit(solution)/shard_map/self_backward/pallas_call | solution.py:473
  359.1 0.9 reshape.123
  360.1 0.3 iota_compare_fusion
  360.5 0.5 fusion
  360.9 0.6 pad.24.tg
  361.6 168.4 %reduce_all.1 = (bf16[2,256,768]{2,1,0:T(8,128)(2,1)}, f32[2,256,768]{2,1,0:T(8,128)}, f32[2,128,768]{2,1,0:T(8,128)}, f32[8,768]{1,0:T(8,128)}, f32[32,128]{1,0...) custom-call(bf16[4,4,192,1536]{3,2,1,0:T(8,128)(2,1)} %bitcast.35, ...), custom_call_target="tpu_custom_call" | custom-call | tf_op jit(solution)/shard_map/reduce_all/pallas_call | solution.py:1039
  530.0 0.0 copy-start.2
  530.0 0.0 copy-start.1
  530.0 1.0 slice.73
  531.1 0.9 slice.74
  532.0 0.8 pad_maximum_fusion.1
  532.8 0.0 copy-done.2
  532.8 1.0 fusion.3
  533.8 0.0 copy-done.1
  533.8 0.0 copy-start.4
  533.8 1.0 fusion.2
  534.8 0.0 copy-done.6
  534.8 0.8 slice.72
  535.6 0.8 slice.75
  536.4 0.1 constant_dynamic-slice_fusion
  536.5 0.7 copy.48
  537.1 1.5 slice_reduce_fusion
  538.6 0.9 copy.54
  539.5 1.1 copy.55
  540.6 0.5 copy-done.3
  541.2 0.9 copy.56
  (19 shorter events, 0.1 us)
Async XLA Ops:
  0.7 7.4 %copy-start.12 = (f32[32,3]{0,1:T(4,128)S(1)}, f32[32,3]{0,1:T(4,128)}, u32[]{:S(2)}) copy-start(f32[32,3]{0,1:T(4,128)} %param.30) | copy-start | bytes 1156
  8.7 115.8 %copy-start.8 = (s32[2047]{0:T(1024)S(1)}, s32[2047]{0:T(1024)}, u32[]{:S(2)}) copy-start(s32[2047]{0:T(1024)} %param.26) | copy-start | bytes 24568
  8.7 117.5 %copy-start.9 = (f32[768]{0:T(1024)S(1)}, f32[768]{0:T(1024)}, u32[]{:S(2)}) copy-start(f32[768]{0:T(1024)} %param.27) | copy-start | bytes 9220
  126.7 63.1 %copy-start.10 = (f32[768]{0:T(1024)S(1)}, f32[768]{0:T(1024)}, u32[]{:S(2)}) copy-start(f32[768]{0:T(1024)} %param.28) | copy-start | bytes 9220
  190.4 34.2 %copy-start.11 = (f32[768]{0:T(1024)S(1)}, f32[768]{0:T(1024)}, u32[]{:S(2)}) copy-start(f32[768]{0:T(1024)} %param.29) | copy-start | bytes 9220
  530.0 2.8 copy-start.2
  530.0 3.8 copy-start.1
  532.8 2.0 copy-start.6
  533.8 1.8 copy-start.5
  533.8 2.6 copy-start.7
  533.8 4.8 copy-start.4
  534.8 4.7 copy-start
  539.5 1.7 copy-start.3

commit v2 on v1

v2 whole, which is shorter than its diff:
```python
from functools import partial

import jax
import jax.numpy as jnp
from jax import lax
from jax.experimental import pallas as pl
from jax.experimental.pallas import tpu as pltpu
from jax.sharding import PartitionSpec as P

D = 768
HD = 192
HEADS = 12
DHEAD = 64
FFB = 512
BUCKETS = 32
LEN = 1024
ENC = 512
PIC = 256
TILES = 11
SPAN = 1280
ROWS = 16

precise = lax.Precision.HIGHEST
epsilon = 1e-06
masked_value = -1e30
f32 = jnp.float32
bf16 = jnp.bfloat16
MESH = pl.DeviceIdType.MESH
ANY = pl.BlockSpec(memory_space=pl.ANY)
VMEM_LIMIT = 60 << 20


def nn(a, b):
    return lax.dot_general(a, b, (((1,), (0,)), ((), ())), preferred_element_type=f32)


def nt(a, b):
    return lax.dot_general(a, b, (((1,), (1,)), ((), ())), preferred_element_type=f32)


def tn(a, b):
    return lax.dot_general(a, b, (((0,), (0,)), ((), ())), preferred_element_type=f32)


def rows_loop(total, step, body, unroll=1):
    def run(i, carry):
        body(pl.ds(pl.multiple_of(i * step, step), step))
        return carry

    lax.fori_loop(0, total // step, run, 0, unroll=unroll)


def normed(x, gain):
    factor = lax.rsqrt(jnp.mean(x * x, axis=1, keepdims=True) + epsilon)
    return x * factor * gain


def norm_back(x, gain, upstream):
    factor = lax.rsqrt(jnp.mean(x * x, axis=1, keepdims=True) + epsilon)
    weighted = upstream * gain
    inner = jnp.sum(weighted * x, axis=1, keepdims=True)
    dx = weighted * factor - x * (factor * factor * factor * inner * (1.0 / D))
    return dx, jnp.sum(upstream * x * factor, axis=0, keepdims=True)


def own_blocks():
    me = lax.axis_index("narrow")
    return (me, 3 - me)


def block_rows(blk):
    return pl.ds(pl.multiple_of(blk * 256, 256), 256)


def softmax_rows(v):
    e = jnp.exp(v - jnp.max(v, axis=1, keepdims=True))
    return e * (1.0 / jnp.sum(e, axis=1, keepdims=True))


def place_here():
    d, w, n = lax.axis_index("dp"), lax.axis_index("wide"), lax.axis_index("narrow")
    return d, w, n, n + 1 - 2 * lax.rem(n, 2), lax.rem(n + 2, 4), 3 - n


def remote(src, dst, send, recv, dev):
    return pltpu.make_async_remote_copy(
        src_ref=src, dst_ref=dst, send_sem=send, recv_sem=recv, device_id=dev, device_id_type=MESH
    )


def greet(devs, wide=1):
    d, w, n = place_here()[:3]
    barrier = pltpu.get_barrier_semaphore()
    for dev in devs:
        pl.semaphore_signal(barrier, inc=1, device_id=dev, device_id_type=MESH)

    def line(k, carry):
        dev = (d, lax.rem(w + k, wide), n)
        pl.semaphore_signal(barrier, inc=1, device_id=dev, device_id_type=MESH)
        return carry

    lax.fori_loop(1, wide, line, 0)
    pl.semaphore_wait(barrier, wide - 1 + len(devs))


def loop(lo, hi, body):
    def run(k, carry):
        body(k)
        return carry

    lax.fori_loop(lo, hi, run, 0)


def add_into(dst, src):
    shape = dst.shape
    rl = shape[-2]
    step = 64 if rl % 64 == 0 else rl
    lead = shape[:-2]

    def one(*index):
        for j in range(rl // step):
            spot = index + (slice(j * step, (j + 1) * step), slice(None))
            dst[spot] = dst[spot] + src[spot]

    if len(lead) == 1:
        loop(0, lead[0], one)
    else:
        for i in range(lead[0]):
            loop(0, lead[1], partial(one, i))


def sum_line(wide, own, parts, store):
    w = lax.axis_index("wide")
    rl = own.shape[0]
    step = 64 if rl % 64 == 0 else rl
    for j in range(rl // step):
        r = slice(j * step, (j + 1) * step)

        def add(k, total, r=r):
            return total + parts[lax.rem(w + k, wide), r, :].astype(f32)

        store(r, lax.fori_loop(1, wide, add, own[r, :].astype(f32)))


def core_devs():
    d, w, n, pn, yn, dn = place_here()
    return (d, w, pn)


class CoreSum:
    def __init__(self, step, buf, landed, send, recv):
        self.step, self.buf, self.landed, self.send, self.recv = step, buf, landed, send, recv
        self.side = step // 2

    def copy(self):
        return remote(
            self.buf.at[0], self.landed.at[self.side], self.send.at[0], self.recv.at[self.side], core_devs()
        )

    def finish(self, result):
        @pl.when(lax.rem(self.step, 2) == 0)
        def _():
            self.copy().start()

        @pl.when(lax.rem(self.step, 2) == 1)
        def _():
            self.copy().wait_recv()

            def add(r):
                result[0, r, :] = self.buf[1, r, :] + self.landed[self.side, r, :]

            rows_loop(D, 64, add)
            self.copy().wait_send()


def self_forward_kernel(
    info, xf, w, off, gain, q_o, kv_o, at_o, p_o, h1_o, nf, mask, tb, s
):
    n = pl.program_id(0)
    blks = own_blocks()

    @pl.when(n == 0)
    def _():
        def norm_rows(r):
            nf[r, :] = normed(xf[r, :].astype(f32), gain[...]).astype(bf16)

        rows_loop(LEN, 64, norm_rows)
        start, length = info[0], info[1]
        for i in range(2):
            h1_o[i * 256 : (i + 1) * 256, :] = xf[block_rows(blks[i]), :].astype(f32)

            def mask_rows(r, i=i):
                shape = (ROWS, LEN)
                qi = blks[i] * 256 + r.start + lax.broadcasted_iota(jnp.int32, shape, 0)
                kj = lax.broadcasted_iota(jnp.int32, shape, 1)
                inside = (qi >= start) & (qi < start + PIC) & (kj >= start) & (kj < start + PIC)
                allowed = ((kj <= qi) | inside) & (kj < length)
                mask[pl.ds(i * 256 + r.start, ROWS), :] = jnp.where(allowed, 0.0, masked_value)

            rows_loop(256, ROWS, mask_rows)

    kv_o[0] = nn(nf[...], w[0, :, 384:768]).astype(bf16).T
    for i in range(2):
        q_o[0, i * 256 : (i + 1) * 256, :] = nn(nf[block_rows(blks[i]), :], w[0, :, 0:192]).astype(bf16)
    for h in range(3):
        for t in range(TILES):
            line = jnp.broadcast_to(off[0, h : h + 1, 128 * t : 128 * t + 256], (128, 256))
            tb[t] = pltpu.roll(line, 129, 1, stride=1, stride_axis=0)[:, :128]
        hs = slice(h * DHEAD, (h + 1) * DHEAD)
        vs = slice(HD + h * DHEAD, HD + (h + 1) * DHEAD)
        for i in range(2):
            s[...] = nn(q_o[0, i * 256 : (i + 1) * 256, hs], kv_o[0, hs, :])
            for r in range(2):
                idx = [jnp.minimum(kb - 2 * blks[i] - r, 3) + 7 for kb in range(8)]

                def soft_rows(rr, i=i, r=r, h=h, idx=idx):
                    bias = jnp.concatenate([tb[idx[kb], rr, :] for kb in range(8)], axis=1)
                    v = s[pl.ds(r * 128 + rr.start, ROWS), :] + bias
                    v = v + mask[pl.ds(i * 256 + r * 128 + rr.start, ROWS), :]
                    p_o[0, h, pl.ds(i * 256 + r * 128 + rr.start, ROWS), :] = softmax_rows(v).astype(bf16)

                rows_loop(128, ROWS, soft_rows, unroll=8)
            at_o[0, i * 256 : (i + 1) * 256, hs] = nt(
                p_o[0, h, i * 256 : (i + 1) * 256, :], kv_o[0, vs, :]
            ).astype(bf16)
    h1_o[...] += nt(at_o[0], w[0, :, 192:384])


def whole(shape):
    zero = (0,) * len(shape)
    return pl.BlockSpec(shape, lambda n: zero)


def slab(shape):
    zero = (0,) * len(shape)
    return pl.BlockSpec((1,) + shape, lambda n: (n,) + zero)


def pair_slab(shape):
    zero = (0,) * len(shape)
    return pl.BlockSpec((1,) + shape, lambda n: (n // 2,) + zero)


def params(collective_id=None):
    if collective_id is None:
        return pltpu.CompilerParams(dimension_semantics=("arbitrary",), vmem_limit_bytes=VMEM_LIMIT)
    return pltpu.CompilerParams(
        dimension_semantics=("arbitrary",),
        vmem_limit_bytes=VMEM_LIMIT,
        collective_id=collective_id,
        has_side_effects=True,
    )


def out(shape, dtype):
    return jax.ShapeDtypeStruct(shape, dtype)


SMEM = pl.BlockSpec(memory_space=pltpu.SMEM)


def cost(gflop):
    return pl.CostEstimate(flops=int(gflop * 1e9), bytes_accessed=20 << 20, transcendentals=0)


def self_forward(info, xf, w, off, gain):
    return pl.pallas_call(
        self_forward_kernel,
        grid=(4,),
        in_specs=[SMEM, whole((LEN, D)), slab((D, D)), slab((3, 2048)), whole((1, D))],
        out_specs=[slab((512, HD)), slab((2 * HD, LEN)), slab((512, HD)), slab((3, 512, LEN)), whole((512, D))],
        out_shape=[
            out((4, 512, HD), bf16),
            out((4, 2 * HD, LEN), bf16),
            out((4, 512, HD), bf16),
            out((4, 3, 512, LEN), bf16),
            out((512, D), f32),
        ],
        scratch_shapes=[
            pltpu.VMEM((LEN, D), bf16),
            pltpu.VMEM((512, LEN), f32),
            pltpu.VMEM((TILES, 128, 128), f32),
            pltpu.VMEM((256, LEN), f32),
        ],
        compiler_params=params(),
        cost_estimate=cost(20),
        name="self_forward",
    )(info, xf, w, off, gain)


def cross_forward_kernel(h1, ef, w, gain, q_o, kv_o, at_o, p_o, h2_o, nc, s):
    n = pl.program_id(0)

    @pl.when(n == 0)
    def _():
        def norm_rows(r):
            x = h1[r, :]
            nc[r, :] = normed(x, gain[...]).astype(bf16)
            h2_o[r, :] = x

        rows_loop(512, 64, norm_rows)

    kv_o[0] = nn(ef[...], w[0, :, 384:768]).astype(bf16).T
    q_o[0] = nn(nc[...], w[0, :, 0:192]).astype(bf16)
    for h in range(3):
        hs = slice(h * DHEAD, (h + 1) * DHEAD)
        vs = slice(HD + h * DHEAD, HD + (h + 1) * DHEAD)
        s[...] = nn(q_o[0, :, hs], kv_o[0, hs, :])

        def soft_rows(r, h=h):
            p_o[0, h, r, :] = softmax_rows(s[r, :]).astype(bf16)

        rows_loop(512, 16, soft_rows, unroll=32)
        at_o[0, :, hs] = nt(p_o[0, h], kv_o[0, vs, :]).astype(bf16)
    h2_o[...] += nt(at_o[0], w[0, :, 192:384])


def cross_forward(h1, ef, w, gain):
    return pl.pallas_call(
        cross_forward_kernel,
        grid=(4,),
        in_specs=[whole((512, D)), whole((ENC, D)), slab((D, D)), whole((1, D))],
        out_specs=[slab((512, HD)), slab((2 * HD, ENC)), slab((512, HD)), slab((3, 512, ENC)), whole((512, D))],
        out_shape=[
            out((4, 512, HD), bf16),
            out((4, 2 * HD, ENC), bf16),
            out((4, 512, HD), bf16),
            out((4, 3, 512, ENC), bf16),
            out((512, D), f32),
        ],
        scratch_shapes=[pltpu.VMEM((512, D), bf16), pltpu.VMEM((512, ENC), f32)],
        compiler_params=params(),
        cost_estimate=cost(10),
        name="cross_forward",
    )(h1, ef, w, gain)


GELU_A = 0.7978845608028654
GELU_B = 0.044715


def feed_kernel(
    h2, cf, w, gain, gw_o, out_o, d2_o, gg_o, nf, nft, ct, gu, da, act, dgu, acc, buf, landed, send, recv
):
    n = pl.program_id(0)
    slot = lax.rem(n, 2)
    core = CoreSum(n, buf, landed, send, recv)

    @pl.when(n == 0)
    def _():
        def norm_rows(r):
            x = h2[r, :]
            nf[r, :] = normed(x, gain[...]).astype(bf16)
            acc[r, :] = x
            d2_o[r, :] = jnp.zeros((64, D), f32)

        greet((core_devs(),))
        rows_loop(512, 64, norm_rows)
        nft[...] = nf[...].T
        ct[...] = cf[...].T

    gu[...] = nn(nf[...], w[0, :, : 2 * FFB])
    da[...] = nn(cf[...], w[0, :, 2 * FFB :])

    def gelu_rows(r):
        gate = gu[r, :FFB]
        up = gu[r, FFB:]
        d_act = da[r, :]
        sq = gate * gate
        th = jnp.tanh(GELU_A * gate * (1.0 + GELU_B * sq))
        half = 0.5 + 0.5 * th
        gelu = gate * half
        slope = half + 0.5 * GELU_A * gate * (1.0 - th * th) * (1.0 + 3.0 * GELU_B * sq)
        act[r, :] = (gelu * up).astype(bf16)
        dgu[r, :FFB] = (d_act * up * slope).astype(bf16)
        dgu[r, FFB:] = (d_act * gelu).astype(bf16)

    rows_loop(512, 16, gelu_rows, unroll=32)
    acc[...] += nt(act[...], w[0, :, 2 * FFB :])
    buf[slot, :, : 2 * FFB] = nn(nft[...], dgu[...]).astype(bf16)
    buf[slot, :, 2 * FFB :] = nn(ct[...], act[...]).astype(bf16)
    d2_o[...] += nt(dgu[...], w[0, :, : 2 * FFB])
    core.finish(gw_o)

    @pl.when(n == 3)
    def _():
        gg_o[...] = jnp.zeros((1, D), f32)

        def back_rows(r):
            dx, gg = norm_back(h2[r, :], gain[...], d2_o[r, :])
            d2_o[r, :] = cf[r, :].astype(f32) + dx
            gg_o[...] += gg
            out_o[r, :] = acc[r, :].astype(bf16)

        rows_loop(512, 64, back_rows)


def feed(h2, cf, w, gain):
    return pl.pallas_call(
        feed_kernel,
        grid=(4,),
        in_specs=[whole((512, D)), whole((512, D)), slab((D, 3 * FFB)), whole((1, D))],
        out_specs=[pair_slab((D, 3 * FFB)), whole((512, D)), whole((512, D)), whole((1, D))],
        out_shape=[out((2, D, 3 * FFB), bf16), out((512, D), bf16), out((512, D), f32), out((1, D), f32)],
        scratch_shapes=[
            pltpu.VMEM((512, D), bf16),
            pltpu.VMEM((D, 512), bf16),
            pltpu.VMEM((D, 512), bf16),
            pltpu.VMEM((512, 2 * FFB), f32),
            pltpu.VMEM((512, FFB), f32),
            pltpu.VMEM((512, FFB), bf16),
            pltpu.VMEM((512, 2 * FFB), bf16),
            pltpu.VMEM((512, D), f32),
            pltpu.VMEM((2, D, 3 * FFB), bf16),
            pltpu.VMEM((2, D, 3 * FFB), bf16),
            pltpu.SemaphoreType.DMA((1,)),
            pltpu.SemaphoreType.DMA((2,)),
        ],
        compiler_params=params(2),
        cost_estimate=cost(30),
        name="feed",
    )(h2, cf, w, gain)


def cross_backward_kernel(
    h1, ef, d2, w, gain, q, kv, at, p, gff,
    gw_o, d1_o, gg_o, ge_o, gep_o, o1, o2,
    d2b, d2t, nct, eft, get, do, dp, ds, dq, dkv, buf, landed, rx, ry, send, recv, load, fs, fr,
):
    n = pl.program_id(0)
    slot = lax.rem(n, 2)
    core = CoreSum(n, buf, landed, send, recv)
    d, wi, me, pn, yn, dn = place_here()
    y = me // 2
    mine = pl.ds(pl.multiple_of(d * 384, 128), 384)
    other = pl.ds(pl.multiple_of(384 - d * 384, 128), 384)
    late = pl.ds(D, D)
    loads = [
        pltpu.make_async_copy(gff.at[:, :, :, mine], o1, load.at[0]),
        pltpu.make_async_copy(gff.at[y, :, :, late], o2, load.at[1]),
    ]
    sends = [
        remote(gff.at[:, :, :, other], rx, fs.at[0], fr.at[0], (1 - d, wi, me)),
        remote(gff.at[1 - y, :, :, late], ry, fs.at[1], fr.at[1], (d, wi, yn)),
    ]

    @pl.when(n == 0)
    def _():
        def norm_rows(r):
            d2b[r, :] = d2[r, :].astype(bf16)
            d1_o[r, :] = jnp.zeros((64, D), f32)
            dp[r, :] = normed(h1[r, :], gain[...])

        for copy in loads:
            copy.start()
        greet(((d, wi, pn), (d, wi, yn), (1 - d, wi, me)))
        for copy in sends:
            copy.start()
        rows_loop(512, 64, norm_rows)
        nct[...] = dp[...].astype(bf16).T
        d2t[...] = d2b[...].T
        eft[...] = ef[...].T
        get[...] = jnp.zeros((D, ENC), f32)

    do[...] = nn(d2b[...], w[0, :, 192:384]).astype(bf16)
    for h in range(3):
        hs = slice(h * DHEAD, (h + 1) * DHEAD)
        vs = slice(HD + h * DHEAD, HD + (h + 1) * DHEAD)
        dp[:, :ENC] = nn(do[:, hs], kv[0, vs, :])

        def grad_rows(r, h=h, hs=hs):
            delta = jnp.sum(do[r, hs].astype(f32) * at[0, r, hs].astype(f32), axis=1, keepdims=True)
            ds[r, :] = (p[0, h, r, :].astype(f32) * (dp[r, :ENC] - delta)).astype(bf16)

        rows_loop(512, 16, grad_rows, unroll=32)
        dq[:, hs] = nt(ds[...], kv[0, hs, :]).astype(bf16)
        dkv[hs, :] = tn(q[0, :, hs], ds[...]).astype(bf16)
        dkv[vs, :] = tn(do[:, hs], p[0, h]).astype(bf16)
    d1_o[...] += nt(dq[...], w[0, :, 0:192])
    get[...] += nn(w[0, :, 384:768], dkv[...])
    buf[slot, :, 0:384] = jnp.concatenate([nn(nct[...], dq[...]), nn(d2t[...], at[0])], axis=1).astype(bf16)
    buf[slot, :, 384:768] = nt(eft[...], dkv[...]).astype(bf16)
    core.finish(gw_o)

    @pl.when(n == 3)
    def _():
        gg_o[...] = jnp.zeros((1, D), f32)

        def back_rows(r):
            dx, gg = norm_back(h1[r, :], gain[...], d1_o[r, :])
            d1_o[r, :] = d2[r, :] + dx
            gg_o[...] += gg

        rows_loop(512, 64, back_rows)
        for i in range(2):
            half = slice(i * 128, (i + 1) * 128)
            cols = lambda blk: pl.ds(pl.multiple_of(blk * 128, 128), 128)
            ge_o[half, :] = get[:, cols((me, 3 - me)[i])].T
            gep_o[half, :] = get[:, cols((pn, 3 - pn)[i])].T.astype(bf16)
        for copy in loads:
            copy.wait()
        for copy in sends:
            copy.wait()
        add_into(o1, rx)
        add_into(o2, ry)


def cross_backward(wide, h1, ef, d2, w, gain, q, kv, at, p, gff):
    rl = D // wide
    return pl.pallas_call(
        cross_backward_kernel,
        grid=(4,),
        in_specs=[
            whole((512, D)),
            whole((ENC, D)),
            whole((512, D)),
            slab((D, D)),
            whole((1, D)),
            slab((512, HD)),
            slab((2 * HD, ENC)),
            slab((512, HD)),
            slab((3, 512, ENC)),
            ANY,
        ],
        out_specs=[
            pair_slab((D, D)),
            whole((512, D)),
            whole((1, D)),
            whole((256, D)),
            whole((256, D)),
            whole((2, wide, rl, 384)),
            whole((wide, rl, D)),
        ],
        out_shape=[
            out((2, D, D), bf16),
            out((512, D), f32),
            out((1, D), f32),
            out((256, D), f32),
            out((256, D), bf16),
            out((2, wide, rl, 384), bf16),
            out((wide, rl, D), bf16),
        ],
        scratch_shapes=[
            pltpu.VMEM((512, D), bf16),
            pltpu.VMEM((D, 512), bf16),
            pltpu.VMEM((D, 512), bf16),
            pltpu.VMEM((D, ENC), bf16),
            pltpu.VMEM((D, ENC), f32),
            pltpu.VMEM((512, HD), bf16),
            pltpu.VMEM((512, D), f32),
            pltpu.VMEM((512, ENC), bf16),
            pltpu.VMEM((512, HD), bf16),
            pltpu.VMEM((2 * HD, ENC), bf16),
            pltpu.VMEM((2, D, D), bf16),
            pltpu.VMEM((2, D, D), bf16),
            pltpu.VMEM((2, wide, rl, 384), bf16),
            pltpu.VMEM((wide, rl, D), bf16),
            pltpu.SemaphoreType.DMA((1,)),
            pltpu.SemaphoreType.DMA((2,)),
            pltpu.SemaphoreType.DMA((2,)),
            pltpu.SemaphoreType.DMA((2,)),
            pltpu.SemaphoreType.DMA((2,)),
        ],
        compiler_params=params(3),
        cost_estimate=cost(14),
        name="cross_backward",
    )(h1, ef, d2, w, gain, q, kv, at, p, gff.reshape(2, wide, rl, 3 * FFB))


def self_backward_kernel(
    wide, xf, d1, w, gain, q, kv, at, p, gcr, o1, o2,
    gw_o, g_o, gp_o, dl_o, c1, c2, e1, e2,
    d1b, d1t, nft, nqt, gt, gq, do, dp, ds, dq, dkv, buf, landed, s1, f2, rx, ry, ry1, rz1, rz2,
    send, recv, load, fs, fr, zs, zr,
):
    n = pl.program_id(0)
    blks = own_blocks()
    slot = lax.rem(n, 2)
    core = CoreSum(n, buf, landed, send, recv)
    d, wi, me, pn, yn, dn = place_here()
    y = me // 2
    mine = pl.ds(pl.multiple_of(d * 256, 128), 256)
    other = pl.ds(pl.multiple_of(256 - d * 256, 128), 256)
    late = pl.ds(512, 256)
    loads = [
        pltpu.make_async_copy(gcr.at[:, :, :, mine], c1, load.at[0]),
        pltpu.make_async_copy(gcr.at[y, :, :, late], c2, load.at[1]),
        pltpu.make_async_copy(o1.at[y], s1, load.at[2]),
        pltpu.make_async_copy(o2.at[wi], f2, load.at[3]),
    ]
    sends = [
        remote(o1.at[1 - y], ry1, fs.at[0], fr.at[0], (d, wi, yn)),
        remote(gcr.at[:, :, :, other], rx, fs.at[1], fr.at[1], (1 - d, wi, me)),
        remote(gcr.at[1 - y, :, :, late], ry, fs.at[2], fr.at[2], (d, wi, yn)),
    ]

    def zcopy(path, k):
        row = lax.rem(wi + k, wide)
        src, dst = ((s1, rz1), (o2, rz2))[path]
        return remote(src.at[row], dst.at[wi], zs.at[path, k], zr.at[path, wi], (d, row, me))

    def zgot(path, k):
        row = lax.rem(wi + k, wide)
        ref = (rz1, rz2)[path].at[row]
        return remote(ref, ref, zs.at[path, k], zr.at[path, row], (d, row, me))

    @pl.when(n == 0)
    def _():
        def cast_rows(r):
            d1b[r, :] = d1[r, :].astype(bf16)
            gq[r, :] = jnp.zeros((64, D), f32)

        for copy in loads:
            copy.start()
        greet(((d, wi, pn), (d, wi, yn), (1 - d, wi, me)), wide)
        for copy in sends:
            copy.start()
        loop(1, wide, lambda k: zcopy(1, k).start())
        rows_loop(512, 64, cast_rows)
        d1t[...] = d1b[...].T
        for i in range(4):
            part = normed(xf[i * 256 : (i + 1) * 256, :].astype(f32), gain[...]).astype(bf16)
            nft[:, i * 256 : (i + 1) * 256] = part.T
        for i in range(2):
            part = normed(xf[block_rows(blks[i]), :].astype(f32), gain[...]).astype(bf16)
            nqt[:, i * 256 : (i + 1) * 256] = part.T
        gt[...] = jnp.zeros((D, LEN), f32)

    @pl.when(n == 2)
    def _():
        loads[2].wait()
        sends[0].wait_recv()
        add_into(s1, ry1)
        loop(1, wide, lambda k: zcopy(0, k).start())

    dl_o[0] = jnp.zeros((3, 2048), f32)
    do[...] = nn(d1b[...], w[0, :, 192:384]).astype(bf16)
    for h in range(3):
        hs = slice(h * DHEAD, (h + 1) * DHEAD)
        vs = slice(HD + h * DHEAD, HD + (h + 1) * DHEAD)
        dk = jnp.zeros((DHEAD, LEN), f32)
        dv = jnp.zeros((DHEAD, LEN), f32)
        for i in range(2):
            half = slice(i * 256, (i + 1) * 256)
            dp[...] = nn(do[half, hs], kv[0, vs, :])

            def grad_rows(rr, i=i, h=h, hs=hs):
                rows = pl.ds(i * 256 + rr.start, ROWS)
                delta = jnp.sum(do[rows, hs].astype(f32) * at[0, rows, hs].astype(f32), axis=1, keepdims=True)
                ds[rr, :] = (p[0, h, rows, :].astype(f32) * (dp[rr, :] - delta)).astype(bf16)

            rows_loop(256, ROWS, grad_rows, unroll=16)
            upper, lower = ds[:128, :].astype(f32), ds[128:, :].astype(f32)
            part = jnp.concatenate(
                [
                    upper[:, :896] + lower[:, 128:],
                    upper[:, 896:],
                    jnp.zeros((128, 128), f32),
                    lower[:, :128],
                ],
                axis=1,
            )
            height = 128
            while height > 1:
                height //= 2
                part = part[:height] + pltpu.roll(part[height:], SPAN - height, 1)
            where = pl.ds(pl.multiple_of(768 - 256 * blks[i], 128), SPAN)
            dl_o[0, h : h + 1, where] += pltpu.roll(part, 255, 1)
            dq[half, hs] = nt(ds[...], kv[0, hs, :]).astype(bf16)
            dk = dk + tn(q[0, half, hs], ds[...])
            dv = dv + tn(do[half, hs], p[0, h, half, :])
        dkv[hs, :] = dk.astype(bf16)
        dkv[vs, :] = dv.astype(bf16)
    gq[...] += nt(dq[...], w[0, :, 0:192])
    gt[...] += nn(w[0, :, 384:768], dkv[...])
    buf[slot, :, 0:384] = jnp.concatenate([nn(nqt[...], dq[...]), nn(d1t[...], at[0])], axis=1).astype(bf16)
    buf[slot, :, 384:768] = nt(nft[...], dkv[...]).astype(bf16)
    core.finish(gw_o)

    @pl.when(n == 3)
    def _():
        for i in range(2):
            half = slice(i * 256, (i + 1) * 256)
            g_o[half, :] = gq[half, :] + gt[:, block_rows(blks[i])].T
            gp_o[half, :] = gt[:, block_rows((pn, 3 - pn)[i])].T.astype(bf16)
        loads[0].wait()
        sends[1].wait_recv()
        add_into(c1, rx)
        loads[1].wait()
        sends[2].wait_recv()
        add_into(c2, ry)
        loads[3].wait()
        for path in (1, 0):
            loop(1, wide, lambda k, path=path: zgot(path, k).wait_recv())

        def put(ref):
            def store(r, total):
                ref[r, :] = total.astype(bf16)

            return store

        sum_line(wide, s1.at[wi], rz1, put(e1))
        sum_line(wide, f2, rz2, put(e2))
        for copy in sends:
            copy.wait_send()
        for path in (0, 1):
            loop(1, wide, lambda k, path=path: zcopy(path, k).wait_send())


def self_backward(wide, xf, d1, w, gain, q, kv, at, p, gcr, o1, o2):
    rl = D // wide
    return pl.pallas_call(
        partial(self_backward_kernel, wide),
        grid=(4,),
        in_specs=[
            whole((LEN, D)),
            whole((512, D)),
            slab((D, D)),
            whole((1, D)),
            slab((512, HD)),
            slab((2 * HD, LEN)),
            slab((512, HD)),
            slab((3, 512, LEN)),
            ANY,
            ANY,
            ANY,
        ],
        out_specs=[
            pair_slab((D, D)),
            whole((512, D)),
            whole((512, D)),
            slab((3, 2048)),
            whole((2, wide, rl, 256)),
            whole((wide, rl, 256)),
            whole((rl, 384)),
            whole((rl, D)),
        ],
        out_shape=[
            out((2, D, D), bf16),
            out((512, D), f32),
            out((512, D), bf16),
            out((4, 3, 2048), f32),
            out((2, wide, rl, 256), bf16),
            out((wide, rl, 256), bf16),
            out((rl, 384), bf16),
            out((rl, D), bf16),
        ],
        scratch_shapes=[
            pltpu.VMEM((512, D), bf16),
            pltpu.VMEM((D, 512), bf16),
            pltpu.VMEM((D, LEN), bf16),
            pltpu.VMEM((D, 512), bf16),
            pltpu.VMEM((D, LEN), f32),
            pltpu.VMEM((512, D), f32),
            pltpu.VMEM((512, HD), bf16),
            pltpu.VMEM((256, LEN), f32),
            pltpu.VMEM((256, LEN), bf16),
            pltpu.VMEM((512, HD), bf16),
            pltpu.VMEM((2 * HD, LEN), bf16),
            pltpu.VMEM((2, D, D), bf16),
            pltpu.VMEM((2, D, D), bf16),
            pltpu.VMEM((wide, rl, 384), bf16),
            pltpu.VMEM((rl, D), bf16),
            pltpu.VMEM((2, wide, rl, 256), bf16),
            pltpu.VMEM((wide, rl, 256), bf16),
            pltpu.VMEM((wide, rl, 384), bf16),
            pltpu.VMEM((wide, rl, 384), bf16),
            pltpu.VMEM((wide, rl, D), bf16),
            pltpu.SemaphoreType.DMA((1,)),
            pltpu.SemaphoreType.DMA((2,)),
            pltpu.SemaphoreType.DMA((4,)),
            pltpu.SemaphoreType.DMA((3,)),
            pltpu.SemaphoreType.DMA((3,)),
            pltpu.SemaphoreType.DMA((2, wide)),
            pltpu.SemaphoreType.DMA((2, wide)),
        ],
        compiler_params=params(4),
        cost_estimate=cost(25),
        name="self_backward",
    )(xf, d1, w, gain, q, kv, at, p, gcr.reshape(2, wide, rl, D), o1, o2)


def gather_kernel(
    wide, hid, enc, cot, tab, ps, pc, pf, xf, ef, cf, tabs, gs, gc, gf, ls, ins, inr, zs, zr, ys, yr, xs, xr, cs, cr
):
    d, w, n, pn, yn, dn = place_here()
    y = n // 2
    keep, give = (2 * y + 1, 3 - 2 * y), (2 * y, 2 - 2 * y)
    groups = ((ps, gs, 0, 768, True), (pc, gc, 0, 768, True), (pf, gf, 0, 512, True), (pf, gf, 512, 1024, False))

    def cols(s, which):
        start, width, split = groups[s][2:]
        if which == 2 or not split:
            return pl.ds(start, width)
        half = width // 2
        pos = d if which == 0 else 1 - d
        return pl.ds(pl.multiple_of(start + pos * half, 128), half)

    def own(s, which):
        return groups[s][0].at[:, cols(s, which)]

    def spot(s, slab, row, which):
        return groups[s][1].at[slab, row, :, cols(s, which)]

    def zcopy(s, k):
        return remote(own(s, 0), spot(s, keep[0], w, 0), zs.at[s, k], zr.at[s, w], (d, lax.rem(w + k, wide), n))

    def zgot(s, row):
        return remote(spot(s, keep[0], row, 0), spot(s, keep[0], row, 0), zs.at[s, 0], zr.at[s, row], (1 - d, w, n))

    def ycopy(s, row, src):
        return remote(src, spot(s, keep[0], row, 0), ys.at[s, row], yr.at[s, row], (d, w, yn))

    def ygot(s, row):
        return remote(spot(s, keep[1], row, 0), spot(s, keep[1], row, 0), ys.at[s, row], yr.at[s, row], (d, w, yn))

    def xcopy(s, side, row):
        ref = spot(s, keep[side], row, 0)
        return remote(ref, ref, xs.at[s, side, row], xr.at[s, side, row], (1 - d, w, n))

    def xgot(s, side, row):
        ref = spot(s, keep[side], row, 1)
        return remote(ref, ref, xs.at[s, side, row], xr.at[s, side, row], (1 - d, w, n))

    def ccopy(s, side, row, src=None):
        ref = spot(s, keep[side], row, 2)
        return remote(ref if src is None else src, spot(s, give[side], row, 2), cs.at[s, side, row], cr.at[s, side, row], (d, w, pn))

    def cgot(s, side, row):
        ref = spot(s, give[side], row, 2)
        return remote(ref, ref, cs.at[s, side, row], cr.at[s, side, row], (d, w, pn))

    local = [
        pltpu.make_async_copy(src, dst, ls.at[i])
        for i, (src, dst) in enumerate(
            (
                (ps, gs.at[keep[0], w]),
                (pc, gc.at[keep[0], w]),
                (pf, gf.at[keep[0], w]),
                (hid.at[y], xf.at[n]),
                (enc.at[y], ef.at[n]),
                (cot.at[y], cf.at[0]),
                (tab, tabs.at[keep[0]]),
            )
        )
    ]
    for copy in local:
        copy.start()
    diag, pair = (d, w, dn), (d, w, pn)
    greet((pair, (d, w, yn), diag, (1 - d, w, n)), wide)
    first = [
        remote(hid.at[1 - y], xf.at[n], ins.at[0], inr.at[0], diag),
        remote(enc.at[1 - y], ef.at[n], ins.at[1], inr.at[1], diag),
        remote(cot.at[1 - y], cf.at[1], ins.at[2], inr.at[2], diag),
        remote(tab, tabs.at[give[0]], ins.at[3], inr.at[3], pair),
        remote(tab, tabs.at[keep[0]], ins.at[4], inr.at[4], (d, w, yn)),
        remote(tab, tabs.at[give[0]], ins.at[5], inr.at[5], diag),
        remote(hid.at[y], xf.at[n], ins.at[6], inr.at[6], pair),
        remote(enc.at[y], ef.at[n], ins.at[7], inr.at[7], pair),
    ]
    got = [
        remote(xf.at[dn], xf.at[dn], ins.at[0], inr.at[0], diag),
        remote(ef.at[dn], ef.at[dn], ins.at[1], inr.at[1], diag),
        remote(cf.at[1], cf.at[1], ins.at[2], inr.at[2], diag),
        remote(tabs.at[give[0]], tabs.at[give[0]], ins.at[3], inr.at[3], pair),
        remote(tabs.at[keep[1]], tabs.at[keep[1]], ins.at[4], inr.at[4], (d, w, yn)),
        remote(tabs.at[give[1]], tabs.at[give[1]], ins.at[5], inr.at[5], diag),
        remote(xf.at[pn], xf.at[pn], ins.at[6], inr.at[6], pair),
        remote(ef.at[pn], ef.at[pn], ins.at[7], inr.at[7], pair),
        remote(xf.at[yn], xf.at[yn], ins.at[8], inr.at[8], pair),
        remote(ef.at[yn], ef.at[yn], ins.at[9], inr.at[9], pair),
    ]
    later = [
        remote(xf.at[dn], xf.at[dn], ins.at[8], inr.at[8], pair),
        remote(ef.at[dn], ef.at[dn], ins.at[9], inr.at[9], pair),
    ]
    for copy in first:
        copy.start()
    for s in range(4):
        loop(1, wide, lambda k, s=s: zcopy(s, k).start())
        ycopy(s, w, own(s, 0)).start()
        ccopy(s, 0, w, own(s, 2)).start()
    got[0].wait_recv()
    later[0].start()
    got[1].wait_recv()
    later[1].start()

    def zstep(s):
        def one(k):
            row = lax.rem(w + k, wide)
            zgot(s, row).wait_recv()
            ycopy(s, row, spot(s, keep[0], row, 0)).start()
            if groups[s][4]:
                xcopy(s, 0, row).start()
            else:
                ccopy(s, 0, row).start()

        loop(1, wide, one)

    def ystep(s):
        def one(k):
            row = lax.rem(w + k, wide)
            ygot(s, row).wait_recv()
            if groups[s][4]:
                xcopy(s, 1, row).start()
            else:
                ccopy(s, 1, row).start()

        loop(0, wide, one)

    def xstep(s):
        def one(side):
            def step(k):
                row = lax.rem(w + k, wide)
                xgot(s, side, row).wait_recv()
                ccopy(s, side, row).start()

            return step

        loop(1, wide, one(0))
        loop(0, wide, one(1))

    zstep(0)
    ystep(0)
    zstep(1)
    ystep(1)
    xstep(0)
    zstep(2)
    ystep(2)
    xstep(1)
    zstep(3)
    ystep(3)
    xstep(2)
    for copy in got[2:]:
        copy.wait_recv()
    for copy in local:
        copy.wait()
    for copy in first + later:
        copy.wait_send()

    def finish(k):
        row = lax.rem(w + k, wide)
        for s in range(4):
            for side in range(2):
                cgot(s, side, row).wait_recv()
                ccopy(s, side, row).wait_send()
            ycopy(s, row, spot(s, keep[0], row, 0)).wait_send()
            if groups[s][4]:
                xcopy(s, 1, row).wait_send()

    loop(0, wide, finish)

    def finish_line(k):
        row = lax.rem(w + k, wide)
        for s in range(4):
            zcopy(s, k).wait_send()
            if groups[s][4]:
                xcopy(s, 0, row).wait_send()

    loop(1, wide, finish_line)


def gather(wide, hid, enc, cot, tab, ps, pc, pf):
    rl = ps.shape[0]
    sem = pltpu.SemaphoreType.DMA
    return pl.pallas_call(
        partial(gather_kernel, wide),
        in_specs=[ANY] * 7,
        out_specs=[ANY] * 7,
        out_shape=[
            out((4, 256, D), bf16),
            out((4, 128, D), bf16),
            out((2, 256, D), bf16),
            out((4, 32, 128), f32),
            out((4, wide, rl, D), bf16),
            out((4, wide, rl, D), bf16),
            out((4, wide, rl, 2 * D), bf16),
        ],
        scratch_shapes=[
            sem((7,)),
            sem((10,)),
            sem((10,)),
            sem((4, wide)),
            sem((4, wide)),
            sem((4, wide)),
            sem((4, wide)),
            sem((4, 2, wide)),
            sem((4, 2, wide)),
            sem((4, 2, wide)),
            sem((4, 2, wide)),
        ],
        compiler_params=pltpu.CompilerParams(collective_id=0, has_side_effects=True),
        name="gather",
    )(hid, enc, cot, tab, ps, pc, pf)


def reduce_kernel(
    wide, se, c1, c2, e1, e2, outp, gxo, gxp, geo, gep, xf, d1, gain, gfeed, gcross, tg,
    out_o, gin_o, gen_o, sg_o, st_o, ff_o, cr_o, se_o,
    a1, a2, rx, ry, ry1, cy1, b1, rzs1, rzs2, rzc1, rzc2, fs, fc, xs1, xs2, xc1, xc2, x1, x2,
    rgx, rge, tmp_in, tmp_en, back_in, back_en, rows_f, sg, st, rsg, rst, rsgz, rstz,
    load, ms, mr, ts, tr, zs, zr, ss, sr, os,
):
    d, w, n, pn, yn, dn = place_here()
    y = n // 2
    pair, line_y, diag, line_x = (d, w, pn), (d, w, yn), (d, w, dn), (1 - d, w, n)
    mine = pl.ds(pl.multiple_of(d * 256, 128), 256)
    other = pl.ds(pl.multiple_of(256 - d * 256, 128), 256)
    late = pl.ds(512, 256)
    loads = [
        pltpu.make_async_copy(se.at[:, :, :, mine], a1, load.at[0]),
        pltpu.make_async_copy(se.at[y, :, :, late], a2, load.at[1]),
        pltpu.make_async_copy(c1.at[y], b1, load.at[2]),
        pltpu.make_async_copy(geo, tmp_en, load.at[3]),
        pltpu.make_async_copy(outp.at[0], out_o.at[y], load.at[4]),
    ]
    for copy in loads:
        copy.start()
    greet((pair, line_y, diag, line_x), wide)
    turn = lambda i, src, dst, dev: remote(src, dst, ts.at[i], tr.at[i], dev)
    put = [
        turn(0, se.at[:, :, :, other], rx, line_x),
        turn(1, c1.at[1 - y], cy1, line_y),
        turn(2, se.at[1 - y, :, :, late], ry, line_y),
        turn(3, e1, x1, line_x),
        turn(4, e2, x2, line_x),
    ]
    cross = [
        remote(gxp, rgx, ms.at[0], mr.at[0], pair),
        remote(gep, rge, ms.at[1], mr.at[1], pair),
        remote(outp.at[1], out_o.at[y], ms.at[2], mr.at[2], diag),
    ]
    out_got = remote(out_o.at[1 - y], out_o.at[1 - y], ms.at[2], mr.at[2], diag)
    z_refs = ((a1, rzs1), (a2, rzs2), (b1, rzc1), (c2, rzc2))

    def zcopy(path, k):
        row = lax.rem(w + k, wide)
        src, dst = z_refs[path]
        src = src.at[y, row] if path == 0 else src.at[row]
        return remote(src, dst.at[w], zs.at[path, k], zr.at[path, w], (d, row, n))

    def zgot(path, k):
        row = lax.rem(w + k, wide)
        ref = z_refs[path][1].at[row]
        return remote(ref, ref, zs.at[path, k], zr.at[path, row], (d, row, n))

    def zstart(path):
        loop(1, wide, lambda k: zcopy(path, k).start())

    def zwait(path):
        loop(1, wide, lambda k: zgot(path, k).wait_recv())

    cross[0].start()
    cross[1].start()
    put[0].start()
    put[1].start()
    put[2].start()
    zstart(3)
    cross[2].start()
    put[3].start()
    put[4].start()

    sg[...] = jnp.zeros((8, D), f32)
    sg[1:2, :] = gcross[...]
    sg[2:3, :] = gfeed[...]
    st[...] = tg[...]
    cross[0].wait_recv()
    own = (n, dn)
    for i in (1, 0):

        def back(r, i=i):
            x = xf[own[i], r, :].astype(f32)
            dx, gg = norm_back(x, gain[...], gxo[i, r, :] + rgx[i, r, :].astype(f32))
            total = d1[i, r, :] + dx
            sg[0:1, :] += gg
            if i == 0:
                rows_f[0, r, :] = total
            else:
                tmp_in[r, :] = total.astype(bf16)

        rows_loop(256, 32, back, unroll=2)
        if i == 1:
            in_send = remote(tmp_in, back_in, ms.at[3], mr.at[3], diag)
            in_send.start()
    in_local = pltpu.make_async_copy(rows_f.at[0], gin_o.at[y], os.at[0])
    in_local.start()
    cross[1].wait_recv()
    loads[3].wait()
    back_en[0] = (tmp_en[1] + rge[1].astype(f32)).astype(bf16)
    en_send = remote(back_en.at[0], back_en.at[1], ms.at[4], mr.at[4], diag)
    en_send.start()
    tmp_en[0] = tmp_en[0] + rge[0].astype(f32)
    en_local = pltpu.make_async_copy(tmp_en.at[0], gen_o.at[y], os.at[1])
    en_local.start()

    def small(j, dev):
        return (
            remote(sg, rsg.at[j], ss.at[0, j], sr.at[0, j], dev),
            remote(st, rst.at[j], ss.at[1, j], sr.at[1, j], dev),
        )

    def small_add(j, dev):
        for copy in small(j, dev):
            copy.wait()
        sg[...] += rsg[j]
        st[...] += rst[j]

    def small_line(k):
        dev = (d, lax.rem(w + k, wide), n)
        return (
            remote(sg, rsgz.at[w], ss.at[0, 3 + k], sr.at[0, 3 + w], dev),
            remote(st, rstz.at[w], ss.at[1, 3 + k], sr.at[1, 3 + w], dev),
        )

    def start_all(copies):
        for copy in copies:
            copy.start()

    start_all(small(0, pair))
    small_add(0, pair)
    start_all(small(1, line_y))

    loads[2].wait()
    put[1].wait_recv()
    add_into(b1, cy1)
    zstart(2)
    small_add(1, line_y)
    start_all(small(2, line_x))
    loads[1].wait()
    put[2].wait_recv()
    add_into(a2, ry)
    zstart(1)
    small_add(2, line_x)
    loop(1, wide, lambda k: start_all(small_line(k)))
    rsgz[w] = sg[...]
    rstz[w] = st[...]
    loads[0].wait()
    put[0].wait_recv()
    add_into(a1, rx)
    y1 = turn(5, a1.at[1 - y], ry1, line_y)
    y1.start()

    def keep(ref, cols):
        def store(r, total):
            ref[r, cols] = total.astype(bf16)

        return store

    everything = slice(None)
    zwait(3)
    sum_line(wide, c2.at[w], rzc2, keep(fc, late))
    f_c2 = turn(6, fc.at[:, late], xc2, line_x)
    f_c2.start()
    zwait(2)
    sum_line(wide, b1.at[w], rzc1, keep(fc, mine))
    f_c1 = turn(7, fc.at[:, mine], xc1, line_x)
    f_c1.start()
    y1.wait_recv()
    rl = e1.shape[0]

    def add_side(k):
        a1[y, k] = a1[y, k] + ry1[k]

    loop(0, wide, add_side)
    zstart(0)

    def small_wait(k):
        row = lax.rem(w + k, wide)
        for i, ref in enumerate((rsgz, rstz)):
            remote(ref.at[row], ref.at[row], ss.at[i, 3], sr.at[i, 3 + row], line_x).wait_recv()

    loop(1, wide, small_wait)
    sg_o[...] = lax.fori_loop(1, wide, lambda k, t: t + rsgz[k], rsgz[0])
    st_o[...] = lax.fori_loop(1, wide, lambda k, t: t + rstz[k], rstz[0])

    zwait(1)
    sum_line(wide, a2.at[w], rzs2, keep(fs, late))
    f_s2 = turn(8, fs.at[:, late], xs2, line_x)
    f_s2.start()

    in_send.wait_recv()

    def widen(r):
        rows_f[1, r, :] = back_in[r, :].astype(f32)

    rows_loop(256, 64, widen)
    in_last = pltpu.make_async_copy(rows_f.at[1], gin_o.at[1 - y], os.at[2])
    in_last.start()
    en_send.wait_recv()
    tmp_en[1] = back_en[1].astype(f32)
    en_last = pltpu.make_async_copy(tmp_en.at[1], gen_o.at[1 - y], os.at[3])
    en_last.start()

    f_mine = pl.ds(pl.multiple_of(d * 384, 128), 384)
    f_other = pl.ds(pl.multiple_of(384 - d * 384, 128), 384)
    put[3].wait_recv()
    put[4].wait_recv()
    ff_o[:, f_mine] = e1[...].astype(f32)
    ff_o[:, f_other] = x1[...].astype(f32)
    ff_o[:, pl.ds(D, D)] = e2[...].astype(f32) + x2[...].astype(f32)
    f_c1.wait_recv()
    f_c2.wait_recv()
    cr_o[:, mine] = fc[:, mine].astype(f32)
    cr_o[:, other] = xc1[...].astype(f32)
    cr_o[:, late] = fc[:, late].astype(f32) + xc2[...].astype(f32)
    zwait(0)
    sum_line(wide, a1.at[y, w], rzs1, keep(fs, mine))
    f_s1 = turn(9, fs.at[:, mine], xs1, line_x)
    f_s1.start()
    out_got.wait_recv()
    f_s2.wait_recv()
    se_o[:, mine] = fs[:, mine].astype(f32)
    se_o[:, late] = fs[:, late].astype(f32) + xs2[...].astype(f32)
    f_s1.wait_recv()
    se_o[:, other] = xs1[...].astype(f32)

    for copy in (in_local, en_local, in_last, en_last, loads[4]):
        copy.wait()
    for copy in (*cross, in_send, en_send, *put, y1, f_c1, f_c2, f_s1, f_s2):
        copy.wait_send()

    def finish(k):
        for path in range(4):
            zcopy(path, k).wait_send()
        for copy in small_line(k):
            copy.wait_send()

    loop(1, wide, finish)


def reduce_all(wide, se, c1, c2, e1, e2, outp, gxo, gxp, geo, gep, xf, d1, gain, gfeed, gcross, tg):
    rl = D // wide
    se = se.reshape(2, wide, rl, D)
    sem = pltpu.SemaphoreType.DMA
    V = pl.BlockSpec(memory_space=pltpu.VMEM)
    v = lambda *shape: pltpu.VMEM(shape, bf16)
    return pl.pallas_call(
        partial(reduce_kernel, wide),
        in_specs=[ANY, ANY, V, V, V, ANY, V, ANY, ANY, ANY, V, V, V, V, V, V],
        out_specs=[ANY, ANY, ANY, V, V, V, V, V],
        out_shape=[
            out((2, 256, D), bf16),
            out((2, 256, D), f32),
            out((2, 128, D), f32),
            out((8, D), f32),
            out((32, 128), f32),
            out((rl, 2 * D), f32),
            out((rl, D), f32),
            out((rl, D), f32),
        ],
        scratch_shapes=[
            v(2, wide, rl, 256),
            v(wide, rl, 256),
            v(2, wide, rl, 256),
            v(wide, rl, 256),
            v(wide, rl, 256),
            v(wide, rl, 256),
            v(wide, rl, 256),
            v(wide, rl, 256),
            v(wide, rl, 256),
            v(wide, rl, 256),
            v(wide, rl, 256),
            v(rl, D),
            v(rl, D),
            v(rl, 256),
            v(rl, 256),
            v(rl, 256),
            v(rl, 256),
            v(rl, 384),
            v(rl, D),
            v(2, 256, D),
            v(2, 128, D),
            v(256, D),
            pltpu.VMEM((2, 128, D), f32),
            v(256, D),
            v(2, 128, D),
            pltpu.VMEM((2, 256, D), f32),
            pltpu.VMEM((8, D), f32),
            pltpu.VMEM((32, 128), f32),
            pltpu.VMEM((3, 8, D), f32),
            pltpu.VMEM((3, 32, 128), f32),
            pltpu.VMEM((wide, 8, D), f32),
            pltpu.VMEM((wide, 32, 128), f32),
            sem((5,)),
            sem((5,)),
            sem((5,)),
            sem((10,)),
            sem((10,)),
            sem((4, wide)),
            sem((4, wide)),
            sem((2, 3 + wide)),
            sem((2, 3 + wide)),
            sem((4,)),
        ],
        compiler_params=pltpu.CompilerParams(
            collective_id=1, has_side_effects=True, vmem_limit_bytes=VMEM_LIMIT
        ),
        name="reduce_all",
    )(se, c1, c2, e1, e2, outp, gxo, gxp, geo, gep, xf, d1, gain, gfeed, gcross, tg)


def on_device(
    wide, hidden_in, encoder_out, cotangent, piece_starts, valid_lengths, bucket_table,
    gain_self, gain_cross, gain_feed, relative_bias, *mats
):
    me = lax.axis_index("narrow")
    micro = me // 2
    sq, sk, sv, so, cq, ck, cv, co, gate, up, down = mats
    ps = jnp.concatenate((sq, so, sk, sv), axis=1)
    pc = jnp.concatenate((cq, co, ck, cv), axis=1)
    pf = jnp.concatenate((gate, up, down), axis=1)
    tab = jnp.pad(relative_bias.T, ((0, 29), (0, 96)))
    xf, ef, cf, tabs, ws, wc, wf = gather(
        wide, hidden_in[:, 0], encoder_out[:, 0], cotangent[:, 0], tab, ps, pc, pf
    )
    ws, wc, wf = (g.reshape(4, D, g.shape[-1]) for g in (ws, wc, wf))
    xs, es, cs = xf.reshape(LEN, D), ef.reshape(ENC, D), cf.reshape(512, D)
    table = tabs[:, :3, :32].reshape(12, 32)
    one_hot = (bucket_table[:, None] == jnp.arange(BUCKETS)[None, :]).astype(f32)
    off = lax.dot_general(table, one_hot, (((1,), (1,)), ((), ())), precision=precise)
    off = jnp.pad(off, ((0, 0), (0, 1))).reshape(4, 3, 2048)
    info = jnp.stack([piece_starts[micro, 0], valid_lengths[micro, 0]])
    gains = [g.reshape(1, D) for g in (gain_self, gain_cross, gain_feed)]

    q, kv, at, p, h1 = self_forward(info, xs, ws, off, gains[0])
    cq, ckv, cat, cp, h2 = cross_forward(h1, es, wc, gains[1])
    gff, outp, d2, gg_feed = feed(h2, cs, wf, gains[2])
    gcr, d1, gg_cross, geo, gep, o1, o2 = cross_backward(wide, h1, es, d2, wc, gains[1], cq, ckv, cat, cp, gff)
    gse, gxo, gxp, dl, c1, c2, e1, e2 = self_backward(wide, xs, d1, ws, gains[0], q, kv, at, p, gcr, o1, o2)

    dl = jnp.where(me % 2 == 1, dl, dl.reshape(2, 2, 3, 2048)[:, ::-1].reshape(4, 3, 2048))
    doff = dl.reshape(12, 2048)[:, :2047]
    tg = lax.dot_general(one_hot, doff, (((0,), (1,)), ((), ())), precision=precise)
    tg = jnp.pad(tg, ((0, 0), (0, 116)))
    two = lambda a: a.reshape(2, -1, D)
    outs, gin, gen, sg, st, f, b, a = reduce_all(
        wide, gse, c1, c2, e1, e2, two(outp), two(gxo), two(gxp), two(geo), two(gep), xf, two(d1), gains[0], gg_feed, gg_cross, tg
    )
    tg = lax.dynamic_slice_in_dim(st, me * 3, 3, axis=1)
    return (
        outs[:, None], gin[:, None], gen[:, None],
        sg[0], sg[1], sg[2], tg,
        a[:, :192], a[:, 384:576], a[:, 576:], a[:, 192:384],
        b[:, :192], b[:, 384:576], b[:, 576:], b[:, 192:384],
        f[:, :512], f[:, 512:1024], f[:, 1024:],
    )


def solution(mesh):
    rows = P(None, ("dp", "wide"), "narrow", None)
    mat = P("wide", "narrow")
    return jax.shard_map(
        partial(on_device, mesh.shape["wide"]),
        mesh=mesh,
        in_specs=(rows, rows, rows, P(None, ("dp", "wide")), P(None, ("dp", "wide")), P(), P(), P(), P(), P(None, "narrow"))
        + (mat,) * 11,
        out_specs=(rows, rows, rows, P(), P(), P(), P(None, "narrow")) + (mat,) * 11,
        check_vma=False,
    )
```

time: 543 us -> 368 us (0.68)
  Pallas kernels: 515 us -> 338 us
    pallas_call x2, Pallas kernels: 237 us -> 119 us  [the longest x1 72.3 us: reduce_all(): pl.pallas_call(partial(reduce_kernel, wide), in_specs=[ANY, ANY, V, V, V,...]
    pallas_call x1, Pallas kernels: 63.1 us -> 28.1 us  [self_forward(): pl.pallas_call(self_forward_kernel, grid=(4,), in_specs=[SMEM, whole((LEN...]
    pallas_call x1, Pallas kernels: 34.2 us -> 16.2 us  [cross_forward(): pl.pallas_call(cross_forward_kernel, grid=(4,), in_specs=[whole((512, D))...]
where the time goes in v2:
time: 368 us
  Pallas kernels  338 us (92%)
  local copies, waits for them, and re-layouts  20.6 us (6%)
  other arithmetic  6.17 us (2%)
    pallas_call x1, Pallas kernels, gather(): pl.pallas_call(partial(gather_kernel, wide), in_specs=[ANY] * 7, out_spec...  115 us
    pallas_call x1, Pallas kernels, reduce_all(): pl.pallas_call(partial(reduce_kernel, wide), in_specs=[ANY, ANY, V, V, V,...  72.3 us
    pallas_call x1, Pallas kernels, self_backward(): pl.pallas_call(partial(self_backward_kernel, wide), grid=(4,), in_specs=[...  46.3 us
    pallas_call x1, Pallas kernels, cross_backward(): pl.pallas_call(cross_backward_kernel, grid=(4,), in_specs=[whole((512, D)...  34.9 us
    pallas_call x1, Pallas kernels, self_forward(): pl.pallas_call(self_forward_kernel, grid=(4,), in_specs=[SMEM, whole((LEN...  28.1 us
    pallas_call x1, Pallas kernels, feed(): pl.pallas_call(feed_kernel, grid=(4,), in_specs=[whole((512, D)), whole((...  25.1 us
    pallas_call x1, Pallas kernels, cross_forward(): pl.pallas_call(cross_forward_kernel, grid=(4,), in_specs=[whole((512, D))...  16.2 us

profile of v2, /device:TPU:0, one launch (start us, length us, event | category | flops | bytes accessed | tf_op | source)
XLA Modules:
  0.0 367.5 jit_solution(6644812674332257291)
XLA Ops:
  0.7 1.3 constant_dynamic-slice_fusion.1
  1.9 1.9 pad_add_fusion.info
  3.8 1.3 reshape.110.gain
  5.1 1.3 reshape.113.gain
  6.4 1.3 reshape.116.gain
  7.6 1.3 pad.12.tab
  8.9 2.0 pad_maximum_fusion.pf
  10.9 2.3 pad_maximum_fusion.1
  13.1 0.0 copy-start.5
  13.2 115.1 %gather.1 = (bf16[4,256,768]{2,1,0:T(8,128)(2,1)}, bf16[4,128,768]{2,1,0:T(8,128)(2,1)}, bf16[2,256,768]{2,1,0:T(8,128)(2,1)}, f32[4,32,128]{2,1,0:T(8,128)}, bf...) custom-call(bf16[2,256,768]{2,1,0:T(8,128)(2,1)} %bitcast.45, ...), custom_call_target="tpu_custom_call" | custom-call | tf_op jit(solution)/shard_map/gather/pallas_call | solution.py:966
  128.2 0.7 slice.48
  129.0 0.0 copy-done.5
  129.0 0.9 fusion.1
  129.9 0.7 reshape.109.off
  130.6 28.1 %self_forward.1 = (bf16[4,512,192]{2,1,0:T(8,128)(2,1)}, bf16[4,384,1024]{2,1,0:T(8,128)(2,1)}, bf16[4,512,192]{2,1,0:T(8,128)(2,1)}, bf16[4,3,512,1024]{3,2,1,0:T(8,128)(2,1)}, f32[512,768]{1,0:T(8,128)}) custom-call(s32[2]{0:T(128)} %pad_add_fusion.info, bf16[1024,768]{1,0:T(8,128)(2,1)} %bitcast.35, bf16[4,768,768]{2,1,0:T(8,128)(2,1)} %bitcast.52, ...), custom_call_target="tpu_custom_call" | custom-call | flops 20000000000 | bytes 20971520 | tf_op jit(solution)/shard_map/self_forward/pallas_call | solution.py:267
  158.7 16.2 %cross_forward.1 = (bf16[4,512,192]{2,1,0:T(8,128)(2,1)}, bf16[4,384,512]{2,1,0:T(8,128)(2,1)}, bf16[4,512,192]{2,1,0:T(8,128)(2,1)}, bf16[4,3,512,512]{3,2,1,0:T(8,128)(2,1)}, f32[512,768]{1,0:T(8,128)}) custom-call(f32[512,768]{1,0:T(8,128)} %get-tuple-element.65.h1, bf16[512,768]{1,0:T(8,128)(2,1)} %bitcast.56, bf16[4,768,768]{2,1,0:T(8,128)(2,1)} %bitcast.54, ...), custom_call_target="tpu_custom_call" | custom-call | flops 10000000000 | bytes 20971520 | tf_op jit(solution)/shard_map/cross_forward/pallas_call | solution.py:319
  175.0 25.1 %feed.1 = (bf16[2,768,1536]{2,1,0:T(8,128)(2,1)}, bf16[512,768]{1,0:T(8,128)(2,1)}, f32[512,768]{1,0:T(8,128)}, f32[1,768]{1,0:T(1,128)}) custom-call(f32[512,768]{1,0:T(8,128)} %get-tuple-element.68.h2, bf16[512,768]{1,0:T(8,128)(2,1)} %bitcast.58, bf16[4,768,1536]{2,1,0:T(8,128)(2,1)} %bitcast.51, f32[1,768]{1,0:T(1,128)} %reshape.116.gain), custom_call_target="tpu_custom_call" | custom-call | flops 30000001024 | bytes 20971520 | tf_op jit(solution)/shard_map/feed/pallas_call | solution.py:399
  200.1 34.9 %cross_backward.1 = (bf16[2,768,768]{2,1,0:T(8,128)(2,1)}, f32[512,768]{1,0:T(8,128)}, f32[1,768]{1,0:T(1,128)}, f32[256,768]{1,0:T(8,128)}, bf16[256,768]{1,0:T...) custom-call(f32[512,768]{1,0:T(8,128)} %get-tuple-element.65.h1, bf16[512,768]{1,0:T(8,128)(2,1)} %bitcast.57, ...), custom_call_target="tpu_custom_call" | custom-call | flops 14000000000 | bytes 20971520 | tf_op jit(solution)/shard_map/cross_backward/pallas_call | solution.py:510
  235.0 46.3 %self_backward.1 = (bf16[2,768,768]{2,1,0:T(8,128)(2,1)}, f32[512,768]{1,0:T(8,128)}, bf16[512,768]{1,0:T(8,128)(2,1)}, f32[4,3,2048]{2,1,0:T(4,128)}, bf16[2,4,...) custom-call(bf16[1024,768]{1,0:T(8,128)(2,1)} %bitcast.36, ...), custom_call_target="tpu_custom_call" | custom-call | flops 24999999488 | bytes 20971520 | tf_op jit(solution)/shard_map/self_backward/pallas_call | solution.py:712
  281.3 0.9 rev.3
  282.3 0.1 bitcast_select_fusion
  282.4 1.0 fusion.2
  283.4 0.6 pad.14.tg
  284.0 72.3 %reduce_all.1 = (bf16[2,256,768]{2,1,0:T(8,128)(2,1)}, f32[2,256,768]{2,1,0:T(8,128)}, f32[2,128,768]{2,1,0:T(8,128)}, f32[8,768]{1,0:T(8,128)}, f32[32,128]{1,0...) custom-call(bf16[2,4,192,768]{3,2,1,0:T(8,128)(2,1)} %bitcast.34, ...), custom_call_target="tpu_custom_call" | custom-call | tf_op jit(solution)/shard_map/reduce_all/pallas_call | solution.py:1237
  356.3 0.0 copy-start.2
  356.4 1.5 slice_reduce_fusion
  357.8 0.8 constant_dynamic-slice_fusion
  358.6 0.7 copy.48
  359.3 0.0 copy-start.1
  359.3 2.3 fusion.9
  361.6 0.0 copy-done.2
  361.6 1.0 fusion.8
  362.5 0.0 copy-start.4
  362.5 0.0 copy-done.1
  362.5 0.0 copy-start
  362.6 1.0 fusion.7
  363.6 0.5 copy-done.4
  364.1 0.9 copy.53
  365.0 0.0 copy-done
  365.0 0.0 copy-start.3
  365.0 1.1 copy.54
  366.1 0.5 copy-done.3
  366.7 0.9 copy.55
  (3 shorter events, 0.1 us)
Async XLA Ops:
  13.1 115.8 %copy-start.5 = (s32[2047]{0:T(1024)S(1)}, s32[2047]{0:T(1024)}, u32[]{:S(2)}) copy-start(s32[2047]{0:T(1024)} %param.26) | copy-start | bytes 24568
  356.3 5.2 %copy-start.2 = (f32[192,768]{1,0:T(8,128)S(1)}, f32[192,768]{1,0:T(8,128)}, u32[]{:S(2)}) copy-start(f32[192,768]{1,0:T(8,128)} %get-tuple-element.104) | copy-start | bytes 1769476
  359.3 3.3 copy-start.1
  362.5 1.6 copy-start.4
  362.5 2.4 copy-start
  365.0 1.7 copy-start.3

commit v3 on v2

--- a/solution.py
+++ b/solution.py
@@ -1,3 +1,4 @@
+import math
 from functools import partial
 
 import jax
@@ -173,59 +174,6 @@
             self.copy().wait_send()
 
 
-def self_forward_kernel(
-    info, xf, w, off, gain, q_o, kv_o, at_o, p_o, h1_o, nf, mask, tb, s
-):
-    n = pl.program_id(0)
-    blks = own_blocks()
-
-    @pl.when(n == 0)
-    def _():
-        def norm_rows(r):
-            nf[r, :] = normed(xf[r, :].astype(f32), gain[...]).astype(bf16)
-
-        rows_loop(LEN, 64, norm_rows)
-        start, length = info[0], info[1]
-        for i in range(2):
-            h1_o[i * 256 : (i + 1) * 256, :] = xf[block_rows(blks[i]), :].astype(f32)
-
-            def mask_rows(r, i=i):
-                shape = (ROWS, LEN)
-                qi = blks[i] * 256 + r.start + lax.broadcasted_iota(jnp.int32, shape, 0)
-                kj = lax.broadcasted_iota(jnp.int32, shape, 1)
-                inside = (qi >= start) & (qi < start + PIC) & (kj >= start) & (kj < start + PIC)
-                allowed = ((kj <= qi) | inside) & (kj < length)
-                mask[pl.ds(i * 256 + r.start, ROWS), :] = jnp.where(allowed, 0.0, masked_value)
-
-            rows_loop(256, ROWS, mask_rows)
-
-    kv_o[0] = nn(nf[...], w[0, :, 384:768]).astype(bf16).T
-    for i in range(2):
-        q_o[0, i * 256 : (i + 1) * 256, :] = nn(nf[block_rows(blks[i]), :], w[0, :, 0:192]).astype(bf16)
-    for h in range(3):
-        for t in range(TILES):
-            line = jnp.broadcast_to(off[0, h : h + 1, 128 * t : 128 * t + 256], (128, 256))
-            tb[t] = pltpu.roll(line, 129, 1, stride=1, stride_axis=0)[:, :128]
-        hs = slice(h * DHEAD, (h + 1) * DHEAD)
-        vs = slice(HD + h * DHEAD, HD + (h + 1) * DHEAD)
-        for i in range(2):
-            s[...] = nn(q_o[0, i * 256 : (i + 1) * 256, hs], kv_o[0, hs, :])
-            for r in range(2):
-                idx = [jnp.minimum(kb - 2 * blks[i] - r, 3) + 7 for kb in range(8)]
-
-                def soft_rows(rr, i=i, r=r, h=h, idx=idx):
-                    bias = jnp.concatenate([tb[idx[kb], rr, :] for kb in range(8)], axis=1)
-                    v = s[pl.ds(r * 128 + rr.start, ROWS), :] + bias
-                    v = v + mask[pl.ds(i * 256 + r * 128 + rr.start, ROWS), :]
-                    p_o[0, h, pl.ds(i * 256 + r * 128 + rr.start, ROWS), :] = softmax_rows(v).astype(bf16)
-
-                rows_loop(128, ROWS, soft_rows, unroll=8)
-            at_o[0, i * 256 : (i + 1) * 256, hs] = nt(
-                p_o[0, h, i * 256 : (i + 1) * 256, :], kv_o[0, vs, :]
-            ).astype(bf16)
-    h1_o[...] += nt(at_o[0], w[0, :, 192:384])
-
-
 def whole(shape):
     zero = (0,) * len(shape)
     return pl.BlockSpec(shape, lambda n: zero)
@@ -263,163 +211,571 @@
     return pl.CostEstimate(flops=int(gflop * 1e9), bytes_accessed=20 << 20, transcendentals=0)
 
 
-def self_forward(info, xf, w, off, gain):
+GELU_A = 0.7978845608028654
+GELU_B = 0.044715
+
+
+FORWARD_VMEM = 58 << 20
+ORDER_ATT = (1, 0, 3, 2)
+ORDER_FEED = (1, 0, 2, 3)
+
+
+def pick(order, k):
+    index = order[3]
+    for i in (2, 1, 0):
+        index = jnp.where(k == i, order[i], index)
+    return index
+
+
+def forward_kernel(
+    wide, ps_s, vl_s, hid, enc, cot, tab, hot, ps, pc, pf, gain_s, gain_c, gain_f,
+    xf, gs, gc, gf, gff, ef, q1, kv1, at1, p1, q2, kv2, at2, p2, h1, out_o, d2_o, gg_o,
+    wbuf, stage, xv, ev, tabs, off, nf, mask, tb, s, h2, nc, nct, cv, ct, gu, da, act, dgu, acc, buf, landed,
+    ls, ins, inr, ws, vs, zs, zr, ys, yr, xs, xr, cs, cr, fsend, frecv, fout,
+):
+    step = pl.program_id(0)
+    d, w, n, pn, yn, dn = place_here()
+    y = n // 2
+    blks = (n, dn)
+    rl = ps.shape[0]
+    groups = ((ps, gs, 0, 768, True), (pc, gc, 0, 768, True), (pf, gf, 0, 1024, True), (pf, gf, 1024, 512, False))
+    keep, give = (1, 3), (0, 2)
+    diag, pair, line_x, line_y = (d, w, dn), (d, w, pn), (1 - d, w, n), (d, w, yn)
+
+    def cols(g, which):
+        start, width, split = groups[g][2:]
+        if which == 2 or not split:
+            return pl.ds(start, width)
+        half = width // 2
+        pos = d if which == 0 else 1 - d
+        return pl.ds(pl.multiple_of(start + pos * half, 128), half)
+
+    def own(g, which):
+        return groups[g][0].at[:, cols(g, which)]
+
+    def spot(g, slot, row, which):
+        return groups[g][1].at[slot, row, :, cols(g, which)]
+
+    def zcopy(g, k):
+        dev = (d, lax.rem(w + k, wide), n)
+        if g == 4:
+            ref = spot(3, 3, w, 0)
+            return remote(ref, ref, zs.at[4, k], zr.at[4, w], dev)
+        return remote(own(g, 0), spot(g, 1, w, 0), zs.at[g, k], zr.at[g, w], dev)
+
+    def zgot(g, row):
+        ref = spot(3, 3, row, 0) if g == 4 else spot(g, 1, row, 0)
+        return remote(ref, ref, zs.at[g, 0], zr.at[g, row], line_x)
+
+    def ycopy(g, row, src=None):
+        ref = spot(g, 1, row, 0)
+        return remote(ref if src is None else src, spot(g, 3, row, 0), ys.at[g, row], yr.at[g, row], line_y)
+
+    def ygot(g, row):
+        return remote(spot(g, 3, row, 0), spot(g, 3, row, 0), ys.at[g, row], yr.at[g, row], line_y)
+
+    def xcopy(g, side, row):
+        ref = spot(g, keep[side], row, 0)
+        return remote(ref, ref, xs.at[g, side, row], xr.at[g, side, row], line_x)
+
+    def xgot(g, side, row):
+        ref = spot(g, keep[side], row, 1)
+        return remote(ref, ref, xs.at[g, side, row], xr.at[g, side, row], line_x)
+
+    def ccopy(g, side, row, src=None):
+        ref = spot(g, keep[side], row, 2)
+        return remote(
+            ref if src is None else src, spot(g, give[side], row, 2), cs.at[g, side, row], cr.at[g, side, row], pair
+        )
+
+    def cgot(g, side, row):
+        ref = spot(g, give[side], row, 2)
+        return remote(ref, ref, cs.at[g, side, row], cr.at[g, side, row], pair)
+
+    def around(first, body):
+        loop(first, wide, lambda k: body(lax.rem(w + k, wide)))
+
+    def zsend(g):
+        loop(1, wide, lambda k: zcopy(g, k).start())
+
+    def own_sends(g):
+        ycopy(g, w, own(g, 0)).start()
+        ccopy(g, 0, w, own(g, 2)).start()
+
+    def zpass(g, then):
+        def one(row):
+            zgot(g, row).wait_recv()
+            for nxt in then:
+                nxt(row).start()
+
+        around(1, one)
+
+    def ypass(g):
+        def one(row):
+            ygot(g, row).wait_recv()
+            xcopy(g, 1, row).start()
+
+        around(0, one)
+
+    def xsend(g):
+        around(1, lambda row: xcopy(g, 0, row).start())
+
+    def xstep(g, side):
+        def one(k):
+            row = lax.rem(w + k, wide)
+            xgot(g, side, row).wait_recv()
+            ccopy(g, side, row).start()
+
+        loop(1 - side, wide, one)
+
+    def cwait(g, side):
+        loop(0, wide, lambda k: cgot(g, side, lax.rem(w + k, wide)).wait_recv())
+
+    straight = rl % 16 == 0
+    many = 16 // math.gcd(rl, 16)
+
+    def slab_copies(ref, slot, b):
+        width = ref.shape[-1]
+        if straight:
+            return [
+                pltpu.make_async_copy(
+                    ref.at[slot, k], wbuf.at[b, pl.ds(k * rl, rl), pl.ds(0, width)], ws.at[b, k]
+                )
+                for k in range(wide)
+            ]
+        return [pltpu.make_async_copy(ref.at[slot], stage.at[:, :, pl.ds(0, width)], ws.at[b, 0])]
+
+    def fetch(ref, slot, b):
+        for copy in slab_copies(ref, slot, b):
+            copy.start()
+
+    def fetched(ref, slot, b):
+        for copy in slab_copies(ref, slot, b):
+            copy.wait()
+        if not straight:
+            width = ref.shape[-1]
+            for k in range(0, wide, many):
+                part = jnp.concatenate([stage[k + i, :, 0:width].astype(f32) for i in range(many)], axis=0)
+                wbuf[b, k * rl : (k + many) * rl, 0:width] = part.astype(bf16)
+
+    local = [
+        pltpu.make_async_copy(src, dst, ls.at[i])
+        for i, (src, dst) in enumerate(
+            (
+                (ps, gs.at[1, w]),
+                (pc, gc.at[1, w]),
+                (pf, gf.at[1, w]),
+                (hid.at[y], xv.at[n]),
+                (enc.at[y], ev.at[n]),
+                (cot.at[y], cv.at[0]),
+            )
+        )
+    ]
+    back = [pltpu.make_async_copy(xv, xf, vs.at[0]), pltpu.make_async_copy(ev, ef, vs.at[1])]
+    early = [
+        remote(tab, tabs.at[0], ins.at[3], inr.at[3], pair),
+        remote(tab, tabs.at[3], ins.at[4], inr.at[4], line_y),
+        remote(tab, tabs.at[2], ins.at[5], inr.at[5], diag),
+        remote(hid.at[1 - y], xv.at[n], ins.at[0], inr.at[0], diag),
+        remote(hid.at[y], xv.at[n], ins.at[6], inr.at[6], pair),
+    ]
+    middle = [
+        remote(enc.at[1 - y], ev.at[n], ins.at[1], inr.at[1], diag),
+        remote(enc.at[y], ev.at[n], ins.at[7], inr.at[7], pair),
+        remote(cot.at[1 - y], cv.at[1], ins.at[2], inr.at[2], diag),
+    ]
+    later = [
+        remote(xv.at[dn], xv.at[dn], ins.at[8], inr.at[8], pair),
+        remote(ev.at[dn], ev.at[dn], ins.at[9], inr.at[9], pair),
+    ]
+
+    def arrived(i, ref):
+        remote(ref, ref, ins.at[i], inr.at[i], pair).wait_recv()
+
+    @pl.when(step == 0)
+    def _():
+        for copy in local:
+            copy.start()
+        greet((pair, line_y, diag, line_x), wide)
+        for copy in early:
+            copy.start()
+        zsend(0)
+        own_sends(0)
+        tabs[1] = tab[...]
+        arrived(6, xv.at[pn])
+        arrived(0, xv.at[dn])
+        later[0].start()
+        arrived(8, xv.at[yn])
+        local[3].wait()
+        back[0].start()
+        arrived(3, tabs.at[0])
+        arrived(4, tabs.at[3])
+        arrived(5, tabs.at[2])
+        start, length = ps_s[y, 0], vl_s[y, 0]
+        for i in range(2):
+
+            def mask_rows(r, i=i):
+                shape = (32, LEN)
+                qi = blks[i] * 256 + r.start + lax.broadcasted_iota(jnp.int32, shape, 0)
+                kj = lax.broadcasted_iota(jnp.int32, shape, 1)
+                inside = (qi >= start) & (qi < start + PIC) & (kj >= start) & (kj < start + PIC)
+                allowed = ((kj <= qi) | inside) & (kj < length)
+                mask[pl.ds(i * 256 + r.start, 32), :] = jnp.where(allowed, 0.0, masked_value)
+
+            rows_loop(256, 32, mask_rows)
+        for i in range(4):
+
+            def norm_rows(r, i=i):
+                nf[pl.ds(i * 256 + r.start, 64), :] = normed(xv[i, r, :].astype(f32), gain_s[...]).astype(bf16)
+
+            rows_loop(256, 64, norm_rows)
+        for i in range(2):
+            h1[i * 256 : (i + 1) * 256, :] = xv[blks[i]].astype(f32)
+        zpass(0, (lambda row: ycopy(0, row), lambda row: xcopy(0, 0, row)))
+        zsend(1)
+        own_sends(1)
+        middle[0].start()
+        middle[1].start()
+        xstep(0, 0)
+        for i in range(3):
+            local[i].wait()
+        fetch(gs, 1, 0)
+
+    @pl.when(step < 4)
+    def _():
+        b = lax.rem(step, 2)
+        slot = pick(ORDER_ATT, step)
+        fetched(gs, slot, b)
+        off[...] = lax.dot_general(
+            tabs[slot, 0:8, 0:BUCKETS], hot[...], (((1,), (0,)), ((), ())), precision=precise, preferred_element_type=f32
+        )
+        kv1[0] = nn(nf[...], wbuf[b, :, 384:768]).astype(bf16).T
+        for i in range(2):
+            q1[0, i * 256 : (i + 1) * 256, :] = nn(nf[block_rows(blks[i]), :], wbuf[b, :, 0:192]).astype(bf16)
+        for h in range(3):
+            for t in range(TILES):
+                line = jnp.broadcast_to(off[h : h + 1, 128 * t : 128 * t + 256], (128, 256))
+                tb[t] = pltpu.roll(line, 129, 1, stride=1, stride_axis=0)[:, :128]
+            hs = slice(h * DHEAD, (h + 1) * DHEAD)
+            vs_ = slice(HD + h * DHEAD, HD + (h + 1) * DHEAD)
+            for i in range(2):
+                s[...] = nn(q1[0, i * 256 : (i + 1) * 256, hs], kv1[0, hs, :])
+                for r in range(2):
+                    idx = [jnp.minimum(kb - 2 * blks[i] - r, 3) + 7 for kb in range(8)]
+
+                    def soft_rows(rr, i=i, r=r, h=h, idx=idx):
+                        bias = jnp.concatenate([tb[idx[kb], rr, :] for kb in range(8)], axis=1)
+                        v = s[pl.ds(r * 128 + rr.start, ROWS), :] + bias
+                        v = v + mask[pl.ds(i * 256 + r * 128 + rr.start, ROWS), :]
+                        p1[0, h, pl.ds(i * 256 + r * 128 + rr.start, ROWS), :] = softmax_rows(v).astype(bf16)
+
+                    rows_loop(128, ROWS, soft_rows, unroll=8)
+                at1[0, i * 256 : (i + 1) * 256, hs] = nt(
+                    p1[0, h, i * 256 : (i + 1) * 256, :], kv1[0, vs_, :]
+                ).astype(bf16)
+        h1[...] += nt(at1[0], wbuf[b, :, 192:384])
+
+    @pl.when(step == 0)
+    def _():
+        cwait(0, 0)
+        fetch(gs, 0, 1)
+        ypass(0)
+        zpass(1, (lambda row: ycopy(1, row),))
+        zsend(2)
+        own_sends(2)
+        own_sends(3)
+
+    @pl.when(step == 1)
+    def _():
+        xstep(0, 1)
+        fetch(gs, 3, 0)
+        xsend(1)
+        middle[2].start()
+
+    @pl.when(step == 2)
+    def _():
+        cwait(0, 1)
+        fetch(gs, 2, 1)
+        ypass(1)
+        zpass(2, (lambda row: ycopy(2, row),))
+        zsend(3)
+        ygot(3, w).wait_recv()
+        ccopy(3, 1, w).start()
+        zsend(4)
+
+    @pl.when(step == 3)
+    def _():
+        xstep(1, 0)
+        fetch(gc, 1, 0)
+        xsend(2)
+        arrived(1, ev.at[dn])
+        later[1].start()
+        arrived(7, ev.at[pn])
+        arrived(9, ev.at[yn])
+        local[4].wait()
+        back[1].start()
+
+        def norm_rows(r):
+            x = h1[r, :]
+            nc[r, :] = normed(x, gain_c[...]).astype(bf16)
+            h2[r, :] = x
+
+        rows_loop(512, 64, norm_rows)
+
+    @pl.when((step >= 4) & (step < 8))
+    def _():
+        b = lax.rem(step, 2)
+        fetched(gc, pick(ORDER_ATT, step - 4), b)
+        kv2[0] = nn(ev[...].reshape(ENC, D), wbuf[b, :, 384:768]).astype(bf16).T
+        q2[0] = nn(nc[...], wbuf[b, :, 0:192]).astype(bf16)
+        for h in range(3):
+            hs = slice(h * DHEAD, (h + 1) * DHEAD)
+            vs_ = slice(HD + h * DHEAD, HD + (h + 1) * DHEAD)
+            gu[:, 0:ENC] = nn(q2[0, :, hs], kv2[0, hs, :])
+
+            def soft_rows(r, h=h):
+                p2[0, h, r, :] = softmax_rows(gu[r, 0:ENC]).astype(bf16)
+
+            rows_loop(512, 16, soft_rows, unroll=32)
+            at2[0, :, hs] = nt(p2[0, h], kv2[0, vs_, :]).astype(bf16)
+        h2[...] += nt(at2[0], wbuf[b, :, 192:384])
+
+    @pl.when(step == 4)
+    def _():
+        cwait(1, 0)
+        fetch(gc, 0, 1)
+
+    @pl.when(step == 5)
+    def _():
+        xstep(1, 1)
+        fetch(gc, 3, 0)
+        ypass(2)
+
+    @pl.when(step == 6)
+    def _():
+        cwait(1, 1)
+        fetch(gc, 2, 1)
+
+    @pl.when(step == 7)
+    def _():
+        xstep(2, 0)
+        zpass(3, (lambda row: ccopy(3, 0, row),))
+        fetch(gf, 1, 0)
+        arrived(2, cv.at[1])
+        local[5].wait()
+
+        def norm_rows(r):
+            x = h2[r, :]
+            nc[r, :] = normed(x, gain_f[...]).astype(bf16)
+            acc[r, :] = x
+            d2_o[r, :] = jnp.zeros((64, D), f32)
+
+        rows_loop(512, 64, norm_rows)
+        nct[...] = nc[...].T
+        ct[...] = cv[...].reshape(512, D).T
+
+    def give_copy(side):
+        return remote(buf.at[0], landed.at[side], fsend.at[side], frecv.at[side], pair)
+
+    def put_out(side):
+        return pltpu.make_async_copy(buf.at[1], gff.at[side], fout.at[side])
+
+    def add_side(side):
+        give_copy(side).wait_recv()
+
+        def add(r):
+            buf[1, r, :] = buf[1, r, :] + landed[side, r, :]
+
+        rows_loop(D, 64, add)
+        put_out(side).start()
+
+    @pl.when(step >= 8)
+    def _():
+        b = lax.rem(step, 2)
+        fetched(gf, pick(ORDER_FEED, step - 8), b)
+        gu[...] = nn(nc[...], wbuf[b, :, : 2 * FFB])
+        da[...] = nn(cv[...].reshape(512, D), wbuf[b, :, 2 * FFB :])
+
+        def gelu_rows(r):
+            gate = gu[r, :FFB]
+            up = gu[r, FFB:]
+            d_act = da[r, :]
+            sq = gate * gate
+            th = jnp.tanh(GELU_A * gate * (1.0 + GELU_B * sq))
+            half = 0.5 + 0.5 * th
+            gelu = gate * half
+            slope = half + 0.5 * GELU_A * gate * (1.0 - th * th) * (1.0 + 3.0 * GELU_B * sq)
+            act[r, :] = (gelu * up).astype(bf16)
+            dgu[r, :FFB] = (d_act * up * slope).astype(bf16)
+            dgu[r, FFB:] = (d_act * gelu).astype(bf16)
+
+        rows_loop(512, 16, gelu_rows, unroll=32)
+        acc[...] += nt(act[...], wbuf[b, :, 2 * FFB :])
+        d2_o[...] += nt(dgu[...], wbuf[b, :, : 2 * FFB])
+
+        @pl.when(step == 10)
+        def _():
+            give_copy(0).wait_send()
+
+        @pl.when(step == 11)
+        def _():
+            put_out(0).wait()
+
+        place = jnp.where((step == 8) | (step == 11), 1, 0)
+        buf[place, :, : 2 * FFB] = nn(nct[...], dgu[...]).astype(bf16)
+        buf[place, :, 2 * FFB :] = nn(ct[...], act[...]).astype(bf16)
+
+    @pl.when(step == 8)
+    def _():
+        cwait(2, 0)
+        cwait(3, 0)
+        fetch(gf, 0, 1)
+
+    @pl.when(step == 9)
+    def _():
+        give_copy(0).start()
+        zpass(4, (lambda row: ccopy(3, 1, row),))
+        xstep(2, 1)
+        cwait(2, 1)
+        cwait(3, 1)
+        fetch(gf, 2, 0)
+
+    @pl.when(step == 10)
+    def _():
+        give_copy(1).start()
+        fetch(gf, 3, 1)
+        add_side(0)
+
+    @pl.when(step == 11)
+    def _():
+        add_side(1)
+        gg_o[...] = jnp.zeros((1, D), f32)
+
+        for i in range(2):
+
+            def back_rows(r, i=i):
+                rows = pl.ds(i * 256 + r.start, 64)
+                dx, gg = norm_back(h2[rows, :], gain_f[...], d2_o[rows, :])
+                d2_o[rows, :] = cv[i, r, :].astype(f32) + dx
+                gg_o[...] += gg
+                out_o[rows, :] = acc[rows, :].astype(bf16)
+
+            rows_loop(256, 64, back_rows, unroll=2)
+        for copy in back:
+            copy.wait()
+        put_out(1).wait()
+        give_copy(1).wait_send()
+        for copy in early + middle + later:
+            copy.wait_send()
+
+        def finish(row):
+            for g in range(4):
+                for side in range(2):
+                    ccopy(g, side, row).wait_send()
+            for g in range(3):
+                ycopy(g, row).wait_send()
+                xcopy(g, 1, row).wait_send()
+
+        around(0, finish)
+        ycopy(3, w).wait_send()
+
+        def finish_line(k):
+            row = lax.rem(w + k, wide)
+            for g in range(5):
+                zcopy(g, k).wait_send()
+            for g in range(3):
+                xcopy(g, 0, row).wait_send()
+
+        loop(1, wide, finish_line)
+
+
+def forward(wide, ps_s, vl_s, hid, enc, cot, tab, hot, ps, pc, pf, gain_s, gain_c, gain_f):
+    rl = ps.shape[0]
+    sem = pltpu.SemaphoreType.DMA
+    V = pl.BlockSpec(memory_space=pltpu.VMEM)
+
+    def turn(first, shape):
+        zero = (0,) * len(shape)
+        return pl.BlockSpec(
+            (1,) + shape, lambda n: (pick(ORDER_ATT, jnp.clip(n - first, 0, 3)),) + zero
+        )
+
+    v = lambda *shape: pltpu.VMEM(shape, bf16)
+    vf = lambda *shape: pltpu.VMEM(shape, f32)
     return pl.pallas_call(
-        self_forward_kernel,
-        grid=(4,),
-        in_specs=[SMEM, whole((LEN, D)), slab((D, D)), slab((3, 2048)), whole((1, D))],
-        out_specs=[slab((512, HD)), slab((2 * HD, LEN)), slab((512, HD)), slab((3, 512, LEN)), whole((512, D))],
+        partial(forward_kernel, wide),
+        grid=(12,),
+        in_specs=[SMEM, SMEM, ANY, ANY, ANY, V, V, V, V, V, V, V, V],
+        out_specs=[ANY] * 6
+        + [turn(0, (512, HD)), turn(0, (2 * HD, LEN)), turn(0, (512, HD)), turn(0, (3, 512, LEN))]
+        + [turn(4, (512, HD)), turn(4, (2 * HD, ENC)), turn(4, (512, HD)), turn(4, (3, 512, ENC))]
+        + [V, V, V, V],
         out_shape=[
+            out((4, 256, D), bf16),
+            out((4, wide, rl, D), bf16),
+            out((4, wide, rl, D), bf16),
+            out((4, wide, rl, 2 * D), bf16),
+            out((2, D, 3 * FFB), bf16),
+            out((4, 128, D), bf16),
             out((4, 512, HD), bf16),
             out((4, 2 * HD, LEN), bf16),
             out((4, 512, HD), bf16),
             out((4, 3, 512, LEN), bf16),
-            out((512, D), f32),
-        ],
-        scratch_shapes=[
-            pltpu.VMEM((LEN, D), bf16),
-            pltpu.VMEM((512, LEN), f32),
-            pltpu.VMEM((TILES, 128, 128), f32),
-            pltpu.VMEM((256, LEN), f32),
-        ],
-        compiler_params=params(),
-        cost_estimate=cost(20),
-        name="self_forward",
-    )(info, xf, w, off, gain)
-
-
-def cross_forward_kernel(h1, ef, w, gain, q_o, kv_o, at_o, p_o, h2_o, nc, s):
-    n = pl.program_id(0)
-
-    @pl.when(n == 0)
-    def _():
-        def norm_rows(r):
-            x = h1[r, :]
-            nc[r, :] = normed(x, gain[...]).astype(bf16)
-            h2_o[r, :] = x
-
-        rows_loop(512, 64, norm_rows)
-
-    kv_o[0] = nn(ef[...], w[0, :, 384:768]).astype(bf16).T
-    q_o[0] = nn(nc[...], w[0, :, 0:192]).astype(bf16)
-    for h in range(3):
-        hs = slice(h * DHEAD, (h + 1) * DHEAD)
-        vs = slice(HD + h * DHEAD, HD + (h + 1) * DHEAD)
-        s[...] = nn(q_o[0, :, hs], kv_o[0, hs, :])
-
-        def soft_rows(r, h=h):
-            p_o[0, h, r, :] = softmax_rows(s[r, :]).astype(bf16)
-
-        rows_loop(512, 16, soft_rows, unroll=32)
-        at_o[0, :, hs] = nt(p_o[0, h], kv_o[0, vs, :]).astype(bf16)
-    h2_o[...] += nt(at_o[0], w[0, :, 192:384])
-
-
-def cross_forward(h1, ef, w, gain):
-    return pl.pallas_call(
-        cross_forward_kernel,
-        grid=(4,),
-        in_specs=[whole((512, D)), whole((ENC, D)), slab((D, D)), whole((1, D))],
-        out_specs=[slab((512, HD)), slab((2 * HD, ENC)), slab((512, HD)), slab((3, 512, ENC)), whole((512, D))],
-        out_shape=[
             out((4, 512, HD), bf16),
             out((4, 2 * HD, ENC), bf16),
             out((4, 512, HD), bf16),
             out((4, 3, 512, ENC), bf16),
             out((512, D), f32),
+            out((512, D), bf16),
+            out((512, D), f32),
+            out((1, D), f32),
         ],
-        scratch_shapes=[pltpu.VMEM((512, D), bf16), pltpu.VMEM((512, ENC), f32)],
-        compiler_params=params(),
-        cost_estimate=cost(10),
-        name="cross_forward",
-    )(h1, ef, w, gain)
-
-
-GELU_A = 0.7978845608028654
-GELU_B = 0.044715
-
-
-def feed_kernel(
-    h2, cf, w, gain, gw_o, out_o, d2_o, gg_o, nf, nft, ct, gu, da, act, dgu, acc, buf, landed, send, recv
-):
-    n = pl.program_id(0)
-    slot = lax.rem(n, 2)
-    core = CoreSum(n, buf, landed, send, recv)
-
-    @pl.when(n == 0)
-    def _():
-        def norm_rows(r):
-            x = h2[r, :]
-            nf[r, :] = normed(x, gain[...]).astype(bf16)
-            acc[r, :] = x
-            d2_o[r, :] = jnp.zeros((64, D), f32)
-
-        greet((core_devs(),))
-        rows_loop(512, 64, norm_rows)
-        nft[...] = nf[...].T
-        ct[...] = cf[...].T
-
-    gu[...] = nn(nf[...], w[0, :, : 2 * FFB])
-    da[...] = nn(cf[...], w[0, :, 2 * FFB :])
-
-    def gelu_rows(r):
-        gate = gu[r, :FFB]
-        up = gu[r, FFB:]
-        d_act = da[r, :]
-        sq = gate * gate
-        th = jnp.tanh(GELU_A * gate * (1.0 + GELU_B * sq))
-        half = 0.5 + 0.5 * th
-        gelu = gate * half
-        slope = half + 0.5 * GELU_A * gate * (1.0 - th * th) * (1.0 + 3.0 * GELU_B * sq)
-        act[r, :] = (gelu * up).astype(bf16)
-        dgu[r, :FFB] = (d_act * up * slope).astype(bf16)
-        dgu[r, FFB:] = (d_act * gelu).astype(bf16)
-
-    rows_loop(512, 16, gelu_rows, unroll=32)
-    acc[...] += nt(act[...], w[0, :, 2 * FFB :])
-    buf[slot, :, : 2 * FFB] = nn(nft[...], dgu[...]).astype(bf16)
-    buf[slot, :, 2 * FFB :] = nn(ct[...], act[...]).astype(bf16)
-    d2_o[...] += nt(dgu[...], w[0, :, : 2 * FFB])
-    core.finish(gw_o)
-
-    @pl.when(n == 3)
-    def _():
-        gg_o[...] = jnp.zeros((1, D), f32)
-
-        def back_rows(r):
-            dx, gg = norm_back(h2[r, :], gain[...], d2_o[r, :])
-            d2_o[r, :] = cf[r, :].astype(f32) + dx
-            gg_o[...] += gg
-            out_o[r, :] = acc[r, :].astype(bf16)
-
-        rows_loop(512, 64, back_rows)
-
-
-def feed(h2, cf, w, gain):
-    return pl.pallas_call(
-        feed_kernel,
-        grid=(4,),
-        in_specs=[whole((512, D)), whole((512, D)), slab((D, 3 * FFB)), whole((1, D))],
-        out_specs=[pair_slab((D, 3 * FFB)), whole((512, D)), whole((512, D)), whole((1, D))],
-        out_shape=[out((2, D, 3 * FFB), bf16), out((512, D), bf16), out((512, D), f32), out((1, D), f32)],
         scratch_shapes=[
-            pltpu.VMEM((512, D), bf16),
-            pltpu.VMEM((D, 512), bf16),
-            pltpu.VMEM((D, 512), bf16),
-            pltpu.VMEM((512, 2 * FFB), f32),
-            pltpu.VMEM((512, FFB), f32),
-            pltpu.VMEM((512, FFB), bf16),
-            pltpu.VMEM((512, 2 * FFB), bf16),
-            pltpu.VMEM((512, D), f32),
-            pltpu.VMEM((2, D, 3 * FFB), bf16),
-            pltpu.VMEM((2, D, 3 * FFB), bf16),
-            pltpu.SemaphoreType.DMA((1,)),
-            pltpu.SemaphoreType.DMA((2,)),
+            v(2, D, 3 * FFB),
+            v(wide, rl, 3 * FFB) if rl % 16 else v(16, 128),
+            v(4, 256, D),
+            v(4, 128, D),
+            vf(4, 32, 128),
+            vf(8, 2048),
+            v(LEN, D),
+            vf(512, LEN),
+            vf(TILES, 128, 128),
+            vf(256, LEN),
+            vf(512, D),
+            v(512, D),
+            v(D, 512),
+            v(2, 256, D),
+            v(D, 512),
+            vf(512, 2 * FFB),
+            vf(512, FFB),
+            v(512, FFB),
+            v(512, 2 * FFB),
+            vf(512, D),
+            v(2, D, 3 * FFB),
+            v(2, D, 3 * FFB),
+            sem((6,)),
+            sem((10,)),
+            sem((10,)),
+            sem((2, wide)),
+            sem((2,)),
+            sem((5, wide)),
+            sem((5, wide)),
+            sem((4, wide)),
+            sem((4, wide)),
+            sem((4, 2, wide)),
+            sem((4, 2, wide)),
+            sem((4, 2, wide)),
+            sem((4, 2, wide)),
+            sem((2,)),
+            sem((2,)),
+            sem((2,)),
         ],
-        compiler_params=params(2),
-        cost_estimate=cost(30),
-        name="feed",
-    )(h2, cf, w, gain)
+        compiler_params=pltpu.CompilerParams(
+            dimension_semantics=("arbitrary",), vmem_limit_bytes=FORWARD_VMEM, collective_id=0, has_side_effects=True
+        ),
+        cost_estimate=cost(60),
+        name="forward",
+    )(ps_s, vl_s, hid, enc, cot, tab, hot, ps, pc, pf, gain_s, gain_c, gain_f)
 
 
 def cross_backward_kernel(
@@ -437,11 +793,11 @@
     late = pl.ds(D, D)
     loads = [
         pltpu.make_async_copy(gff.at[:, :, :, mine], o1, load.at[0]),
-        pltpu.make_async_copy(gff.at[y, :, :, late], o2, load.at[1]),
+        pltpu.make_async_copy(gff.at[0, :, :, late], o2, load.at[1]),
     ]
     sends = [
         remote(gff.at[:, :, :, other], rx, fs.at[0], fr.at[0], (1 - d, wi, me)),
-        remote(gff.at[1 - y, :, :, late], ry, fs.at[1], fr.at[1], (d, wi, yn)),
+        remote(gff.at[1, :, :, late], ry, fs.at[1], fr.at[1], (d, wi, yn)),
     ]
 
     @pl.when(n == 0)
@@ -584,14 +940,14 @@
     late = pl.ds(512, 256)
     loads = [
         pltpu.make_async_copy(gcr.at[:, :, :, mine], c1, load.at[0]),
-        pltpu.make_async_copy(gcr.at[y, :, :, late], c2, load.at[1]),
-        pltpu.make_async_copy(o1.at[y], s1, load.at[2]),
+        pltpu.make_async_copy(gcr.at[0, :, :, late], c2, load.at[1]),
+        pltpu.make_async_copy(o1.at[0], s1, load.at[2]),
         pltpu.make_async_copy(o2.at[wi], f2, load.at[3]),
     ]
     sends = [
-        remote(o1.at[1 - y], ry1, fs.at[0], fr.at[0], (d, wi, yn)),
+        remote(o1.at[1], ry1, fs.at[0], fr.at[0], (d, wi, yn)),
         remote(gcr.at[:, :, :, other], rx, fs.at[1], fr.at[1], (1 - d, wi, me)),
-        remote(gcr.at[1 - y, :, :, late], ry, fs.at[2], fr.at[2], (d, wi, yn)),
+        remote(gcr.at[1, :, :, late], ry, fs.at[2], fr.at[2], (d, wi, yn)),
     ]
 
     def zcopy(path, k):
@@ -780,220 +1136,6 @@
     )(xf, d1, w, gain, q, kv, at, p, gcr.reshape(2, wide, rl, D), o1, o2)
 
 
-def gather_kernel(
-    wide, hid, enc, cot, tab, ps, pc, pf, xf, ef, cf, tabs, gs, gc, gf, ls, ins, inr, zs, zr, ys, yr, xs, xr, cs, cr
-):
-    d, w, n, pn, yn, dn = place_here()
-    y = n // 2
-    keep, give = (2 * y + 1, 3 - 2 * y), (2 * y, 2 - 2 * y)
-    groups = ((ps, gs, 0, 768, True), (pc, gc, 0, 768, True), (pf, gf, 0, 512, True), (pf, gf, 512, 1024, False))
-
-    def cols(s, which):
-        start, width, split = groups[s][2:]
-        if which == 2 or not split:
-            return pl.ds(start, width)
-        half = width // 2
-        pos = d if which == 0 else 1 - d
-        return pl.ds(pl.multiple_of(start + pos * half, 128), half)
-
-    def own(s, which):
-        return groups[s][0].at[:, cols(s, which)]
-
-    def spot(s, slab, row, which):
-        return groups[s][1].at[slab, row, :, cols(s, which)]
-
-    def zcopy(s, k):
-        return remote(own(s, 0), spot(s, keep[0], w, 0), zs.at[s, k], zr.at[s, w], (d, lax.rem(w + k, wide), n))
-
-    def zgot(s, row):
-        return remote(spot(s, keep[0], row, 0), spot(s, keep[0], row, 0), zs.at[s, 0], zr.at[s, row], (1 - d, w, n))
-
-    def ycopy(s, row, src):
-        return remote(src, spot(s, keep[0], row, 0), ys.at[s, row], yr.at[s, row], (d, w, yn))
-
-    def ygot(s, row):
-        return remote(spot(s, keep[1], row, 0), spot(s, keep[1], row, 0), ys.at[s, row], yr.at[s, row], (d, w, yn))
-
-    def xcopy(s, side, row):
-        ref = spot(s, keep[side], row, 0)
-        return remote(ref, ref, xs.at[s, side, row], xr.at[s, side, row], (1 - d, w, n))
-
-    def xgot(s, side, row):
-        ref = spot(s, keep[side], row, 1)
-        return remote(ref, ref, xs.at[s, side, row], xr.at[s, side, row], (1 - d, w, n))
-
-    def ccopy(s, side, row, src=None):
-        ref = spot(s, keep[side], row, 2)
-        return remote(ref if src is None else src, spot(s, give[side], row, 2), cs.at[s, side, row], cr.at[s, side, row], (d, w, pn))
-
-    def cgot(s, side, row):
-        ref = spot(s, give[side], row, 2)
-        return remote(ref, ref, cs.at[s, side, row], cr.at[s, side, row], (d, w, pn))
-
-    local = [
-        pltpu.make_async_copy(src, dst, ls.at[i])
-        for i, (src, dst) in enumerate(
-            (
-                (ps, gs.at[keep[0], w]),
-                (pc, gc.at[keep[0], w]),
-                (pf, gf.at[keep[0], w]),
-                (hid.at[y], xf.at[n]),
-                (enc.at[y], ef.at[n]),
-                (cot.at[y], cf.at[0]),
-                (tab, tabs.at[keep[0]]),
-            )
-        )
-    ]
-    for copy in local:
-        copy.start()
-    diag, pair = (d, w, dn), (d, w, pn)
-    greet((pair, (d, w, yn), diag, (1 - d, w, n)), wide)
-    first = [
-        remote(hid.at[1 - y], xf.at[n], ins.at[0], inr.at[0], diag),
-        remote(enc.at[1 - y], ef.at[n], ins.at[1], inr.at[1], diag),
-        remote(cot.at[1 - y], cf.at[1], ins.at[2], inr.at[2], diag),
-        remote(tab, tabs.at[give[0]], ins.at[3], inr.at[3], pair),
-        remote(tab, tabs.at[keep[0]], ins.at[4], inr.at[4], (d, w, yn)),
-        remote(tab, tabs.at[give[0]], ins.at[5], inr.at[5], diag),
-        remote(hid.at[y], xf.at[n], ins.at[6], inr.at[6], pair),
-        remote(enc.at[y], ef.at[n], ins.at[7], inr.at[7], pair),
-    ]
-    got = [
-        remote(xf.at[dn], xf.at[dn], ins.at[0], inr.at[0], diag),
-        remote(ef.at[dn], ef.at[dn], ins.at[1], inr.at[1], diag),
-        remote(cf.at[1], cf.at[1], ins.at[2], inr.at[2], diag),
-        remote(tabs.at[give[0]], tabs.at[give[0]], ins.at[3], inr.at[3], pair),
-        remote(tabs.at[keep[1]], tabs.at[keep[1]], ins.at[4], inr.at[4], (d, w, yn)),
-        remote(tabs.at[give[1]], tabs.at[give[1]], ins.at[5], inr.at[5], diag),
-        remote(xf.at[pn], xf.at[pn], ins.at[6], inr.at[6], pair),
-        remote(ef.at[pn], ef.at[pn], ins.at[7], inr.at[7], pair),
-        remote(xf.at[yn], xf.at[yn], ins.at[8], inr.at[8], pair),
-        remote(ef.at[yn], ef.at[yn], ins.at[9], inr.at[9], pair),
-    ]
-    later = [
-        remote(xf.at[dn], xf.at[dn], ins.at[8], inr.at[8], pair),
-        remote(ef.at[dn], ef.at[dn], ins.at[9], inr.at[9], pair),
-    ]
-    for copy in first:
-        copy.start()
-    for s in range(4):
-        loop(1, wide, lambda k, s=s: zcopy(s, k).start())
-        ycopy(s, w, own(s, 0)).start()
-        ccopy(s, 0, w, own(s, 2)).start()
-    got[0].wait_recv()
-    later[0].start()
-    got[1].wait_recv()
-    later[1].start()
-
-    def zstep(s):
-        def one(k):
-            row = lax.rem(w + k, wide)
-            zgot(s, row).wait_recv()
-            ycopy(s, row, spot(s, keep[0], row, 0)).start()
-            if groups[s][4]:
-                xcopy(s, 0, row).start()
-            else:
-                ccopy(s, 0, row).start()
-
-        loop(1, wide, one)
-
-    def ystep(s):
-        def one(k):
-            row = lax.rem(w + k, wide)
-            ygot(s, row).wait_recv()
-            if groups[s][4]:
-                xcopy(s, 1, row).start()
-            else:
-                ccopy(s, 1, row).start()
-
-        loop(0, wide, one)
-
-    def xstep(s):
-        def one(side):
-            def step(k):
-                row = lax.rem(w + k, wide)
-                xgot(s, side, row).wait_recv()
-                ccopy(s, side, row).start()
-
-            return step
-
-        loop(1, wide, one(0))
-        loop(0, wide, one(1))
-
-    zstep(0)
-    ystep(0)
-    zstep(1)
-    ystep(1)
-    xstep(0)
-    zstep(2)
-    ystep(2)
-    xstep(1)
-    zstep(3)
-    ystep(3)
-    xstep(2)
-    for copy in got[2:]:
-        copy.wait_recv()
-    for copy in local:
-        copy.wait()
-    for copy in first + later:
-        copy.wait_send()
-
-    def finish(k):
-        row = lax.rem(w + k, wide)
-        for s in range(4):
-            for side in range(2):
-                cgot(s, side, row).wait_recv()
-                ccopy(s, side, row).wait_send()
-            ycopy(s, row, spot(s, keep[0], row, 0)).wait_send()
-            if groups[s][4]:
-                xcopy(s, 1, row).wait_send()
-
-    loop(0, wide, finish)
-
-    def finish_line(k):
-        row = lax.rem(w + k, wide)
-        for s in range(4):
-            zcopy(s, k).wait_send()
-            if groups[s][4]:
-                xcopy(s, 0, row).wait_send()
-
-    loop(1, wide, finish_line)
-
-
-def gather(wide, hid, enc, cot, tab, ps, pc, pf):
-    rl = ps.shape[0]
-    sem = pltpu.SemaphoreType.DMA
-    return pl.pallas_call(
-        partial(gather_kernel, wide),
-        in_specs=[ANY] * 7,
-        out_specs=[ANY] * 7,
-        out_shape=[
-            out((4, 256, D), bf16),
-            out((4, 128, D), bf16),
-            out((2, 256, D), bf16),
-            out((4, 32, 128), f32),
-            out((4, wide, rl, D), bf16),
-            out((4, wide, rl, D), bf16),
-            out((4, wide, rl, 2 * D), bf16),
-        ],
-        scratch_shapes=[
-            sem((7,)),
-            sem((10,)),
-            sem((10,)),
-            sem((4, wide)),
-            sem((4, wide)),
-            sem((4, wide)),
-            sem((4, wide)),
-            sem((4, 2, wide)),
-            sem((4, 2, wide)),
-            sem((4, 2, wide)),
-            sem((4, 2, wide)),
-        ],
-        compiler_params=pltpu.CompilerParams(collective_id=0, has_side_effects=True),
-        name="gather",
-    )(hid, enc, cot, tab, ps, pc, pf)
-
-
 def reduce_kernel(
     wide, se, c1, c2, e1, e2, outp, gxo, gxp, geo, gep, xf, d1, gain, gfeed, gcross, tg,
     out_o, gin_o, gen_o, sg_o, st_o, ff_o, cr_o, se_o,
@@ -1009,8 +1151,8 @@
     late = pl.ds(512, 256)
     loads = [
         pltpu.make_async_copy(se.at[:, :, :, mine], a1, load.at[0]),
-        pltpu.make_async_copy(se.at[y, :, :, late], a2, load.at[1]),
-        pltpu.make_async_copy(c1.at[y], b1, load.at[2]),
+        pltpu.make_async_copy(se.at[0, :, :, late], a2, load.at[1]),
+        pltpu.make_async_copy(c1.at[0], b1, load.at[2]),
         pltpu.make_async_copy(geo, tmp_en, load.at[3]),
         pltpu.make_async_copy(outp.at[0], out_o.at[y], load.at[4]),
     ]
@@ -1020,8 +1162,8 @@
     turn = lambda i, src, dst, dev: remote(src, dst, ts.at[i], tr.at[i], dev)
     put = [
         turn(0, se.at[:, :, :, other], rx, line_x),
-        turn(1, c1.at[1 - y], cy1, line_y),
-        turn(2, se.at[1 - y, :, :, late], ry, line_y),
+        turn(1, c1.at[1], cy1, line_y),
+        turn(2, se.at[1, :, :, late], ry, line_y),
         turn(3, e1, x1, line_x),
         turn(4, e2, x2, line_x),
     ]
@@ -1036,7 +1178,7 @@
     def zcopy(path, k):
         row = lax.rem(w + k, wide)
         src, dst = z_refs[path]
-        src = src.at[y, row] if path == 0 else src.at[row]
+        src = src.at[0, row] if path == 0 else src.at[row]
         return remote(src, dst.at[w], zs.at[path, k], zr.at[path, w], (d, row, n))
 
     def zgot(path, k):
@@ -1137,7 +1279,7 @@
     loads[0].wait()
     put[0].wait_recv()
     add_into(a1, rx)
-    y1 = turn(5, a1.at[1 - y], ry1, line_y)
+    y1 = turn(5, a1.at[1], ry1, line_y)
     y1.start()
 
     def keep(ref, cols):
@@ -1159,7 +1301,7 @@
     rl = e1.shape[0]
 
     def add_side(k):
-        a1[y, k] = a1[y, k] + ry1[k]
+        a1[0, k] = a1[0, k] + ry1[k]
 
     loop(0, wide, add_side)
     zstart(0)
@@ -1204,7 +1346,7 @@
     cr_o[:, other] = xc1[...].astype(f32)
     cr_o[:, late] = fc[:, late].astype(f32) + xc2[...].astype(f32)
     zwait(0)
-    sum_line(wide, a1.at[y, w], rzs1, keep(fs, mine))
+    sum_line(wide, a1.at[0, w], rzs1, keep(fs, mine))
     f_s1 = turn(9, fs.at[:, mine], xs1, line_x)
     f_s1.start()
     out_got.wait_recv()
@@ -1236,7 +1378,7 @@
     v = lambda *shape: pltpu.VMEM(shape, bf16)
     return pl.pallas_call(
         partial(reduce_kernel, wide),
-        in_specs=[ANY, ANY, V, V, V, ANY, V, ANY, ANY, ANY, V, V, V, V, V, V],
+        in_specs=[ANY, ANY, V, V, V, V, V, ANY, ANY, ANY, V, V, V, V, V, V],
         out_specs=[ANY, ANY, ANY, V, V, V, V, V],
         out_shape=[
             out((2, 256, D), bf16),
@@ -1304,33 +1446,27 @@
     gain_self, gain_cross, gain_feed, relative_bias, *mats
 ):
     me = lax.axis_index("narrow")
-    micro = me // 2
     sq, sk, sv, so, cq, ck, cv, co, gate, up, down = mats
     ps = jnp.concatenate((sq, so, sk, sv), axis=1)
     pc = jnp.concatenate((cq, co, ck, cv), axis=1)
     pf = jnp.concatenate((gate, up, down), axis=1)
     tab = jnp.pad(relative_bias.T, ((0, 29), (0, 96)))
-    xf, ef, cf, tabs, ws, wc, wf = gather(
-        wide, hidden_in[:, 0], encoder_out[:, 0], cotangent[:, 0], tab, ps, pc, pf
+    padded = jnp.pad(bucket_table, (0, 1), constant_values=-1)
+    hot = (padded[None, :] == jnp.arange(BUCKETS)[:, None]).astype(f32)
+    gains = [g.reshape(1, D) for g in (gain_self, gain_cross, gain_feed)]
+    (
+        xf, ws, wc, _, gff, ef, q, kv, at, p, cqh, ckv, cat, cp, h1, outp, d2, gg_feed,
+    ) = forward(
+        wide, piece_starts, valid_lengths, hidden_in[:, 0], encoder_out[:, 0], cotangent[:, 0], tab, hot, ps, pc, pf, *gains
     )
-    ws, wc, wf = (g.reshape(4, D, g.shape[-1]) for g in (ws, wc, wf))
-    xs, es, cs = xf.reshape(LEN, D), ef.reshape(ENC, D), cf.reshape(512, D)
-    table = tabs[:, :3, :32].reshape(12, 32)
-    one_hot = (bucket_table[:, None] == jnp.arange(BUCKETS)[None, :]).astype(f32)
-    off = lax.dot_general(table, one_hot, (((1,), (1,)), ((), ())), precision=precise)
-    off = jnp.pad(off, ((0, 0), (0, 1))).reshape(4, 3, 2048)
-    info = jnp.stack([piece_starts[micro, 0], valid_lengths[micro, 0]])
-    gains = [g.reshape(1, D) for g in (gain_self, gain_cross, gain_feed)]
-
-    q, kv, at, p, h1 = self_forward(info, xs, ws, off, gains[0])
-    cq, ckv, cat, cp, h2 = cross_forward(h1, es, wc, gains[1])
-    gff, outp, d2, gg_feed = feed(h2, cs, wf, gains[2])
-    gcr, d1, gg_cross, geo, gep, o1, o2 = cross_backward(wide, h1, es, d2, wc, gains[1], cq, ckv, cat, cp, gff)
+    ws, wc = (g.reshape(4, D, D) for g in (ws, wc))
+    xs, es = xf.reshape(LEN, D), ef.reshape(ENC, D)
+    gcr, d1, gg_cross, geo, gep, o1, o2 = cross_backward(wide, h1, es, d2, wc, gains[1], cqh, ckv, cat, cp, gff)
     gse, gxo, gxp, dl, c1, c2, e1, e2 = self_backward(wide, xs, d1, ws, gains[0], q, kv, at, p, gcr, o1, o2)
-
-    dl = jnp.where(me % 2 == 1, dl, dl.reshape(2, 2, 3, 2048)[:, ::-1].reshape(4, 3, 2048))
-    doff = dl.reshape(12, 2048)[:, :2047]
-    tg = lax.dot_general(one_hot, doff, (((0,), (1,)), ((), ())), precision=precise)
+    tg = lax.dot_general(hot, dl.reshape(12, 2048), (((1,), (1,)), ((), ())), precision=precise)
+    order = jnp.arange(12) // 3 ^ me ^ 1
+    tg = tg.reshape(BUCKETS, 4, 3)
+    tg = sum(jnp.where(order == k, jnp.tile(tg[:, k], (1, 4)), 0.0) for k in range(4))
     tg = jnp.pad(tg, ((0, 0), (0, 116)))
     two = lambda a: a.reshape(2, -1, D)
     outs, gin, gen, sg, st, f, b, a = reduce_all(

time: 368 us -> 307 us (0.83)
  Pallas kernels: 338 us -> 284 us
  local copies, waits for them, and re-layouts: 20.6 us -> 16.2 us
    pallas_call x4 -> x1, Pallas kernels: 185 us -> 128 us  [forward(): pl.pallas_call(partial(forward_kernel, wide), grid=(12,), in_specs=[SMEM,...]
where the time goes in v3:
time: 307 us; the launch traced here: 306 us
  Pallas kernels  284 us (93%)
  local copies, waits for them, and re-layouts  16.2 us (5%)
  other arithmetic  3.89 us (1%)
    pallas_call x1, Pallas kernels, forward(): pl.pallas_call(partial(forward_kernel, wide), grid=(12,), in_specs=[SMEM,...  128 us
    pallas_call x1, Pallas kernels, reduce_all(): pl.pallas_call(partial(reduce_kernel, wide), in_specs=[ANY, ANY, V, V, V,...  72.1 us
    pallas_call x1, Pallas kernels, self_backward(): pl.pallas_call(partial(self_backward_kernel, wide), grid=(4,), in_specs=[...  46.4 us
    pallas_call x1, Pallas kernels, cross_backward(): pl.pallas_call(cross_backward_kernel, grid=(4,), in_specs=[whole((512, D)...  37.4 us

profile of v3, /device:TPU:0, one launch (start us, length us, event | category | flops | bytes accessed | tf_op | source)
XLA Modules:
  0.0 306.0 jit_solution(17813331367605737337)
XLA Ops:
  0.7 0.0 copy-start.9
  0.7 0.0 copy-start.7
  0.7 0.0 copy-start.6
  0.7 0.0 copy-start.5
  0.7 0.0 copy-start.11
  0.7 0.0 copy-start.10
  0.7 0.0 copy-start.12
  0.7 0.0 copy-start.13
  0.7 1.4 reshape.105.gain_s.gain
  2.1 2.3 pad_maximum_fusion.1
  4.4 0.7 pad.13
  5.1 0.7 fusion.1.hot
  5.8 0.0 copy-done.9
  5.8 0.6 reshape.106.gain_c.gain
  6.4 0.0 copy-done.7
  6.4 0.0 copy-done.6
  6.4 0.0 copy-done.5
  6.4 0.9 pad_maximum_fusion.pf
  7.3 0.0 copy-done.11
  7.3 0.6 pad.12.tab
  7.9 0.0 copy-done.10
  7.9 0.6 reshape.107.gain_f
  8.4 0.0 copy-done.12
  8.4 0.6 copy.50.ps_s
  9.1 0.0 copy-done.13
  9.1 0.6 copy.51.vl_s
  9.7 128.0 %forward.1 = (bf16[4,256,768]{2,1,0:T(8,128)(2,1)}, bf16[4,4,192,768]{3,2,1,0:T(8,128)(2,1)}, bf16[4,4,192,768]{3,2,1,0:T(8,128)(2,1)}, bf16[4,4,192,1536]{3,2,1...) custom-call(s32[2,1]{1,0:T(2,128)} %copy.50.ps_s, ...), custom_call_target="tpu_custom_call" | custom-call | flops 60000002048 | bytes 20971520 | tf_op jit(solution)/shard_map/forward/pallas_call | solution.py:705
  137.8 37.4 %cross_backward.1 = (bf16[2,768,768]{2,1,0:T(8,128)(2,1)}, f32[512,768]{1,0:T(8,128)}, f32[1,768]{1,0:T(1,128)}, f32[256,768]{1,0:T(8,128)}, bf16[256,768]{1,0:T...) custom-call(f32[512,768]{1,0:T(8,128)} %get-tuple-element.59.h1, bf16[512,768]{1,0:T(8,128)(2,1)} %bitcast.72, ...), custom_call_target="tpu_custom_call" | custom-call | flops 14000000000 | bytes 20971520 | tf_op jit(solution)/shard_map/cross_backward/pallas_call | solution.py:866
  175.2 46.4 %self_backward.1 = (bf16[2,768,768]{2,1,0:T(8,128)(2,1)}, f32[512,768]{1,0:T(8,128)}, bf16[512,768]{1,0:T(8,128)(2,1)}, f32[4,3,2048]{2,1,0:T(4,128)}, bf16[2,4,...) custom-call(bf16[1024,768]{1,0:T(8,128)(2,1)} %bitcast.50, ...), custom_call_target="tpu_custom_call" | custom-call | flops 24999999488 | bytes 20971520 | tf_op jit(solution)/shard_map/self_backward/pallas_call | solution.py:1068
  221.6 1.2 fusion.2
  222.8 0.1 copy.53
  222.9 0.1 copy.54
  223.0 0.1 copy.55
  223.1 0.1 copy.56
  223.3 0.6 pad.14.tg
  223.9 72.1 %reduce_all.1 = (bf16[2,256,768]{2,1,0:T(8,128)(2,1)}, f32[2,256,768]{2,1,0:T(8,128)}, f32[2,128,768]{2,1,0:T(8,128)}, f32[8,768]{1,0:T(8,128)}, f32[32,128]{1,0...) custom-call(bf16[2,4,192,768]{3,2,1,0:T(8,128)(2,1)} %bitcast.49, ...), custom_call_target="tpu_custom_call" | custom-call | tf_op jit(solution)/shard_map/reduce_all/pallas_call | solution.py:1379
  296.0 0.0 copy-start.2
  296.0 0.0 copy-start.1
  296.0 2.4 fusion.8
  298.4 1.0 fusion.10
  299.4 1.0 fusion.9
  300.3 0.1 constant_dynamic-slice_fusion
  300.4 0.7 copy.60
  301.1 1.5 slice_reduce_fusion
  302.6 0.9 copy.78
  303.4 1.1 copy.79
  304.6 0.5 copy-done.3
  305.1 0.9 copy.80
  (25 shorter events, 0.1 us)
Async XLA Ops:
  0.7 5.1 %copy-start.9 = (f32[768]{0:T(1024)S(1)}, f32[768]{0:T(1024)}, u32[]{:S(2)}) copy-start(f32[768]{0:T(1024)} %param.28) | copy-start | bytes 9220
  0.7 5.7 %copy-start.7 = (bf16[192,512]{1,0:T(8,128)(2,1)S(1)}, bf16[192,512]{1,0:T(8,128)(2,1)}, u32[]{:S(2)}) copy-start(bf16[192,512]{1,0:T(8,128)(2,1)} %param.39) | copy-start | bytes 589828
  0.7 5.7 %copy-start.6 = (bf16[192,512]{1,0:T(8,128)(2,1)S(1)}, bf16[192,512]{1,0:T(8,128)(2,1)}, u32[]{:S(2)}) copy-start(bf16[192,512]{1,0:T(8,128)(2,1)} %param.40) | copy-start | bytes 589828
  0.7 5.7 %copy-start.5 = (bf16[192,512]{1,0:T(8,128)(2,1)S(1)}, bf16[192,512]{1,0:T(8,128)(2,1)}, u32[]{:S(2)}) copy-start(bf16[192,512]{1,0:T(8,128)(2,1)} %param.41) | copy-start | bytes 589828
  0.7 6.6 %copy-start.11 = (f32[32,3]{0,1:T(4,128)S(1)}, f32[32,3]{0,1:T(4,128)}, u32[]{:S(2)}) copy-start(f32[32,3]{0,1:T(4,128)} %param.30) | copy-start | bytes 1156
  0.7 7.2 %copy-start.10 = (f32[768]{0:T(1024)S(1)}, f32[768]{0:T(1024)}, u32[]{:S(2)}) copy-start(f32[768]{0:T(1024)} %param.29) | copy-start | bytes 9220
  0.7 7.7 %copy-start.12 = (s32[2,1]{0,1:T(1,128)S(1)}, s32[2,1]{0,1:T(1,128)}, u32[]{:S(2)}) copy-start(s32[2,1]{0,1:T(1,128)} %param.24) | copy-start | bytes 28
  0.7 8.4 %copy-start.13 = (s32[2,1]{0,1:T(1,128)S(1)}, s32[2,1]{0,1:T(1,128)}, u32[]{:S(2)}) copy-start(s32[2,1]{0,1:T(1,128)} %param.25) | copy-start | bytes 28
  296.0 2.4 copy-start.2
  296.0 3.4 %copy-start.1 = (f32[192,768]{1,0:T(8,128)S(1)}, f32[192,768]{1,0:T(8,128)}, u32[]{:S(2)}) copy-start(f32[192,768]{1,0:T(8,128)} %get-tuple-element.96) | copy-start | bytes 1769476
  298.4 2.0 copy-start.8
  298.4 4.2 %copy-start.4 = (bf16[2,256,768]{2,1,0:T(8,128)(2,1)S(1)}, bf16[2,256,768]{2,1,0:T(8,128)(2,1)}, u32[]{:S(2)}) copy-start(bf16[2,256,768]{2,1,0:T(8,128)(2,1)} %get-tuple-element.90) | copy-start | bytes 2359300
  299.4 4.1 %copy-start = (f32[2,256,768]{2,1,0:T(8,128)S(1)}, f32[2,256,768]{2,1,0:T(8,128)}, u32[]{:S(2)}) copy-start(f32[2,256,768]{2,1,0:T(8,128)} %get-tuple-element.91) | copy-start | bytes 4718596
  303.4 1.7 copy-start.3

commit v4 on v3

--- a/solution.py
+++ b/solution.py
@@ -402,15 +402,6 @@
         zsend(0)
         own_sends(0)
         tabs[1] = tab[...]
-        arrived(6, xv.at[pn])
-        arrived(0, xv.at[dn])
-        later[0].start()
-        arrived(8, xv.at[yn])
-        local[3].wait()
-        back[0].start()
-        arrived(3, tabs.at[0])
-        arrived(4, tabs.at[3])
-        arrived(5, tabs.at[2])
         start, length = ps_s[y, 0], vl_s[y, 0]
         for i in range(2):
 
@@ -422,21 +413,31 @@
                 allowed = ((kj <= qi) | inside) & (kj < length)
                 mask[pl.ds(i * 256 + r.start, 32), :] = jnp.where(allowed, 0.0, masked_value)
 
-            rows_loop(256, 32, mask_rows)
+            rows_loop(256, 32, mask_rows, unroll=2)
+        arrived(6, xv.at[pn])
+        arrived(0, xv.at[dn])
+        later[0].start()
+        zpass(0, (lambda row: ycopy(0, row), lambda row: xcopy(0, 0, row)))
+        zsend(1)
+        arrived(8, xv.at[yn])
+        local[3].wait()
+        back[0].start()
+        arrived(3, tabs.at[0])
+        arrived(4, tabs.at[3])
+        arrived(5, tabs.at[2])
         for i in range(4):
 
             def norm_rows(r, i=i):
                 nf[pl.ds(i * 256 + r.start, 64), :] = normed(xv[i, r, :].astype(f32), gain_s[...]).astype(bf16)
 
-            rows_loop(256, 64, norm_rows)
+            rows_loop(256, 64, norm_rows, unroll=4)
         for i in range(2):
             h1[i * 256 : (i + 1) * 256, :] = xv[blks[i]].astype(f32)
-        zpass(0, (lambda row: ycopy(0, row), lambda row: xcopy(0, 0, row)))
-        zsend(1)
+        xstep(0, 0)
+        ypass(0)
         own_sends(1)
         middle[0].start()
         middle[1].start()
-        xstep(0, 0)
         for i in range(3):
             local[i].wait()
         fetch(gs, 1, 0)
@@ -479,7 +480,6 @@
     def _():
         cwait(0, 0)
         fetch(gs, 0, 1)
-        ypass(0)
         zpass(1, (lambda row: ycopy(1, row),))
         zsend(2)
         own_sends(2)
@@ -520,7 +520,7 @@
             nc[r, :] = normed(x, gain_c[...]).astype(bf16)
             h2[r, :] = x
 
-        rows_loop(512, 64, norm_rows)
+        rows_loop(512, 64, norm_rows, unroll=4)
 
     @pl.when((step >= 4) & (step < 8))
     def _():
@@ -570,7 +570,7 @@
             acc[r, :] = x
             d2_o[r, :] = jnp.zeros((64, D), f32)
 
-        rows_loop(512, 64, norm_rows)
+        rows_loop(512, 64, norm_rows, unroll=4)
         nct[...] = nc[...].T
         ct[...] = cv[...].reshape(512, D).T
 
@@ -812,7 +812,7 @@
         greet(((d, wi, pn), (d, wi, yn), (1 - d, wi, me)))
         for copy in sends:
             copy.start()
-        rows_loop(512, 64, norm_rows)
+        rows_loop(512, 64, norm_rows, unroll=4)
         nct[...] = dp[...].astype(bf16).T
         d2t[...] = d2b[...].T
         eft[...] = ef[...].T
@@ -847,7 +847,7 @@
             d1_o[r, :] = d2[r, :] + dx
             gg_o[...] += gg
 
-        rows_loop(512, 64, back_rows)
+        rows_loop(512, 64, back_rows, unroll=2)
         for i in range(2):
             half = slice(i * 128, (i + 1) * 128)
             cols = lambda blk: pl.ds(pl.multiple_of(blk * 128, 128), 128)
@@ -924,9 +924,9 @@
 
 
 def self_backward_kernel(
-    wide, xf, d1, w, gain, q, kv, at, p, gcr, o1, o2,
-    gw_o, g_o, gp_o, dl_o, c1, c2, e1, e2,
-    d1b, d1t, nft, nqt, gt, gq, do, dp, ds, dq, dkv, buf, landed, s1, f2, rx, ry, ry1, rz1, rz2,
+    wide, xf, d1, w, gain, q, kv, at, p, gcr, o1, o2, outp,
+    gw_o, g_o, gp_o, dl_o, b1, c2, e1, e2, out_o,
+    c1, cy1, d1b, d1t, nft, nqt, gt, gq, do, dp, ds, dq, dkv, buf, landed, s1, f2, rx, ry, ry1, rz1, rz2,
     send, recv, load, fs, fr, zs, zr,
 ):
     n = pl.program_id(0)
@@ -943,12 +943,16 @@
         pltpu.make_async_copy(gcr.at[0, :, :, late], c2, load.at[1]),
         pltpu.make_async_copy(o1.at[0], s1, load.at[2]),
         pltpu.make_async_copy(o2.at[wi], f2, load.at[3]),
+        pltpu.make_async_copy(outp.at[0], out_o.at[y], load.at[4]),
     ]
     sends = [
         remote(o1.at[1], ry1, fs.at[0], fr.at[0], (d, wi, yn)),
         remote(gcr.at[:, :, :, other], rx, fs.at[1], fr.at[1], (1 - d, wi, me)),
         remote(gcr.at[1, :, :, late], ry, fs.at[2], fr.at[2], (d, wi, yn)),
+        remote(outp.at[1], out_o.at[y], fs.at[3], fr.at[3], (d, wi, dn)),
     ]
+    out_got = remote(out_o.at[1 - y], out_o.at[1 - y], fs.at[3], fr.at[3], (d, wi, dn))
+    y_cross = remote(c1.at[1], cy1, fs.at[4], fr.at[4], (d, wi, yn))
 
     def zcopy(path, k):
         row = lax.rem(wi + k, wide)
@@ -968,8 +972,8 @@
 
         for copy in loads:
             copy.start()
-        greet(((d, wi, pn), (d, wi, yn), (1 - d, wi, me)), wide)
-        for copy in sends:
+        greet(((d, wi, pn), (d, wi, yn), (1 - d, wi, me), (d, wi, dn)), wide)
+        for copy in sends[:3]:
             copy.start()
         loop(1, wide, lambda k: zcopy(1, k).start())
         rows_loop(512, 64, cast_rows)
@@ -988,6 +992,14 @@
         sends[0].wait_recv()
         add_into(s1, ry1)
         loop(1, wide, lambda k: zcopy(0, k).start())
+        sends[3].start()
+
+    @pl.when(n == 3)
+    def _():
+        loads[0].wait()
+        sends[1].wait_recv()
+        add_into(c1, rx)
+        y_cross.start()
 
     dl_o[0] = jnp.zeros((3, 2048), f32)
     do[...] = nn(d1b[...], w[0, :, 192:384]).astype(bf16)
@@ -1039,9 +1051,6 @@
             half = slice(i * 256, (i + 1) * 256)
             g_o[half, :] = gq[half, :] + gt[:, block_rows(blks[i])].T
             gp_o[half, :] = gt[:, block_rows((pn, 3 - pn)[i])].T.astype(bf16)
-        loads[0].wait()
-        sends[1].wait_recv()
-        add_into(c1, rx)
         loads[1].wait()
         sends[2].wait_recv()
         add_into(c2, ry)
@@ -1057,13 +1066,21 @@
 
         sum_line(wide, s1.at[wi], rz1, put(e1))
         sum_line(wide, f2, rz2, put(e2))
-        for copy in sends:
+        y_cross.wait_recv()
+
+        def add_cross(k):
+            b1[k] = c1[0, k] + cy1[k]
+
+        loop(0, wide, add_cross)
+        out_got.wait_recv()
+        loads[4].wait()
+        for copy in (*sends, y_cross):
             copy.wait_send()
         for path in (0, 1):
             loop(1, wide, lambda k, path=path: zcopy(path, k).wait_send())
 
 
-def self_backward(wide, xf, d1, w, gain, q, kv, at, p, gcr, o1, o2):
+def self_backward(wide, xf, d1, w, gain, q, kv, at, p, gcr, o1, o2, outp):
     rl = D // wide
     return pl.pallas_call(
         partial(self_backward_kernel, wide),
@@ -1080,28 +1097,33 @@
             ANY,
             ANY,
             ANY,
+            pl.BlockSpec(memory_space=pltpu.VMEM),
         ],
         out_specs=[
             pair_slab((D, D)),
             whole((512, D)),
             whole((512, D)),
             slab((3, 2048)),
-            whole((2, wide, rl, 256)),
+            whole((wide, rl, 256)),
             whole((wide, rl, 256)),
             whole((rl, 384)),
             whole((rl, D)),
+            ANY,
         ],
         out_shape=[
             out((2, D, D), bf16),
             out((512, D), f32),
             out((512, D), bf16),
             out((4, 3, 2048), f32),
-            out((2, wide, rl, 256), bf16),
+            out((wide, rl, 256), bf16),
             out((wide, rl, 256), bf16),
             out((rl, 384), bf16),
             out((rl, D), bf16),
+            out((2, 256, D), bf16),
         ],
         scratch_shapes=[
+            pltpu.VMEM((2, wide, rl, 256), bf16),
+            pltpu.VMEM((wide, rl, 256), bf16),
             pltpu.VMEM((512, D), bf16),
             pltpu.VMEM((D, 512), bf16),
             pltpu.VMEM((D, LEN), bf16),
@@ -1124,22 +1146,22 @@
             pltpu.VMEM((wide, rl, D), bf16),
             pltpu.SemaphoreType.DMA((1,)),
             pltpu.SemaphoreType.DMA((2,)),
-            pltpu.SemaphoreType.DMA((4,)),
-            pltpu.SemaphoreType.DMA((3,)),
-            pltpu.SemaphoreType.DMA((3,)),
+            pltpu.SemaphoreType.DMA((5,)),
+            pltpu.SemaphoreType.DMA((5,)),
+            pltpu.SemaphoreType.DMA((5,)),
             pltpu.SemaphoreType.DMA((2, wide)),
             pltpu.SemaphoreType.DMA((2, wide)),
         ],
         compiler_params=params(4),
         cost_estimate=cost(25),
         name="self_backward",
-    )(xf, d1, w, gain, q, kv, at, p, gcr.reshape(2, wide, rl, D), o1, o2)
+    )(xf, d1, w, gain, q, kv, at, p, gcr.reshape(2, wide, rl, D), o1, o2, outp)
 
 
 def reduce_kernel(
-    wide, se, c1, c2, e1, e2, outp, gxo, gxp, geo, gep, xf, d1, gain, gfeed, gcross, tg,
-    out_o, gin_o, gen_o, sg_o, st_o, ff_o, cr_o, se_o,
-    a1, a2, rx, ry, ry1, cy1, b1, rzs1, rzs2, rzc1, rzc2, fs, fc, xs1, xs2, xc1, xc2, x1, x2,
+    wide, se, b1, c2, e1, e2, gxo, gxp, geo, gep, xf, d1, gain, gfeed, gcross, tg,
+    gin_o, gen_o, sg_o, st_o, ff_o, cr_o, se_o,
+    a1, a2, rx, ry, ry1, rzs1, rzs2, rzc1, rzc2, fs, fc, xs1, xs2, xc1, xc2, x1, x2,
     rgx, rge, tmp_in, tmp_en, back_in, back_en, rows_f, sg, st, rsg, rst, rsgz, rstz,
     load, ms, mr, ts, tr, zs, zr, ss, sr, os,
 ):
@@ -1152,9 +1174,7 @@
     loads = [
         pltpu.make_async_copy(se.at[:, :, :, mine], a1, load.at[0]),
         pltpu.make_async_copy(se.at[0, :, :, late], a2, load.at[1]),
-        pltpu.make_async_copy(c1.at[0], b1, load.at[2]),
-        pltpu.make_async_copy(geo, tmp_en, load.at[3]),
-        pltpu.make_async_copy(outp.at[0], out_o.at[y], load.at[4]),
+        pltpu.make_async_copy(geo, tmp_en, load.at[2]),
     ]
     for copy in loads:
         copy.start()
@@ -1162,7 +1182,6 @@
     turn = lambda i, src, dst, dev: remote(src, dst, ts.at[i], tr.at[i], dev)
     put = [
         turn(0, se.at[:, :, :, other], rx, line_x),
-        turn(1, c1.at[1], cy1, line_y),
         turn(2, se.at[1, :, :, late], ry, line_y),
         turn(3, e1, x1, line_x),
         turn(4, e2, x2, line_x),
@@ -1170,9 +1189,7 @@
     cross = [
         remote(gxp, rgx, ms.at[0], mr.at[0], pair),
         remote(gep, rge, ms.at[1], mr.at[1], pair),
-        remote(outp.at[1], out_o.at[y], ms.at[2], mr.at[2], diag),
     ]
-    out_got = remote(out_o.at[1 - y], out_o.at[1 - y], ms.at[2], mr.at[2], diag)
     z_refs = ((a1, rzs1), (a2, rzs2), (b1, rzc1), (c2, rzc2))
 
     def zcopy(path, k):
@@ -1196,11 +1213,10 @@
     cross[1].start()
     put[0].start()
     put[1].start()
+    zstart(3)
+    zstart(2)
     put[2].start()
-    zstart(3)
-    cross[2].start()
     put[3].start()
-    put[4].start()
 
     sg[...] = jnp.zeros((8, D), f32)
     sg[1:2, :] = gcross[...]
@@ -1227,7 +1243,7 @@
     in_local = pltpu.make_async_copy(rows_f.at[0], gin_o.at[y], os.at[0])
     in_local.start()
     cross[1].wait_recv()
-    loads[3].wait()
+    loads[2].wait()
     back_en[0] = (tmp_en[1] + rge[1].astype(f32)).astype(bf16)
     en_send = remote(back_en.at[0], back_en.at[1], ms.at[4], mr.at[4], diag)
     en_send.start()
@@ -1262,14 +1278,10 @@
     small_add(0, pair)
     start_all(small(1, line_y))
 
-    loads[2].wait()
-    put[1].wait_recv()
-    add_into(b1, cy1)
-    zstart(2)
     small_add(1, line_y)
     start_all(small(2, line_x))
     loads[1].wait()
-    put[2].wait_recv()
+    put[1].wait_recv()
     add_into(a2, ry)
     zstart(1)
     small_add(2, line_x)
@@ -1335,8 +1347,8 @@
 
     f_mine = pl.ds(pl.multiple_of(d * 384, 128), 384)
     f_other = pl.ds(pl.multiple_of(384 - d * 384, 128), 384)
+    put[2].wait_recv()
     put[3].wait_recv()
-    put[4].wait_recv()
     ff_o[:, f_mine] = e1[...].astype(f32)
     ff_o[:, f_other] = x1[...].astype(f32)
     ff_o[:, pl.ds(D, D)] = e2[...].astype(f32) + x2[...].astype(f32)
@@ -1349,14 +1361,13 @@
     sum_line(wide, a1.at[0, w], rzs1, keep(fs, mine))
     f_s1 = turn(9, fs.at[:, mine], xs1, line_x)
     f_s1.start()
-    out_got.wait_recv()
     f_s2.wait_recv()
     se_o[:, mine] = fs[:, mine].astype(f32)
     se_o[:, late] = fs[:, late].astype(f32) + xs2[...].astype(f32)
     f_s1.wait_recv()
     se_o[:, other] = xs1[...].astype(f32)
 
-    for copy in (in_local, en_local, in_last, en_last, loads[4]):
+    for copy in (in_local, en_local, in_last, en_last):
         copy.wait()
     for copy in (*cross, in_send, en_send, *put, y1, f_c1, f_c2, f_s1, f_s2):
         copy.wait_send()
@@ -1370,7 +1381,7 @@
     loop(1, wide, finish)
 
 
-def reduce_all(wide, se, c1, c2, e1, e2, outp, gxo, gxp, geo, gep, xf, d1, gain, gfeed, gcross, tg):
+def reduce_all(wide, se, b1, c2, e1, e2, gxo, gxp, geo, gep, xf, d1, gain, gfeed, gcross, tg):
     rl = D // wide
     se = se.reshape(2, wide, rl, D)
     sem = pltpu.SemaphoreType.DMA
@@ -1378,10 +1389,9 @@
     v = lambda *shape: pltpu.VMEM(shape, bf16)
     return pl.pallas_call(
         partial(reduce_kernel, wide),
-        in_specs=[ANY, ANY, V, V, V, V, V, ANY, ANY, ANY, V, V, V, V, V, V],
-        out_specs=[ANY, ANY, ANY, V, V, V, V, V],
+        in_specs=[ANY, V, V, V, V, V, ANY, ANY, ANY, V, V, V, V, V, V],
+        out_specs=[ANY, ANY, V, V, V, V, V],
         out_shape=[
-            out((2, 256, D), bf16),
             out((2, 256, D), f32),
             out((2, 128, D), f32),
             out((8, D), f32),
@@ -1394,8 +1404,6 @@
             v(2, wide, rl, 256),
             v(wide, rl, 256),
             v(2, wide, rl, 256),
-            v(wide, rl, 256),
-            v(wide, rl, 256),
             v(wide, rl, 256),
             v(wide, rl, 256),
             v(wide, rl, 256),
@@ -1438,7 +1446,7 @@
             collective_id=1, has_side_effects=True, vmem_limit_bytes=VMEM_LIMIT
         ),
         name="reduce_all",
-    )(se, c1, c2, e1, e2, outp, gxo, gxp, geo, gep, xf, d1, gain, gfeed, gcross, tg)
+    )(se, b1, c2, e1, e2, gxo, gxp, geo, gep, xf, d1, gain, gfeed, gcross, tg)
 
 
 def on_device(
@@ -1462,15 +1470,17 @@
     ws, wc = (g.reshape(4, D, D) for g in (ws, wc))
     xs, es = xf.reshape(LEN, D), ef.reshape(ENC, D)
     gcr, d1, gg_cross, geo, gep, o1, o2 = cross_backward(wide, h1, es, d2, wc, gains[1], cqh, ckv, cat, cp, gff)
-    gse, gxo, gxp, dl, c1, c2, e1, e2 = self_backward(wide, xs, d1, ws, gains[0], q, kv, at, p, gcr, o1, o2)
+    gse, gxo, gxp, dl, b1, c2, e1, e2, outs = self_backward(
+        wide, xs, d1, ws, gains[0], q, kv, at, p, gcr, o1, o2, outp.reshape(2, 256, D)
+    )
     tg = lax.dot_general(hot, dl.reshape(12, 2048), (((1,), (1,)), ((), ())), precision=precise)
     order = jnp.arange(12) // 3 ^ me ^ 1
     tg = tg.reshape(BUCKETS, 4, 3)
     tg = sum(jnp.where(order == k, jnp.tile(tg[:, k], (1, 4)), 0.0) for k in range(4))
     tg = jnp.pad(tg, ((0, 0), (0, 116)))
     two = lambda a: a.reshape(2, -1, D)
-    outs, gin, gen, sg, st, f, b, a = reduce_all(
-        wide, gse, c1, c2, e1, e2, two(outp), two(gxo), two(gxp), two(geo), two(gep), xf, two(d1), gains[0], gg_feed, gg_cross, tg
+    gin, gen, sg, st, f, b, a = reduce_all(
+        wide, gse, b1, c2, e1, e2, two(gxo), two(gxp), two(geo), two(gep), xf, two(d1), gains[0], gg_feed, gg_cross, tg
     )
     tg = lax.dynamic_slice_in_dim(st, me * 3, 3, axis=1)
     return (

time: 307 us -> 288 us (0.938)
  Pallas kernels: 284 us -> 265 us
    pallas_call x1, Pallas kernels: 72.1 us -> 55.6 us  [reduce_all(): pl.pallas_call(partial(reduce_kernel, wide), in_specs=[ANY, V, V, V, V, V...]
where the time goes in v4:
time: 288 us; the launch traced here: 287 us
  Pallas kernels  265 us (92%)
  local copies, waits for them, and re-layouts  16.2 us (6%)
  other arithmetic  3.89 us (1%)
    pallas_call x1, Pallas kernels, forward(): pl.pallas_call(partial(forward_kernel, wide), grid=(12,), in_specs=[SMEM,...  126 us
    pallas_call x1, Pallas kernels, reduce_all(): pl.pallas_call(partial(reduce_kernel, wide), in_specs=[ANY, V, V, V, V, V...  55.6 us
    pallas_call x1, Pallas kernels, self_backward(): pl.pallas_call(partial(self_backward_kernel, wide), grid=(4,), in_specs=[...  47.7 us
    pallas_call x1, Pallas kernels, cross_backward(): pl.pallas_call(cross_backward_kernel, grid=(4,), in_specs=[whole((512, D)...  35.9 us

profile of v4, /device:TPU:0, one launch (start us, length us, event | category | flops | bytes accessed | tf_op | source)
XLA Modules:
  0.0 287.3 jit_solution(13988541474935185261)
XLA Ops:
  0.7 0.0 copy-start.9
  0.7 0.0 copy-start.7
  0.7 0.0 copy-start.6
  0.7 0.0 copy-start.5
  0.7 0.0 copy-start.11
  0.7 0.0 copy-start.10
  0.7 0.0 copy-start.12
  0.7 0.0 copy-start.13
  0.7 1.4 reshape.105.gain_s.gain
  2.1 2.3 pad_maximum_fusion.1
  4.4 0.7 pad.13
  5.1 0.7 fusion.1.hot
  5.8 0.0 copy-done.9
  5.8 0.6 reshape.106.gain_c.gain
  6.4 0.0 copy-done.7
  6.4 0.0 copy-done.6
  6.4 0.0 copy-done.5
  6.4 0.9 pad_maximum_fusion.pf
  7.3 0.0 copy-done.11
  7.3 0.6 pad.12.tab
  7.9 0.0 copy-done.10
  7.9 0.6 reshape.107.gain_f
  8.4 0.0 copy-done.12
  8.4 0.6 copy.50.ps_s
  9.1 0.0 copy-done.13
  9.1 0.6 copy.51.vl_s
  9.7 126.0 %forward.1 = (bf16[4,256,768]{2,1,0:T(8,128)(2,1)}, bf16[4,4,192,768]{3,2,1,0:T(8,128)(2,1)}, bf16[4,4,192,768]{3,2,1,0:T(8,128)(2,1)}, bf16[4,4,192,1536]{3,2,1...) custom-call(s32[2,1]{1,0:T(2,128)} %copy.50.ps_s, ...), custom_call_target="tpu_custom_call" | custom-call | flops 60000002048 | bytes 20971520 | tf_op jit(solution)/shard_map/forward/pallas_call | solution.py:705
  135.7 35.9 %cross_backward.1 = (bf16[2,768,768]{2,1,0:T(8,128)(2,1)}, f32[512,768]{1,0:T(8,128)}, f32[1,768]{1,0:T(1,128)}, f32[256,768]{1,0:T(8,128)}, bf16[256,768]{1,0:T...) custom-call(f32[512,768]{1,0:T(8,128)} %get-tuple-element.59.h1, bf16[512,768]{1,0:T(8,128)(2,1)} %bitcast.72, ...), custom_call_target="tpu_custom_call" | custom-call | flops 14000000000 | bytes 20971520 | tf_op jit(solution)/shard_map/cross_backward/pallas_call | solution.py:866
  171.6 47.7 %self_backward.1 = (bf16[2,768,768]{2,1,0:T(8,128)(2,1)}, f32[512,768]{1,0:T(8,128)}, bf16[512,768]{1,0:T(8,128)(2,1)}, f32[4,3,2048]{2,1,0:T(4,128)}, bf16[4,19...) custom-call(bf16[1024,768]{1,0:T(8,128)(2,1)} %bitcast.50, ...), custom_call_target="tpu_custom_call" | custom-call | flops 24999999488 | bytes 20971520 | tf_op jit(solution)/shard_map/self_backward/pallas_call | solution.py:1085
  219.4 1.2 fusion.2
  220.6 0.1 copy.53
  220.7 0.1 copy.54
  220.8 0.1 copy.55
  220.9 0.1 copy.56
  221.1 0.6 pad.14.tg
  221.7 55.6 %reduce_all.1 = (f32[2,256,768]{2,1,0:T(8,128)}, f32[2,128,768]{2,1,0:T(8,128)}, f32[8,768]{1,0:T(8,128)}, f32[32,128]{1,0:T(8,128)}, f32[192,1536]{1,0:T(8,128)...) custom-call(bf16[2,4,192,768]{3,2,1,0:T(8,128)(2,1)} %bitcast.49, bf16[4,192,256]{2,1,0:T(8,128)(2,1)} %get-tuple-element.80.b1, ...), custom_call_target="tpu_custom_call" | custom-call | tf_op jit(solution)/shard_map/reduce_all/pallas_call | solution.py:1390
  277.3 0.0 copy-start.2
  277.3 0.0 copy-start.1
  277.3 2.4 fusion.8
  279.7 1.0 fusion.10
  280.7 1.0 fusion.9
  281.7 0.1 constant_dynamic-slice_fusion
  281.8 0.7 copy.60
  282.4 1.5 slice_reduce_fusion
  283.9 0.9 copy.78
  284.8 1.1 copy.79
  285.9 0.5 copy-done.4
  286.5 0.9 copy.80
  (25 shorter events, 0.1 us)
Async XLA Ops:
  0.7 5.1 %copy-start.9 = (f32[768]{0:T(1024)S(1)}, f32[768]{0:T(1024)}, u32[]{:S(2)}) copy-start(f32[768]{0:T(1024)} %param.28) | copy-start | bytes 9220
  0.7 5.7 %copy-start.7 = (bf16[192,512]{1,0:T(8,128)(2,1)S(1)}, bf16[192,512]{1,0:T(8,128)(2,1)}, u32[]{:S(2)}) copy-start(bf16[192,512]{1,0:T(8,128)(2,1)} %param.39) | copy-start | bytes 589828
  0.7 5.7 %copy-start.6 = (bf16[192,512]{1,0:T(8,128)(2,1)S(1)}, bf16[192,512]{1,0:T(8,128)(2,1)}, u32[]{:S(2)}) copy-start(bf16[192,512]{1,0:T(8,128)(2,1)} %param.40) | copy-start | bytes 589828
  0.7 5.7 %copy-start.5 = (bf16[192,512]{1,0:T(8,128)(2,1)S(1)}, bf16[192,512]{1,0:T(8,128)(2,1)}, u32[]{:S(2)}) copy-start(bf16[192,512]{1,0:T(8,128)(2,1)} %param.41) | copy-start | bytes 589828
  0.7 6.6 %copy-start.11 = (f32[32,3]{0,1:T(4,128)S(1)}, f32[32,3]{0,1:T(4,128)}, u32[]{:S(2)}) copy-start(f32[32,3]{0,1:T(4,128)} %param.30) | copy-start | bytes 1156
  0.7 7.2 %copy-start.10 = (f32[768]{0:T(1024)S(1)}, f32[768]{0:T(1024)}, u32[]{:S(2)}) copy-start(f32[768]{0:T(1024)} %param.29) | copy-start | bytes 9220
  0.7 7.7 %copy-start.12 = (s32[2,1]{0,1:T(1,128)S(1)}, s32[2,1]{0,1:T(1,128)}, u32[]{:S(2)}) copy-start(s32[2,1]{0,1:T(1,128)} %param.24) | copy-start | bytes 28
  0.7 8.4 %copy-start.13 = (s32[2,1]{0,1:T(1,128)S(1)}, s32[2,1]{0,1:T(1,128)}, u32[]{:S(2)}) copy-start(s32[2,1]{0,1:T(1,128)} %param.25) | copy-start | bytes 28
  277.3 2.4 copy-start.2
  277.3 3.4 %copy-start.1 = (f32[192,768]{1,0:T(8,128)S(1)}, f32[192,768]{1,0:T(8,128)}, u32[]{:S(2)}) copy-start(f32[192,768]{1,0:T(8,128)} %get-tuple-element.96) | copy-start | bytes 1769476
  279.7 2.0 copy-start.8
  279.7 4.2 %copy-start.3 = (bf16[2,256,768]{2,1,0:T(8,128)(2,1)S(1)}, bf16[2,256,768]{2,1,0:T(8,128)(2,1)}, u32[]{:S(2)}) copy-start(bf16[2,256,768]{2,1,0:T(8,128)(2,1)} %get-tuple-element.78) | copy-start | bytes 2359300
  280.7 4.1 %copy-start = (f32[2,256,768]{2,1,0:T(8,128)S(1)}, f32[2,256,768]{2,1,0:T(8,128)}, u32[]{:S(2)}) copy-start(f32[2,256,768]{2,1,0:T(8,128)} %get-tuple-element.91) | copy-start | bytes 4718596
  284.8 1.7 copy-start.4

commit v5 on v4

--- a/solution.py
+++ b/solution.py
@@ -779,22 +779,33 @@
 
 
 def cross_backward_kernel(
-    h1, ef, d2, w, gain, q, kv, at, p, gff,
-    gw_o, d1_o, gg_o, ge_o, gep_o, o1, o2,
-    d2b, d2t, nct, eft, get, do, dp, ds, dq, dkv, buf, landed, rx, ry, send, recv, load, fs, fr,
+    wide, h1, ef, d2, w, gain, q, kv, at, p, gff,
+    gw_o, d1_o, gg_o, ge_o, gep_o, o1, o2, o3,
+    d2b, d2t, nct, eft, get, do, dp, ds, dq, dkv, buf, landed, rx, ry, rz, send, recv, load, fs, fr, zs, zr,
 ):
     n = pl.program_id(0)
     slot = lax.rem(n, 2)
     core = CoreSum(n, buf, landed, send, recv)
     d, wi, me, pn, yn, dn = place_here()
     y = me // 2
-    mine = pl.ds(pl.multiple_of(d * 384, 128), 384)
-    other = pl.ds(pl.multiple_of(384 - d * 384, 128), 384)
-    late = pl.ds(D, D)
+    mine = pl.ds(pl.multiple_of(d * 256, 128), 256)
+    other = pl.ds(pl.multiple_of(256 - d * 256, 128), 256)
+    late = pl.ds(512, 640)
+    third = pl.ds(1152, 384)
     loads = [
         pltpu.make_async_copy(gff.at[:, :, :, mine], o1, load.at[0]),
         pltpu.make_async_copy(gff.at[0, :, :, late], o2, load.at[1]),
+        pltpu.make_async_copy(gff.at[:, wi, :, third], o3, load.at[2]),
     ]
+
+    def zcopy(k):
+        row = lax.rem(wi + k, wide)
+        return remote(gff.at[:, row, :, third], rz.at[wi], zs.at[k], zr.at[wi], (d, row, me))
+
+    def zgot(k):
+        row = lax.rem(wi + k, wide)
+        return remote(rz.at[row], rz.at[row], zs.at[k], zr.at[row], (d, row, me))
+
     sends = [
         remote(gff.at[:, :, :, other], rx, fs.at[0], fr.at[0], (1 - d, wi, me)),
         remote(gff.at[1, :, :, late], ry, fs.at[1], fr.at[1], (d, wi, yn)),
@@ -809,9 +820,10 @@
 
         for copy in loads:
             copy.start()
-        greet(((d, wi, pn), (d, wi, yn), (1 - d, wi, me)))
+        greet(((d, wi, pn), (d, wi, yn), (1 - d, wi, me)), wide)
         for copy in sends:
             copy.start()
+        loop(1, wide, lambda k: zcopy(k).start())
         rows_loop(512, 64, norm_rows, unroll=4)
         nct[...] = dp[...].astype(bf16).T
         d2t[...] = d2b[...].T
@@ -859,12 +871,24 @@
             copy.wait()
         add_into(o1, rx)
         add_into(o2, ry)
+        loop(1, wide, lambda k: zgot(k).wait_recv())
+        rl = o3.shape[1]
+        part = 64 if rl % 64 == 0 else rl
+        for i in range(2):
+            for j in range(rl // part):
+                r = slice(j * part, (j + 1) * part)
+
+                def add(k, total, i=i, r=r):
+                    return total + rz[lax.rem(wi + k, wide), i, r, :].astype(f32)
+
+                o3[i, r, :] = lax.fori_loop(1, wide, add, o3[i, r, :].astype(f32)).astype(bf16)
+        loop(1, wide, lambda k: zcopy(k).wait_send())
 
 
 def cross_backward(wide, h1, ef, d2, w, gain, q, kv, at, p, gff):
     rl = D // wide
     return pl.pallas_call(
-        cross_backward_kernel,
+        partial(cross_backward_kernel, wide),
         grid=(4,),
         in_specs=[
             whole((512, D)),
@@ -884,8 +908,9 @@
             whole((1, D)),
             whole((256, D)),
             whole((256, D)),
-            whole((2, wide, rl, 384)),
-            whole((wide, rl, D)),
+            whole((2, wide, rl, 256)),
+            whole((wide, rl, 640)),
+            whole((2, rl, 384)),
         ],
         out_shape=[
             out((2, D, D), bf16),
@@ -893,8 +918,9 @@
             out((1, D), f32),
             out((256, D), f32),
             out((256, D), bf16),
-            out((2, wide, rl, 384), bf16),
-            out((wide, rl, D), bf16),
+            out((2, wide, rl, 256), bf16),
+            out((wide, rl, 640), bf16),
+            out((2, rl, 384), bf16),
         ],
         scratch_shapes=[
             pltpu.VMEM((512, D), bf16),
@@ -909,13 +935,16 @@
             pltpu.VMEM((2 * HD, ENC), bf16),
             pltpu.VMEM((2, D, D), bf16),
             pltpu.VMEM((2, D, D), bf16),
-            pltpu.VMEM((2, wide, rl, 384), bf16),
-            pltpu.VMEM((wide, rl, D), bf16),
+            pltpu.VMEM((2, wide, rl, 256), bf16),
+            pltpu.VMEM((wide, rl, 640), bf16),
+            pltpu.VMEM((wide, 2, rl, 384), bf16),
             pltpu.SemaphoreType.DMA((1,)),
             pltpu.SemaphoreType.DMA((2,)),
+            pltpu.SemaphoreType.DMA((3,)),
             pltpu.SemaphoreType.DMA((2,)),
             pltpu.SemaphoreType.DMA((2,)),
-            pltpu.SemaphoreType.DMA((2,)),
+            pltpu.SemaphoreType.DMA((wide,)),
+            pltpu.SemaphoreType.DMA((wide,)),
         ],
         compiler_params=params(3),
         cost_estimate=cost(14),
@@ -924,9 +953,9 @@
 
 
 def self_backward_kernel(
-    wide, xf, d1, w, gain, q, kv, at, p, gcr, o1, o2, outp,
+    wide, xf, d1, w, gain, q, kv, at, p, gcr, o1, o2, o3, outp,
     gw_o, g_o, gp_o, dl_o, b1, c2, e1, e2, out_o,
-    c1, cy1, d1b, d1t, nft, nqt, gt, gq, do, dp, ds, dq, dkv, buf, landed, s1, f2, rx, ry, ry1, rz1, rz2,
+    c1, cy1, d1b, d1t, nft, nqt, gt, gq, do, dp, ds, dq, dkv, buf, landed, s1, f2, s3, rx, ry, ry1, ry3, rz1, rz2,
     send, recv, load, fs, fr, zs, zr,
 ):
     n = pl.program_id(0)
@@ -944,6 +973,7 @@
         pltpu.make_async_copy(o1.at[0], s1, load.at[2]),
         pltpu.make_async_copy(o2.at[wi], f2, load.at[3]),
         pltpu.make_async_copy(outp.at[0], out_o.at[y], load.at[4]),
+        pltpu.make_async_copy(o3.at[0], s3, load.at[5]),
     ]
     sends = [
         remote(o1.at[1], ry1, fs.at[0], fr.at[0], (d, wi, yn)),
@@ -953,6 +983,7 @@
     ]
     out_got = remote(out_o.at[1 - y], out_o.at[1 - y], fs.at[3], fr.at[3], (d, wi, dn))
     y_cross = remote(c1.at[1], cy1, fs.at[4], fr.at[4], (d, wi, yn))
+    y_third = remote(o3.at[1], ry3, fs.at[5], fr.at[5], (d, wi, yn))
 
     def zcopy(path, k):
         row = lax.rem(wi + k, wide)
@@ -986,16 +1017,17 @@
             nqt[:, i * 256 : (i + 1) * 256] = part.T
         gt[...] = jnp.zeros((D, LEN), f32)
 
+    @pl.when(n == 1)
+    def _():
+        sends[3].start()
+        y_third.start()
+
     @pl.when(n == 2)
     def _():
         loads[2].wait()
         sends[0].wait_recv()
         add_into(s1, ry1)
         loop(1, wide, lambda k: zcopy(0, k).start())
-        sends[3].start()
-
-    @pl.when(n == 3)
-    def _():
         loads[0].wait()
         sends[1].wait_recv()
         add_into(c1, rx)
@@ -1058,14 +1090,17 @@
         for path in (1, 0):
             loop(1, wide, lambda k, path=path: zgot(path, k).wait_recv())
 
-        def put(ref):
+        def put(ref, cols):
             def store(r, total):
-                ref[r, :] = total.astype(bf16)
+                ref[r, cols] = total.astype(bf16)
 
             return store
 
-        sum_line(wide, s1.at[wi], rz1, put(e1))
-        sum_line(wide, f2, rz2, put(e2))
+        sum_line(wide, s1.at[wi], rz1, put(e1, slice(None)))
+        sum_line(wide, f2, rz2, put(e2, slice(0, 640)))
+        loads[5].wait()
+        y_third.wait_recv()
+        e2[:, 640:1024] = s3[...] + ry3[...]
         y_cross.wait_recv()
 
         def add_cross(k):
@@ -1074,13 +1109,13 @@
         loop(0, wide, add_cross)
         out_got.wait_recv()
         loads[4].wait()
-        for copy in (*sends, y_cross):
+        for copy in (*sends, y_cross, y_third):
             copy.wait_send()
         for path in (0, 1):
             loop(1, wide, lambda k, path=path: zcopy(path, k).wait_send())
 
 
-def self_backward(wide, xf, d1, w, gain, q, kv, at, p, gcr, o1, o2, outp):
+def self_backward(wide, xf, d1, w, gain, q, kv, at, p, gcr, o1, o2, o3, outp):
     rl = D // wide
     return pl.pallas_call(
         partial(self_backward_kernel, wide),
@@ -1097,6 +1132,7 @@
             ANY,
             ANY,
             ANY,
+            ANY,
             pl.BlockSpec(memory_space=pltpu.VMEM),
         ],
         out_specs=[
@@ -1106,8 +1142,8 @@
             slab((3, 2048)),
             whole((wide, rl, 256)),
             whole((wide, rl, 256)),
-            whole((rl, 384)),
-            whole((rl, D)),
+            whole((rl, 256)),
+            whole((rl, 1024)),
             ANY,
         ],
         out_shape=[
@@ -1117,8 +1153,8 @@
             out((4, 3, 2048), f32),
             out((wide, rl, 256), bf16),
             out((wide, rl, 256), bf16),
-            out((rl, 384), bf16),
-            out((rl, D), bf16),
+            out((rl, 256), bf16),
+            out((rl, 1024), bf16),
             out((2, 256, D), bf16),
         ],
         scratch_shapes=[
@@ -1137,25 +1173,27 @@
             pltpu.VMEM((2 * HD, LEN), bf16),
             pltpu.VMEM((2, D, D), bf16),
             pltpu.VMEM((2, D, D), bf16),
-            pltpu.VMEM((wide, rl, 384), bf16),
-            pltpu.VMEM((rl, D), bf16),
+            pltpu.VMEM((wide, rl, 256), bf16),
+            pltpu.VMEM((rl, 640), bf16),
+            pltpu.VMEM((rl, 384), bf16),
             pltpu.VMEM((2, wide, rl, 256), bf16),
             pltpu.VMEM((wide, rl, 256), bf16),
-            pltpu.VMEM((wide, rl, 384), bf16),
-            pltpu.VMEM((wide, rl, 384), bf16),
-            pltpu.VMEM((wide, rl, D), bf16),
+            pltpu.VMEM((wide, rl, 256), bf16),
+            pltpu.VMEM((rl, 384), bf16),
+            pltpu.VMEM((wide, rl, 256), bf16),
+            pltpu.VMEM((wide, rl, 640), bf16),
             pltpu.SemaphoreType.DMA((1,)),
             pltpu.SemaphoreType.DMA((2,)),
-            pltpu.SemaphoreType.DMA((5,)),
-            pltpu.SemaphoreType.DMA((5,)),
-            pltpu.SemaphoreType.DMA((5,)),
+            pltpu.SemaphoreType.DMA((6,)),
+            pltpu.SemaphoreType.DMA((6,)),
+            pltpu.SemaphoreType.DMA((6,)),
             pltpu.SemaphoreType.DMA((2, wide)),
             pltpu.SemaphoreType.DMA((2, wide)),
         ],
         compiler_params=params(4),
         cost_estimate=cost(25),
         name="self_backward",
-    )(xf, d1, w, gain, q, kv, at, p, gcr.reshape(2, wide, rl, D), o1, o2, outp)
+    )(xf, d1, w, gain, q, kv, at, p, gcr.reshape(2, wide, rl, D), o1, o2, o3, outp)
 
 
 def reduce_kernel(
@@ -1215,8 +1253,6 @@
     put[1].start()
     zstart(3)
     zstart(2)
-    put[2].start()
-    put[3].start()
 
     sg[...] = jnp.zeros((8, D), f32)
     sg[1:2, :] = gcross[...]
@@ -1277,22 +1313,23 @@
     start_all(small(0, pair))
     small_add(0, pair)
     start_all(small(1, line_y))
-
-    small_add(1, line_y)
-    start_all(small(2, line_x))
     loads[1].wait()
     put[1].wait_recv()
     add_into(a2, ry)
     zstart(1)
-    small_add(2, line_x)
-    loop(1, wide, lambda k: start_all(small_line(k)))
-    rsgz[w] = sg[...]
-    rstz[w] = st[...]
     loads[0].wait()
     put[0].wait_recv()
     add_into(a1, rx)
     y1 = turn(5, a1.at[1], ry1, line_y)
     y1.start()
+    put[2].start()
+    put[3].start()
+    small_add(1, line_y)
+    start_all(small(2, line_x))
+    small_add(2, line_x)
+    loop(1, wide, lambda k: start_all(small_line(k)))
+    rsgz[w] = sg[...]
+    rstz[w] = st[...]
 
     def keep(ref, cols):
         def store(r, total):
@@ -1345,13 +1382,11 @@
     en_last = pltpu.make_async_copy(tmp_en.at[1], gen_o.at[1 - y], os.at[3])
     en_last.start()
 
-    f_mine = pl.ds(pl.multiple_of(d * 384, 128), 384)
-    f_other = pl.ds(pl.multiple_of(384 - d * 384, 128), 384)
     put[2].wait_recv()
     put[3].wait_recv()
-    ff_o[:, f_mine] = e1[...].astype(f32)
-    ff_o[:, f_other] = x1[...].astype(f32)
-    ff_o[:, pl.ds(D, D)] = e2[...].astype(f32) + x2[...].astype(f32)
+    ff_o[:, mine] = e1[...].astype(f32)
+    ff_o[:, other] = x1[...].astype(f32)
+    ff_o[:, pl.ds(512, 1024)] = e2[...].astype(f32) + x2[...].astype(f32)
     f_c1.wait_recv()
     f_c2.wait_recv()
     cr_o[:, mine] = fc[:, mine].astype(f32)
@@ -1416,8 +1451,8 @@
             v(rl, 256),
             v(rl, 256),
             v(rl, 256),
-            v(rl, 384),
-            v(rl, D),
+            v(rl, 256),
+            v(rl, 1024),
             v(2, 256, D),
             v(2, 128, D),
             v(256, D),
@@ -1469,9 +1504,9 @@
     )
     ws, wc = (g.reshape(4, D, D) for g in (ws, wc))
     xs, es = xf.reshape(LEN, D), ef.reshape(ENC, D)
-    gcr, d1, gg_cross, geo, gep, o1, o2 = cross_backward(wide, h1, es, d2, wc, gains[1], cqh, ckv, cat, cp, gff)
+    gcr, d1, gg_cross, geo, gep, o1, o2, o3 = cross_backward(wide, h1, es, d2, wc, gains[1], cqh, ckv, cat, cp, gff)
     gse, gxo, gxp, dl, b1, c2, e1, e2, outs = self_backward(
-        wide, xs, d1, ws, gains[0], q, kv, at, p, gcr, o1, o2, outp.reshape(2, 256, D)
+        wide, xs, d1, ws, gains[0], q, kv, at, p, gcr, o1, o2, o3, outp.reshape(2, 256, D)
     )
     tg = lax.dot_general(hot, dl.reshape(12, 2048), (((1,), (1,)), ((), ())), precision=precise)
     order = jnp.arange(12) // 3 ^ me ^ 1

time: 288 us -> 284 us (0.986)
  Pallas kernels: 265 us -> 261 us
    pallas_call x1, Pallas kernels: 35.9 us -> 32 us  [cross_backward(): pl.pallas_call(partial(cross_backward_kernel, wide), grid=(4,), in_specs=...]
    pallas_call x1, Pallas kernels: 47.7 us -> 51.1 us  [self_backward(): pl.pallas_call(partial(self_backward_kernel, wide), grid=(4,), in_specs=[...]
    pallas_call x1, Pallas kernels: 55.6 us -> 52.4 us  [reduce_all(): pl.pallas_call(partial(reduce_kernel, wide), in_specs=[ANY, V, V, V, V, V...]
where the time goes in v5:
time: 284 us
  Pallas kernels  261 us (92%)
  local copies, waits for them, and re-layouts  16.2 us (6%)
  other arithmetic  3.89 us (1%)
    pallas_call x1, Pallas kernels, forward(): pl.pallas_call(partial(forward_kernel, wide), grid=(12,), in_specs=[SMEM,...  126 us
    pallas_call x1, Pallas kernels, reduce_all(): pl.pallas_call(partial(reduce_kernel, wide), in_specs=[ANY, V, V, V, V, V...  52.4 us
    pallas_call x1, Pallas kernels, self_backward(): pl.pallas_call(partial(self_backward_kernel, wide), grid=(4,), in_specs=[...  51.1 us
    pallas_call x1, Pallas kernels, cross_backward(): pl.pallas_call(partial(cross_backward_kernel, wide), grid=(4,), in_specs=...  32 us

profile of v5, /device:TPU:0, one launch (start us, length us, event | category | flops | bytes accessed | tf_op | source)
XLA Modules:
  0.0 283.5 jit_solution(16265842167588417207)
XLA Ops:
  0.7 0.0 copy-start.9
  0.7 0.0 copy-start.7
  0.7 0.0 copy-start.6
  0.7 0.0 copy-start.5
  0.7 0.0 copy-start.11
  0.7 0.0 copy-start.10
  0.7 0.0 copy-start.12
  0.7 0.0 copy-start.13
  0.7 1.4 reshape.105.gain_s.gain
  2.1 2.3 pad_maximum_fusion.1
  4.4 0.7 pad.13
  5.1 0.7 fusion.1.hot
  5.8 0.0 copy-done.9
  5.8 0.6 reshape.106.gain_c.gain
  6.4 0.0 copy-done.7
  6.4 0.0 copy-done.6
  6.4 0.0 copy-done.5
  6.4 0.9 pad_maximum_fusion.pf
  7.3 0.0 copy-done.11
  7.3 0.6 pad.12.tab
  7.9 0.0 copy-done.10
  7.9 0.6 reshape.107.gain_f
  8.4 0.0 copy-done.12
  8.4 0.6 copy.50.ps_s
  9.1 0.6 copy.51.vl_s
  9.7 126.0 %forward.1 = (bf16[4,256,768]{2,1,0:T(8,128)(2,1)}, bf16[4,4,192,768]{3,2,1,0:T(8,128)(2,1)}, bf16[4,4,192,768]{3,2,1,0:T(8,128)(2,1)}, bf16[4,4,192,1536]{3,2,1...) custom-call(s32[2,1]{1,0:T(2,128)} %copy.50.ps_s, ...), custom_call_target="tpu_custom_call" | custom-call | flops 60000002048 | bytes 20971520 | tf_op jit(solution)/shard_map/forward/pallas_call | solution.py:705
  135.7 32.0 %cross_backward.1 = (bf16[2,768,768]{2,1,0:T(8,128)(2,1)}, f32[512,768]{1,0:T(8,128)}, f32[1,768]{1,0:T(1,128)}, f32[256,768]{1,0:T(8,128)}, bf16[256,768]{1,0:T...) custom-call(f32[512,768]{1,0:T(8,128)} %get-tuple-element.60.h1, ...), custom_call_target="tpu_custom_call" | custom-call | flops 14000000000 | bytes 20971520 | tf_op jit(solution)/shard_map/cross_backward/pallas_call | solution.py:890
  167.7 51.1 %self_backward.1 = (bf16[2,768,768]{2,1,0:T(8,128)(2,1)}, f32[512,768]{1,0:T(8,128)}, bf16[512,768]{1,0:T(8,128)(2,1)}, f32[4,3,2048]{2,1,0:T(4,128)}, bf16[4,19...) custom-call(bf16[1024,768]{1,0:T(8,128)(2,1)} %bitcast.50, ...), custom_call_target="tpu_custom_call" | custom-call | flops 24999999488 | bytes 20971520 | tf_op jit(solution)/shard_map/self_backward/pallas_call | solution.py:1120
  218.8 1.2 fusion.2
  220.0 0.1 copy.53
  220.1 0.1 copy.54
  220.3 0.1 copy.55
  220.4 0.1 copy.56
  220.5 0.6 pad.14.tg
  221.1 52.4 %reduce_all.1 = (f32[2,256,768]{2,1,0:T(8,128)}, f32[2,128,768]{2,1,0:T(8,128)}, f32[8,768]{1,0:T(8,128)}, f32[32,128]{1,0:T(8,128)}, f32[192,1536]{1,0:T(8,128)...) custom-call(bf16[2,4,192,768]{3,2,1,0:T(8,128)(2,1)} %bitcast.49, bf16[4,192,256]{2,1,0:T(8,128)(2,1)} %get-tuple-element.82.b1, ...), custom_call_target="tpu_custom_call" | custom-call | tf_op jit(solution)/shard_map/reduce_all/pallas_call | solution.py:1425
  273.5 0.0 copy-start.2
  273.5 0.0 copy-start.1
  273.6 2.4 fusion.8
  275.9 1.0 fusion.10
  276.9 1.0 fusion.9
  277.9 0.1 constant_dynamic-slice_fusion
  278.0 0.7 copy.60
  278.6 1.5 slice_reduce_fusion
  280.1 0.0 copy-done.3
  280.1 0.9 copy.78
  281.0 1.1 copy.79
  282.1 0.5 copy-done.4
  282.7 0.9 copy.80
  (25 shorter events, 0.1 us)
Async XLA Ops:
  0.7 5.1 %copy-start.9 = (f32[768]{0:T(1024)S(1)}, f32[768]{0:T(1024)}, u32[]{:S(2)}) copy-start(f32[768]{0:T(1024)} %param.28) | copy-start | bytes 9220
  0.7 5.7 %copy-start.7 = (bf16[192,512]{1,0:T(8,128)(2,1)S(1)}, bf16[192,512]{1,0:T(8,128)(2,1)}, u32[]{:S(2)}) copy-start(bf16[192,512]{1,0:T(8,128)(2,1)} %param.39) | copy-start | bytes 589828
  0.7 5.7 %copy-start.6 = (bf16[192,512]{1,0:T(8,128)(2,1)S(1)}, bf16[192,512]{1,0:T(8,128)(2,1)}, u32[]{:S(2)}) copy-start(bf16[192,512]{1,0:T(8,128)(2,1)} %param.40) | copy-start | bytes 589828
  0.7 5.7 %copy-start.5 = (bf16[192,512]{1,0:T(8,128)(2,1)S(1)}, bf16[192,512]{1,0:T(8,128)(2,1)}, u32[]{:S(2)}) copy-start(bf16[192,512]{1,0:T(8,128)(2,1)} %param.41) | copy-start | bytes 589828
  0.7 6.6 %copy-start.11 = (f32[32,3]{0,1:T(4,128)S(1)}, f32[32,3]{0,1:T(4,128)}, u32[]{:S(2)}) copy-start(f32[32,3]{0,1:T(4,128)} %param.30) | copy-start | bytes 1156
  0.7 7.2 %copy-start.10 = (f32[768]{0:T(1024)S(1)}, f32[768]{0:T(1024)}, u32[]{:S(2)}) copy-start(f32[768]{0:T(1024)} %param.29) | copy-start | bytes 9220
  0.7 7.7 %copy-start.12 = (s32[2,1]{0,1:T(1,128)S(1)}, s32[2,1]{0,1:T(1,128)}, u32[]{:S(2)}) copy-start(s32[2,1]{0,1:T(1,128)} %param.24) | copy-start | bytes 28
  0.7 8.4 %copy-start.13 = (s32[2,1]{0,1:T(1,128)S(1)}, s32[2,1]{0,1:T(1,128)}, u32[]{:S(2)}) copy-start(s32[2,1]{0,1:T(1,128)} %param.25) | copy-start | bytes 28
  273.5 2.4 copy-start.2
  273.5 3.4 %copy-start.1 = (f32[192,768]{1,0:T(8,128)S(1)}, f32[192,768]{1,0:T(8,128)}, u32[]{:S(2)}) copy-start(f32[192,768]{1,0:T(8,128)} %get-tuple-element.98) | copy-start | bytes 1769476
  275.9 2.0 copy-start.8
  275.9 4.2 %copy-start.3 = (bf16[2,256,768]{2,1,0:T(8,128)(2,1)S(1)}, bf16[2,256,768]{2,1,0:T(8,128)(2,1)}, u32[]{:S(2)}) copy-start(bf16[2,256,768]{2,1,0:T(8,128)(2,1)} %get-tuple-element.80) | copy-start | bytes 2359300
  276.9 4.1 %copy-start = (f32[2,256,768]{2,1,0:T(8,128)S(1)}, f32[2,256,768]{2,1,0:T(8,128)}, u32[]{:S(2)}) copy-start(f32[2,256,768]{2,1,0:T(8,128)} %get-tuple-element.93) | copy-start | bytes 4718596
  281.0 1.7 copy-start.4

commit v6 on v5

--- a/solution.py
+++ b/solution.py
@@ -228,7 +228,7 @@
 
 
 def forward_kernel(
-    wide, ps_s, vl_s, hid, enc, cot, tab, hot, ps, pc, pf, gain_s, gain_c, gain_f,
+    wide, ps_s, vl_s, hid, enc, cot, tab, hot, ps, pc, pf, gains,
     xf, gs, gc, gf, gff, ef, q1, kv1, at1, p1, q2, kv2, at2, p2, h1, out_o, d2_o, gg_o,
     wbuf, stage, xv, ev, tabs, off, nf, mask, tb, s, h2, nc, nct, cv, ct, gu, da, act, dgu, acc, buf, landed,
     ls, ins, inr, ws, vs, zs, zr, ys, yr, xs, xr, cs, cr, fsend, frecv, fout,
@@ -428,7 +428,7 @@
         for i in range(4):
 
             def norm_rows(r, i=i):
-                nf[pl.ds(i * 256 + r.start, 64), :] = normed(xv[i, r, :].astype(f32), gain_s[...]).astype(bf16)
+                nf[pl.ds(i * 256 + r.start, 64), :] = normed(xv[i, r, :].astype(f32), gains[0:1, :]).astype(bf16)
 
             rows_loop(256, 64, norm_rows, unroll=4)
         for i in range(2):
@@ -517,7 +517,7 @@
 
         def norm_rows(r):
             x = h1[r, :]
-            nc[r, :] = normed(x, gain_c[...]).astype(bf16)
+            nc[r, :] = normed(x, gains[1:2, :]).astype(bf16)
             h2[r, :] = x
 
         rows_loop(512, 64, norm_rows, unroll=4)
@@ -566,7 +566,7 @@
 
         def norm_rows(r):
             x = h2[r, :]
-            nc[r, :] = normed(x, gain_f[...]).astype(bf16)
+            nc[r, :] = normed(x, gains[2:3, :]).astype(bf16)
             acc[r, :] = x
             d2_o[r, :] = jnp.zeros((64, D), f32)
 
@@ -636,6 +636,7 @@
         give_copy(0).start()
         zpass(4, (lambda row: ccopy(3, 1, row),))
         xstep(2, 1)
+        fetch(gf, 3, 1)
         cwait(2, 1)
         cwait(3, 1)
         fetch(gf, 2, 0)
@@ -643,7 +644,6 @@
     @pl.when(step == 10)
     def _():
         give_copy(1).start()
-        fetch(gf, 3, 1)
         add_side(0)
 
     @pl.when(step == 11)
@@ -655,7 +655,7 @@
 
             def back_rows(r, i=i):
                 rows = pl.ds(i * 256 + r.start, 64)
-                dx, gg = norm_back(h2[rows, :], gain_f[...], d2_o[rows, :])
+                dx, gg = norm_back(h2[rows, :], gains[2:3, :], d2_o[rows, :])
                 d2_o[rows, :] = cv[i, r, :].astype(f32) + dx
                 gg_o[...] += gg
                 out_o[rows, :] = acc[rows, :].astype(bf16)
@@ -689,7 +689,7 @@
         loop(1, wide, finish_line)
 
 
-def forward(wide, ps_s, vl_s, hid, enc, cot, tab, hot, ps, pc, pf, gain_s, gain_c, gain_f):
+def forward(wide, ps_s, vl_s, hid, enc, cot, tab, hot, ps, pc, pf, gains):
     rl = ps.shape[0]
     sem = pltpu.SemaphoreType.DMA
     V = pl.BlockSpec(memory_space=pltpu.VMEM)
@@ -705,7 +705,7 @@
     return pl.pallas_call(
         partial(forward_kernel, wide),
         grid=(12,),
-        in_specs=[SMEM, SMEM, ANY, ANY, ANY, V, V, V, V, V, V, V, V],
+        in_specs=[SMEM, SMEM, ANY, ANY, ANY, V, V, V, V, V, V],
         out_specs=[ANY] * 6
         + [turn(0, (512, HD)), turn(0, (2 * HD, LEN)), turn(0, (512, HD)), turn(0, (3, 512, LEN))]
         + [turn(4, (512, HD)), turn(4, (2 * HD, ENC)), turn(4, (512, HD)), turn(4, (3, 512, ENC))]
@@ -775,7 +775,7 @@
         ),
         cost_estimate=cost(60),
         name="forward",
-    )(ps_s, vl_s, hid, enc, cot, tab, hot, ps, pc, pf, gain_s, gain_c, gain_f)
+    )(ps_s, vl_s, hid, enc, cot, tab, hot, ps, pc, pf, gains)
 
 
 def cross_backward_kernel(
@@ -816,7 +816,7 @@
         def norm_rows(r):
             d2b[r, :] = d2[r, :].astype(bf16)
             d1_o[r, :] = jnp.zeros((64, D), f32)
-            dp[r, :] = normed(h1[r, :], gain[...])
+            dp[r, :] = normed(h1[r, :], gain[1:2, :])
 
         for copy in loads:
             copy.start()
@@ -855,7 +855,7 @@
         gg_o[...] = jnp.zeros((1, D), f32)
 
         def back_rows(r):
-            dx, gg = norm_back(h1[r, :], gain[...], d1_o[r, :])
+            dx, gg = norm_back(h1[r, :], gain[1:2, :], d1_o[r, :])
             d1_o[r, :] = d2[r, :] + dx
             gg_o[...] += gg
 
@@ -895,7 +895,7 @@
             whole((ENC, D)),
             whole((512, D)),
             slab((D, D)),
-            whole((1, D)),
+            whole((3, D)),
             slab((512, HD)),
             slab((2 * HD, ENC)),
             slab((512, HD)),
@@ -1010,10 +1010,10 @@
         rows_loop(512, 64, cast_rows)
         d1t[...] = d1b[...].T
         for i in range(4):
-            part = normed(xf[i * 256 : (i + 1) * 256, :].astype(f32), gain[...]).astype(bf16)
+            part = normed(xf[i * 256 : (i + 1) * 256, :].astype(f32), gain[0:1, :]).astype(bf16)
             nft[:, i * 256 : (i + 1) * 256] = part.T
         for i in range(2):
-            part = normed(xf[block_rows(blks[i]), :].astype(f32), gain[...]).astype(bf16)
+            part = normed(xf[block_rows(blks[i]), :].astype(f32), gain[0:1, :]).astype(bf16)
             nqt[:, i * 256 : (i + 1) * 256] = part.T
         gt[...] = jnp.zeros((D, LEN), f32)
 
@@ -1124,7 +1124,7 @@
             whole((LEN, D)),
             whole((512, D)),
             slab((D, D)),
-            whole((1, D)),
+            whole((3, D)),
             slab((512, HD)),
             slab((2 * HD, LEN)),
             slab((512, HD)),
@@ -1264,7 +1264,7 @@
 
         def back(r, i=i):
             x = xf[own[i], r, :].astype(f32)
-            dx, gg = norm_back(x, gain[...], gxo[i, r, :] + rgx[i, r, :].astype(f32))
+            dx, gg = norm_back(x, gain[0:1, :], gxo[i, r, :] + rgx[i, r, :].astype(f32))
             total = d1[i, r, :] + dx
             sg[0:1, :] += gg
             if i == 0:
@@ -1496,17 +1496,17 @@
     tab = jnp.pad(relative_bias.T, ((0, 29), (0, 96)))
     padded = jnp.pad(bucket_table, (0, 1), constant_values=-1)
     hot = (padded[None, :] == jnp.arange(BUCKETS)[:, None]).astype(f32)
-    gains = [g.reshape(1, D) for g in (gain_self, gain_cross, gain_feed)]
+    gains = jnp.stack((gain_self, gain_cross, gain_feed))
     (
         xf, ws, wc, _, gff, ef, q, kv, at, p, cqh, ckv, cat, cp, h1, outp, d2, gg_feed,
     ) = forward(
-        wide, piece_starts, valid_lengths, hidden_in[:, 0], encoder_out[:, 0], cotangent[:, 0], tab, hot, ps, pc, pf, *gains
+        wide, piece_starts, valid_lengths, hidden_in[:, 0], encoder_out[:, 0], cotangent[:, 0], tab, hot, ps, pc, pf, gains
     )
     ws, wc = (g.reshape(4, D, D) for g in (ws, wc))
     xs, es = xf.reshape(LEN, D), ef.reshape(ENC, D)
-    gcr, d1, gg_cross, geo, gep, o1, o2, o3 = cross_backward(wide, h1, es, d2, wc, gains[1], cqh, ckv, cat, cp, gff)
+    gcr, d1, gg_cross, geo, gep, o1, o2, o3 = cross_backward(wide, h1, es, d2, wc, gains, cqh, ckv, cat, cp, gff)
     gse, gxo, gxp, dl, b1, c2, e1, e2, outs = self_backward(
-        wide, xs, d1, ws, gains[0], q, kv, at, p, gcr, o1, o2, o3, outp.reshape(2, 256, D)
+        wide, xs, d1, ws, gains, q, kv, at, p, gcr, o1, o2, o3, outp.reshape(2, 256, D)
     )
     tg = lax.dot_general(hot, dl.reshape(12, 2048), (((1,), (1,)), ((), ())), precision=precise)
     order = jnp.arange(12) // 3 ^ me ^ 1
@@ -1515,7 +1515,7 @@
     tg = jnp.pad(tg, ((0, 0), (0, 116)))
     two = lambda a: a.reshape(2, -1, D)
     gin, gen, sg, st, f, b, a = reduce_all(
-        wide, gse, b1, c2, e1, e2, two(gxo), two(gxp), two(geo), two(gep), xf, two(d1), gains[0], gg_feed, gg_cross, tg
+        wide, gse, b1, c2, e1, e2, two(gxo), two(gxp), two(geo), two(gep), xf, two(d1), gains, gg_feed, gg_cross, tg
     )
     tg = lax.dynamic_slice_in_dim(st, me * 3, 3, axis=1)
     return (

time: 284 us -> 282 us (level)
  no operation moved by 1% of the time
where the time goes in v6:
time: 282 us; the launch traced here: 281 us
  Pallas kernels  259 us (92%)
  local copies, waits for them, and re-layouts  15.8 us (6%)
  other arithmetic  4.5 us (2%)
    pallas_call x1, Pallas kernels, forward(): pl.pallas_call(partial(forward_kernel, wide), grid=(12,), in_specs=[SMEM,...  124 us
    pallas_call x1, Pallas kernels, reduce_all(): pl.pallas_call(partial(reduce_kernel, wide), in_specs=[ANY, V, V, V, V, V...  51.7 us
    pallas_call x1, Pallas kernels, self_backward(): pl.pallas_call(partial(self_backward_kernel, wide), grid=(4,), in_specs=[...  51 us
    pallas_call x1, Pallas kernels, cross_backward(): pl.pallas_call(partial(cross_backward_kernel, wide), grid=(4,), in_specs=...  32 us

profile of v6, /device:TPU:0, one launch (start us, length us, event | category | flops | bytes accessed | tf_op | source)
XLA Modules:
  0.0 281.1 jit_solution(3282949288582981118)
XLA Ops:
  0.7 0.0 copy-start.7
  0.7 0.0 copy-start.6
  0.7 0.0 copy-start.5
  0.7 0.0 copy-start.9
  0.7 0.0 copy-start.10
  0.7 0.0 copy-start.11
  0.7 0.8 stack.12
  1.5 0.7 stack.13
  2.2 0.7 stack.14
  2.9 0.6 pad_maximum_fusion.3.gains.gain
  3.5 2.3 pad_maximum_fusion.1
  5.8 0.7 pad.13
  6.5 0.7 fusion.1.hot
  7.2 0.0 copy-done.7
  7.2 0.0 copy-done.6
  7.2 0.0 copy-done.5
  7.2 0.9 pad_maximum_fusion.pf
  8.0 0.0 copy-done.9
  8.0 0.6 pad.12.tab
  8.7 0.0 copy-done.10
  8.7 0.6 copy.50.ps_s
  9.3 0.0 copy-done.11
  9.3 0.6 copy.51.vl_s
  10.0 124.1 %forward.1 = (bf16[4,256,768]{2,1,0:T(8,128)(2,1)}, bf16[4,4,192,768]{3,2,1,0:T(8,128)(2,1)}, bf16[4,4,192,768]{3,2,1,0:T(8,128)(2,1)}, bf16[4,4,192,1536]{3,2,1...) custom-call(s32[2,1]{1,0:T(2,128)} %copy.50.ps_s, ...), custom_call_target="tpu_custom_call" | custom-call | flops 60000002048 | bytes 20971520 | tf_op jit(solution)/shard_map/forward/pallas_call | solution.py:705
  134.1 32.0 %cross_backward.1 = (bf16[2,768,768]{2,1,0:T(8,128)(2,1)}, f32[512,768]{1,0:T(8,128)}, f32[1,768]{1,0:T(1,128)}, f32[256,768]{1,0:T(8,128)}, bf16[256,768]{1,0:T...) custom-call(f32[512,768]{1,0:T(8,128)} %get-tuple-element.60.h1, ...), custom_call_target="tpu_custom_call" | custom-call | flops 14000000000 | bytes 20971520 | tf_op jit(solution)/shard_map/cross_backward/pallas_call | solution.py:890
  166.0 51.0 %self_backward.1 = (bf16[2,768,768]{2,1,0:T(8,128)(2,1)}, f32[512,768]{1,0:T(8,128)}, bf16[512,768]{1,0:T(8,128)(2,1)}, f32[4,3,2048]{2,1,0:T(4,128)}, bf16[4,19...) custom-call(bf16[1024,768]{1,0:T(8,128)(2,1)} %bitcast.51, ...), custom_call_target="tpu_custom_call" | custom-call | flops 24999999488 | bytes 20971520 | tf_op jit(solution)/shard_map/self_backward/pallas_call | solution.py:1120
  217.0 1.2 fusion.2
  218.3 0.1 copy.53
  218.4 0.1 copy.54
  218.5 0.1 copy.55
  218.6 0.1 copy.56
  218.8 0.6 pad.14.tg
  219.4 51.7 %reduce_all.1 = (f32[2,256,768]{2,1,0:T(8,128)}, f32[2,128,768]{2,1,0:T(8,128)}, f32[8,768]{1,0:T(8,128)}, f32[32,128]{1,0:T(8,128)}, f32[192,1536]{1,0:T(8,128)...) custom-call(bf16[2,4,192,768]{3,2,1,0:T(8,128)(2,1)} %bitcast.49, bf16[4,192,256]{2,1,0:T(8,128)(2,1)} %get-tuple-element.82.b1, ...), custom_call_target="tpu_custom_call" | custom-call | tf_op jit(solution)/shard_map/reduce_all/pallas_call | solution.py:1425
  271.1 0.0 copy-start.2
  271.1 0.0 copy-start.1
  271.1 2.4 fusion.8
  273.4 0.0 copy-done.2
  273.4 1.0 fusion.10
  274.4 0.0 copy-done.1
  274.4 1.0 fusion.9
  275.4 0.0 copy-done.8
  275.4 0.1 constant_dynamic-slice_fusion
  275.5 0.7 copy.60
  276.1 1.5 slice_reduce_fusion
  277.6 0.9 copy.78
  278.5 1.1 copy.79
  279.7 0.5 copy-done.4
  280.2 0.9 copy.80
  (22 shorter events, 0.1 us)
Async XLA Ops:
  0.7 6.5 %copy-start.7 = (bf16[192,512]{1,0:T(8,128)(2,1)S(1)}, bf16[192,512]{1,0:T(8,128)(2,1)}, u32[]{:S(2)}) copy-start(bf16[192,512]{1,0:T(8,128)(2,1)} %param.39) | copy-start | bytes 589828
  0.7 6.5 %copy-start.6 = (bf16[192,512]{1,0:T(8,128)(2,1)S(1)}, bf16[192,512]{1,0:T(8,128)(2,1)}, u32[]{:S(2)}) copy-start(bf16[192,512]{1,0:T(8,128)(2,1)} %param.40) | copy-start | bytes 589828
  0.7 6.5 %copy-start.5 = (bf16[192,512]{1,0:T(8,128)(2,1)S(1)}, bf16[192,512]{1,0:T(8,128)(2,1)}, u32[]{:S(2)}) copy-start(bf16[192,512]{1,0:T(8,128)(2,1)} %param.41) | copy-start | bytes 589828
  0.7 7.4 %copy-start.9 = (f32[32,3]{0,1:T(4,128)S(1)}, f32[32,3]{0,1:T(4,128)}, u32[]{:S(2)}) copy-start(f32[32,3]{0,1:T(4,128)} %param.30) | copy-start | bytes 1156
  0.7 8.0 %copy-start.10 = (s32[2,1]{0,1:T(1,128)S(1)}, s32[2,1]{0,1:T(1,128)}, u32[]{:S(2)}) copy-start(s32[2,1]{0,1:T(1,128)} %param.24) | copy-start | bytes 28
  0.7 8.6 %copy-start.11 = (s32[2,1]{0,1:T(1,128)S(1)}, s32[2,1]{0,1:T(1,128)}, u32[]{:S(2)}) copy-start(s32[2,1]{0,1:T(1,128)} %param.25) | copy-start | bytes 28
  271.1 2.4 copy-start.2
  271.1 3.4 %copy-start.1 = (f32[192,768]{1,0:T(8,128)S(1)}, f32[192,768]{1,0:T(8,128)}, u32[]{:S(2)}) copy-start(f32[192,768]{1,0:T(8,128)} %get-tuple-element.98) | copy-start | bytes 1769476
  273.4 2.0 copy-start.8
  273.4 4.2 %copy-start.3 = (bf16[2,256,768]{2,1,0:T(8,128)(2,1)S(1)}, bf16[2,256,768]{2,1,0:T(8,128)(2,1)}, u32[]{:S(2)}) copy-start(bf16[2,256,768]{2,1,0:T(8,128)(2,1)} %get-tuple-element.80) | copy-start | bytes 2359300
  274.4 4.1 %copy-start = (f32[2,256,768]{2,1,0:T(8,128)S(1)}, f32[2,256,768]{2,1,0:T(8,128)}, u32[]{:S(2)}) copy-start(f32[2,256,768]{2,1,0:T(8,128)} %get-tuple-element.93) | copy-start | bytes 4718596
  278.5 1.7 copy-start.4
